TPU v7x, 32 devices: a whole 2x2x4 slice. The times are simulated.
32 devices in a mesh: section: 2 (over x), row: 4 (over y, core), col: 4 (over z).
Axes of the slice: x: 2, y: 2, z: 4, core: 2. Of those that a mesh axis runs over, the one named last changes fastest.
Arguments:
- image: bfloat16 [32, 64, 1024], P('section', 'row', 'col'), may hold values from -6 to 6
- conv_kernel: float32 [7, 7, 1024], P(None, None, 'col'), may hold values from -0.875 to 0.875
- norm_gain: float32 [1024], P('col'), may hold values from 0.1 to 1.9
- w_in: bfloat16 [1024, 4096], P('row', 'col'), may hold values from -0.1875 to 0.1875
- w_out: bfloat16 [4096, 1024], P('row', 'col'), may hold values from -0.09375 to 0.09375
- upstream: bfloat16 [32, 64, 1024], P('section', 'row', 'col'), may hold values from -6 to 6
Outputs:
- output: bfloat16 [32, 64, 1024], P('section', 'row', 'col')
- image_grad: float32 [32, 64, 1024], P('section', 'row', 'col')
All inputs are finite; a program needn't handle non-finite values.
Results may differ from a plain program's by a relative error of at most 0.0095.
Values may be sent and summed in bfloat16 or wider, within the bound.
No kernel may reach another device: no remote copies, remote signals or barrier semaphores. Data moves between devices by JAX's collectives and lax.ppermute only.
A program may use at most 64 MiB of HBM per device.

v0:
```python
import math

import jax
import jax.numpy as jnp
from jax import lax
from jax.sharding import PartitionSpec as P

KERNEL = 7


EPSILON = 1e-06


def extended(block, sides, width):
    for axis, dim in sides:
        count = lax.axis_size(axis)
        forward = [(i, i + 1) for i in range(count - 1)]
        backward = [(target, source) for source, target in forward]
        low = lax.ppermute(
            lax.slice_in_dim(block, block.shape[dim] - width, None, axis=dim), axis, forward
        )
        high = lax.ppermute(lax.slice_in_dim(block, 0, width, axis=dim), axis, backward)
        block = jnp.concatenate([low, block, high], axis=dim)
    return block


def depthwise(padded, kernel, height, breadth, start):
    total = jnp.zeros((height, breadth, padded.shape[2]), jnp.float32)
    for row_off in range(KERNEL):
        for col_off in range(KERNEL):
            lead = start - row_off if start > 0 else row_off
            side = start - col_off if start > 0 else col_off
            total = (
                total
                + padded[lead : lead + height, side : side + breadth, :] * kernel[row_off, col_off]
            )
    return total


def gelu_slope(preact):
    return 0.5 * (1.0 + lax.erf(preact / math.sqrt(2.0))) + preact * jnp.exp(
        -0.5 * preact * preact
    ) / math.sqrt(2.0 * math.pi)


def transposed(left, right):
    return lax.dot_general(
        left, right, (((1,), (1,)), ((), ())), preferred_element_type=jnp.float32
    )


def local(image, conv_kernel, norm_gain, w_in, w_out, upstream):
    height, breadth, chan_local = image.shape
    cells = height * breadth
    margin = KERNEL // 2
    channels_all = chan_local * lax.axis_size("col")
    padded = extended(image, (("section", 0), ("row", 1)), margin)
    mixed = depthwise(padded.astype(jnp.float32), conv_kernel, height, breadth, 0)
    first_sum, second_sum = lax.psum(
        (jnp.sum(mixed, axis=-1), jnp.sum(mixed * mixed, axis=-1)), "col"
    )
    centre = first_sum[..., None] / channels_all
    centred = mixed - centre
    spread = second_sum[..., None] / channels_all - centre * centre
    inv_std = lax.rsqrt(spread + EPSILON)
    normed = centred * inv_std
    scaled = (normed * norm_gain).astype(jnp.bfloat16).reshape(cells, chan_local)
    features = lax.all_gather(scaled, "col", axis=1, tiled=True)
    columns = features
    preact = jnp.dot(
        columns, lax.all_gather(w_in, "row", axis=0, tiled=True), preferred_element_type=jnp.float32
    )
    hidden = jax.nn.gelu(preact, approximate=False).astype(jnp.bfloat16)
    hidden_all = lax.all_gather(hidden, "col", axis=1, tiled=True)
    columns = hidden_all
    branch = jnp.dot(
        columns,
        lax.all_gather(w_out, "row", axis=0, tiled=True),
        preferred_element_type=jnp.float32,
    )
    flat_image = image.reshape(cells, chan_local).astype(jnp.float32)
    output = (flat_image + branch).astype(jnp.bfloat16).reshape(image.shape)
    grad_flat = upstream.reshape(cells, chan_local)
    hidden_terms = transposed(grad_flat, lax.all_gather(w_out, "row", axis=0, tiled=True))
    hidden_grad = lax.psum_scatter(
        hidden_terms.astype(jnp.bfloat16), "col", scatter_dimension=1, tiled=True
    ).astype(jnp.float32)
    act_grad = (hidden_grad * gelu_slope(preact)).astype(jnp.bfloat16)
    feature_terms = transposed(act_grad, lax.all_gather(w_in, "row", axis=0, tiled=True))
    feature_grad = lax.psum_scatter(
        feature_terms.astype(jnp.bfloat16), "col", scatter_dimension=1, tiled=True
    ).astype(jnp.float32)
    normed_grad = feature_grad.reshape(image.shape) * norm_gain
    grad_first, grad_second = lax.psum(
        (jnp.sum(normed_grad, axis=-1), jnp.sum(normed_grad * normed, axis=-1)), "col"
    )
    mixed_grad = inv_std * (
        normed_grad
        - grad_first[..., None] / channels_all
        - normed * (grad_second[..., None] / channels_all)
    )
    grad_pad = extended(
        mixed_grad.astype(jnp.bfloat16), (("section", 0), ("row", 1)), margin
    ).astype(mixed_grad.dtype)
    image_grad = upstream.astype(jnp.float32) + depthwise(
        grad_pad, conv_kernel, height, breadth, 2 * margin
    )
    return (output, image_grad)


def solution(mesh):
    in_specs = (
        P("section", "row", "col"),
        P(None, None, "col"),
        P("col"),
        P("row", "col"),
        P("row", "col"),
        P("section", "row", "col"),
    )
    out_specs = (P("section", "row", "col"), P("section", "row", "col"))
    return jax.shard_map(local, mesh=mesh, in_specs=in_specs, out_specs=out_specs, check_vma=False)
```

profile of v0, /device:TPU:1, one launch (start us, length us, event | category | flops | bytes accessed | tf_op | source)
XLA Modules:
  0.0 196.1 jit_solution(15735442699452314758)
XLA Ops:
  7.2 0.0 all-gather.8.cloned.1.call-start
  7.2 0.7 all-gather.8.cloned.1.call-update
  7.9 0.0 all-gather.4.cloned.1.call-start
  7.9 0.7 all-gather.4.cloned.1.call-update
  8.6 0.0 reduce-scatter.3.cloned.1.call-start
  8.7 26.0 %all-gather.8.cloned.1.call-done = bf16[4096,256]{1,0:T(8,128)(2,1)} async-done(((bf16[1024,256]{1,0:T(8,128)(2,1)}), bf16[4096,256]{1,0:T(8,128)(2,1)}) %all-gather.8.cloned.1.call-update) | async-done | bytes 2097168 | tf_op jit(solution)/shard_map/all_gather | solution.py:78
  34.7 3.8 %convolution_convert_fusion = bf16[256,4096]{1,0:T(8,128)(2,1)} fusion(bf16[256,256]{1,0:T(8,128)(2,1)} %bitcast.64, bf16[4096,256]{1,0:T(8,128)(2,1)} %all-gather.8.cloned.1.call-done), kind=kOutput, calls=%fused_computation | convolution fusion | flops 537919488 | bytes 4325376 | tf_op jit(solution)/shard_map/dot_general | solution.py:47
  38.4 0.0 copy-start.2
  38.4 0.0 copy-start.3
  38.4 0.0 reduce-scatter.3.cloned.1.call-update
  38.5 0.0 reduce-scatter.5.cloned.1.call-start
  38.5 0.8 copy-done.2
  39.3 3.1 %collective-permute-start = (bf16[3,16,256]{2,1,0:T(8,128)(2,1)S(1)}, bf16[3,16,256]{2,1,0:T(8,128)(2,1)S(1)}, u32[]{:S(2)}, u32[]{:S(2)}) collective-permute-start(bf16[3,16,256]{2,1,0:T(8,128)(2,1)S(1)} %get-tuple-element.16), channel_id=1, source_target_pairs={{0,16},{1,17},{2,18},{3,19},{4,20},{5,21},{6,22},{7,23},{8,24},{9,... | collective-permute-start | bytes 73736 | tf_op jit(solution)/shard_map/ppermute | solution.py:19
  42.4 1.3 collective-permute-start.1
  43.7 0.0 copy-done.3
  43.8 0.0 collective-permute-done
  43.8 3.6 %collective-permute-done.1 = bf16[3,16,256]{2,1,0:T(8,128)(2,1)S(1)} collective-permute-done((bf16[3,16,256]{2,1,0:T(8,128)(2,1)S(1)}, bf16[3,16,256]{2,1,0:T(8,128)(2,1)S(1)}, u32[]{:S(2)}, u32[]{:S(2)}) %collective-permute-start.1) | collective-permute-done | bytes 24608 | tf_op jit(solution)/shard_map/ppermute | solution.py:22
  47.4 3.2 %collective-permute-start.3 = (bf16[22,3,256]{2,1,0:T(4,128)(2,1)S(1)}, bf16[22,3,256]{2,1,0:T(4,128)(2,1)S(1)}, u32[]{:S(2)}, u32[]{:S(2)}) collective-permute-start(bf16[22,3,256]{2,1,0:T(4,128)(2,1)S(1)} %get-tuple-element.12), channel_id=1, source_target_pairs={{4,0},{8,4},{12,8},{5,1},{9,5},{13,9},{6,2},{10,6},{14,10},{7,3},{... | collective-permute-start | bytes 101384 | tf_op jit(solution)/shard_map/ppermute | solution.py:22
  50.7 2.4 %collective-permute-start.2 = (bf16[22,3,256]{2,1,0:T(4,128)(2,1)S(1)}, bf16[22,3,256]{2,1,0:T(4,128)(2,1)S(1)}, u32[]{:S(2)}, u32[]{:S(2)}) collective-permute-start(bf16[22,3,256]{2,1,0:T(4,128)(2,1)S(1)} %get-tuple-element.11), channel_id=1, source_target_pairs={{0,4},{4,8},{8,12},{1,5},{5,9},{9,13},{2,6},{6,10},{10,14},{3,7},{... | collective-permute-start | bytes 101384 | tf_op jit(solution)/shard_map/ppermute | solution.py:19
  53.0 1.1 collective-permute-done.3
  54.1 0.8 collective-permute-done.2
  54.9 0.1 maximum_convert_fusion
  55.0 0.0 copy-start.4
  55.0 1.8 fusion.125
  56.8 15.4 %all-reduce.1 = (f32[16,16]{1,0:T(8,128)S(1)}, f32[16,16]{1,0:T(8,128)S(1)}) all-reduce(f32[16,16]{1,0:T(8,128)S(1)} %get-tuple-element.3, f32[16,16]{1,0:T(8,128)S(1)} %get-tuple-element.2), channel_id=1, replica_groups=mesh['section'=2,'row'=4,'col'=4] {'col'}, use_global_device_ids=true, to_apply=%region_3.0 | all-reduce | flops 512 | bytes 4096 | tf_op jit(solution)/shard_map/psum | solution.py:59
  72.2 0.0 copy-done.4
  72.2 0.1 multiply_convert_fusion.1
  72.4 20.2 %all_gather.14 = bf16[256,1024]{1,0:T(8,128)(2,1)S(1)} all-gather(bf16[256,256]{1,0:T(8,128)(2,1)S(1)} %bitcast.65), channel_id=1, replica_groups=mesh['section'=2,'row'=4,'col'=4] {'col'}, dimensions={1}, use_global_device_ids=true | all-gather | bytes 655360 | tf_op jit(solution)/shard_map/all_gather | solution.py:68
  92.5 0.0 all-gather.4.cloned.1.call-done
  92.5 5.3 %fusion.3 = (bf16[256,1024]{1,0:T(8,128)(2,1)}, f32[256,1024]{1,0:T(8,128)S(1)}) fusion(bf16[256,1024]{1,0:T(8,128)(2,1)S(1)} %all_gather.14, bf16[1024,1024]{1,0:T(8,128)(2,1)} %all-gather.4.cloned.1.call-done), kind=kOutput, calls=%fused_computation.8 | convolution fusion | flops 553910272 | bytes 4194304 | tf_op jit(solution)/shard_map/dot_general | solution.py:70
  97.8 15.4 %reduce-scatter.3.cloned.1.call-done = bf16[256,1024]{1,0:T(8,128)(2,1)} async-done(((bf16[256,4096]{1,0:T(8,128)(2,1)}), bf16[256,1024]{1,0:T(8,128)(2,1)}) %reduce-scatter.3.cloned.1.call-update) | async-done | bytes 524304 | tf_op jit(solution)/shard_map/reduce_scatter | solution.py:85
  113.3 3.6 %convolution_convert_fusion.1 = bf16[256,1024]{1,0:T(8,128)(2,1)} fusion(bf16[1024,1024]{1,0:T(8,128)(2,1)} %all-gather.4.cloned.1.call-done, f32[256,1024]{1,0:T(8,128)S(1)} %get-tuple-element.69, bf16[256,1024]{1,0:T(8,128)(2,1)} %reduce-scatter.3.cloned.1.call-done), kind=kOutput, calls=%fused_computation.3 | convolution fusion | flops 540016640 | bytes 4194304 | tf_op jit(solution)/shard_map/dot_general | solution.py:47
  116.8 0.0 copy-start
  116.8 0.0 reduce-scatter.5.cloned.1.call-update
  116.9 0.0 all-gather.6.cloned.1.call-start
  116.9 0.5 all-gather.6.cloned.1.call-update
  117.5 18.8 %reduce-scatter.5.cloned.1.call-done = bf16[256,256]{1,0:T(8,128)(2,1)} async-done(((bf16[256,1024]{1,0:T(8,128)(2,1)}), bf16[256,256]{1,0:T(8,128)(2,1)}) %reduce-scatter.5.cloned.1.call-update) | async-done | bytes 131088 | tf_op jit(solution)/shard_map/reduce_scatter | solution.py:90
  136.2 1.0 multiply_reduce_fusion.1
  137.2 0.1 reduce_sum.41
  137.3 0.9 convert_element_type.53
  138.3 0.2 multiply_reduce_fusion
  138.5 13.5 %all-reduce = (f32[16,16]{1,0:T(8,128)S(1)}, f32[16,16]{1,0:T(8,128)S(1)}) all-reduce(f32[16,16]{1,0:T(8,128)S(1)} %multiply_reduce_fusion, f32[16,16]{1,0:T(8,128)S(1)} %reduce_sum.41), channel_id=1, replica_groups=mesh['section'=2,'row'=4,'col'=4] {'col'}, use_global_device_ids=true, to_apply=%region_9.0 | all-reduce | flops 512 | bytes 4096 | tf_op jit(solution)/shard_map/psum | solution.py:94
  152.0 1.1 multiply_convert_fusion
  153.2 1.3 collective-permute-start.5
  154.5 4.0 %collective-permute-start.4 = (bf16[3,16,256]{2,1,0:T(8,128)(2,1)S(1)}, bf16[3,16,256]{2,1,0:T(8,128)(2,1)S(1)}, u32[]{:S(2)}, u32[]{:S(2)}) collective-permute-start(bf16[3,16,256]{2,1,0:T(8,128)(2,1)S(1)} %get-tuple-element.13), channel_id=1, source_target_pairs={{0,16},{1,17},{2,18},{3,19},{4,20},{5,21},{6,22},{7,23},{8,24},{9,... | collective-permute-start | bytes 73736 | tf_op jit(solution)/shard_map/ppermute | solution.py:19
  158.4 0.0 collective-permute-done.5
  158.5 0.9 collective-permute-done.4
  159.4 8.1 %collective-permute-start.7 = (bf16[22,3,256]{2,1,0:T(4,128)(2,1)S(1)}, bf16[22,3,256]{2,1,0:T(4,128)(2,1)S(1)}, u32[]{:S(2)}, u32[]{:S(2)}) collective-permute-start(bf16[22,3,256]{2,1,0:T(4,128)(2,1)S(1)} %get-tuple-element.10), channel_id=1, source_target_pairs={{4,0},{8,4},{12,8},{5,1},{9,5},{13,9},{6,2},{10,6},{14,10},{7,3},{... | collective-permute-start | bytes 101384 | tf_op jit(solution)/shard_map/ppermute | solution.py:22
  167.6 3.0 %collective-permute-start.6 = (bf16[22,3,256]{2,1,0:T(4,128)(2,1)S(1)}, bf16[22,3,256]{2,1,0:T(4,128)(2,1)S(1)}, u32[]{:S(2)}, u32[]{:S(2)}) collective-permute-start(bf16[22,3,256]{2,1,0:T(4,128)(2,1)S(1)} %get-tuple-element.9), channel_id=1, source_target_pairs={{0,4},{4,8},{8,12},{1,5},{5,9},{9,13},{2,6},{6,10},{10,14},{3,7},{... | collective-permute-start | bytes 101384 | tf_op jit(solution)/shard_map/ppermute | solution.py:19
  170.6 13.4 %all-gather.6.cloned.1.call-done = bf16[256,4096]{1,0:T(8,128)(2,1)} async-done(((bf16[256,1024]{1,0:T(8,128)(2,1)}), bf16[256,4096]{1,0:T(8,128)(2,1)}) %all-gather.6.cloned.1.call-update) | async-done | bytes 2097168 | tf_op jit(solution)/shard_map/all_gather | solution.py:74
  184.0 0.0 copy-done
  184.0 0.0 copy-start.1
  184.0 3.0 %fusion = bf16[256,256]{1,0:T(8,128)(2,1)} fusion(bf16[256,4096]{1,0:T(8,128)(2,1)} %all-gather.6.cloned.1.call-done, bf16[4096,256]{1,0:T(8,128)(2,1)S(1)} %copy-done, bf16[256,256]{1,0:T(8,128)(2,1)S(1)} %bitcast.66), kind=kOutput, calls=%fused_computation.5 | convolution fusion | flops 537067520 | bytes 4456448 | tf_op jit(solution)/shard_map/dot_general | solution.py:76
  187.0 0.0 collective-permute-done.7
  187.0 0.0 collective-permute-done.6
  187.0 0.1 maximum_convert_fusion.1
  187.1 0.0 copy-done.1
  187.1 2.4 %fusion.24 = f32[16,16,256]{2,1,0:T(8,128)} fusion(f32[22,22,256]{2,1,0:T(8,128)S(1)} %maximum_convert_fusion.1, bf16[16,16,256]{2,1,0:T(8,128)(2,1)S(1)} %copy-done.1, f32[256]{0:T(256)S(1)} %bitcast.162, f32[256]{0:T(256)S(1)} %bitcast.164, f32[256]{0:T(256)S(1)} %bitcast.70, f32[256]{0:T(256)S(1)} %bitcast.72, f32[256]{0:T(256)S(1)} %bitcast.74, ...), kind=kLoop, calls=%fused_computation.39 | loop fusion | flops 6488064 | bytes 13288448 | tf_op jit(solution)/shard_map/add | solution.py:105
  (12 shorter events, 0.2 us)
Async XLA Ops:
  7.2 27.5 %all-gather.8.cloned.1.call-start = ((), (), s32[]{:S(2)}) async-start(), calls=%async_computation.4 | async-start | bytes 2621440 | tf_op jit(solution)/shard_map/all_gather | solution.py:78
  7.9 84.6 %all-gather.4.cloned.1.call-start = ((), (), s32[]{:S(2)}) async-start(), calls=%async_computation.2 | async-start | bytes 2621440 | tf_op jit(solution)/shard_map/all_gather | solution.py:71
  8.6 104.6 %reduce-scatter.3.cloned.1.call-start = ((), (), s32[]{:S(2)}) async-start(), calls=%async_computation.5 | async-start | bytes 2621440 | tf_op jit(solution)/shard_map/reduce_scatter | solution.py:85
  38.4 0.9 copy-start.2
  38.4 5.3 %copy-start.3 = (f32[7,7,256]{2,1,0:T(8,128)S(1)}, f32[7,7,256]{2,1,0:T(8,128)}, u32[]{:S(2)}) copy-start(f32[7,7,256]{2,1,0:T(8,128)} %param.7) | copy-start | bytes 150532
  38.5 97.8 %reduce-scatter.5.cloned.1.call-start = ((), (), s32[]{:S(2)}) async-start(), calls=%async_computation.6 | async-start | bytes 655360 | tf_op jit(solution)/shard_map/reduce_scatter | solution.py:90
  39.3 4.5 %collective-permute-start = (bf16[3,16,256]{2,1,0:T(8,128)(2,1)S(1)}, bf16[3,16,256]{2,1,0:T(8,128)(2,1)S(1)}, u32[]{:S(2)}, u32[]{:S(2)}) collective-permute-start(bf16[3,16,256]{2,1,0:T(8,128)(2,1)S(1)} %get-tuple-element.16), channel_id=1, source_target_pairs={{0,16},{1,17},{2,18},{3,19},{4,20},{5,21},{6,22},{7,23},{8,24},{9,... | collective-permute-start | bytes 73736 | tf_op jit(solution)/shard_map/ppermute | solution.py:19
  42.4 5.0 %collective-permute-start.1 = (bf16[3,16,256]{2,1,0:T(8,128)(2,1)S(1)}, bf16[3,16,256]{2,1,0:T(8,128)(2,1)S(1)}, u32[]{:S(2)}, u32[]{:S(2)}) collective-permute-start(bf16[3,16,256]{2,1,0:T(8,128)(2,1)S(1)} %get-tuple-element.15), channel_id=1, source_target_pairs={{16,0},{17,1},{18,2},{19,3},{20,4},{21,5},{22,6},{23,7},{24,8},{25... | collective-permute-start | bytes 73736 | tf_op jit(solution)/shard_map/ppermute | solution.py:22
  47.4 6.7 %collective-permute-start.3 = (bf16[22,3,256]{2,1,0:T(4,128)(2,1)S(1)}, bf16[22,3,256]{2,1,0:T(4,128)(2,1)S(1)}, u32[]{:S(2)}, u32[]{:S(2)}) collective-permute-start(bf16[22,3,256]{2,1,0:T(4,128)(2,1)S(1)} %get-tuple-element.12), channel_id=1, source_target_pairs={{4,0},{8,4},{12,8},{5,1},{9,5},{13,9},{6,2},{10,6},{14,10},{7,3},{... | collective-permute-start | bytes 101384 | tf_op jit(solution)/shard_map/ppermute | solution.py:22
  50.7 4.3 %collective-permute-start.2 = (bf16[22,3,256]{2,1,0:T(4,128)(2,1)S(1)}, bf16[22,3,256]{2,1,0:T(4,128)(2,1)S(1)}, u32[]{:S(2)}, u32[]{:S(2)}) collective-permute-start(bf16[22,3,256]{2,1,0:T(4,128)(2,1)S(1)} %get-tuple-element.11), channel_id=1, source_target_pairs={{0,4},{4,8},{8,12},{1,5},{5,9},{9,13},{2,6},{6,10},{10,14},{3,7},{... | collective-permute-start | bytes 101384 | tf_op jit(solution)/shard_map/ppermute | solution.py:19
  55.0 17.2 %copy-start.4 = (f32[256]{0:T(256)S(1)}, f32[256]{0:T(256)}, u32[]{:S(2)}) copy-start(f32[256]{0:T(256)} %param.8) | copy-start | bytes 3076
  116.8 67.1 %copy-start = (bf16[4096,256]{1,0:T(8,128)(2,1)S(1)}, bf16[4096,256]{1,0:T(8,128)(2,1)}, u32[]{:S(2)}) copy-start(bf16[4096,256]{1,0:T(8,128)(2,1)} %all-gather.8.cloned.1.call-done) | copy-start | bytes 6291460
  116.9 67.1 %all-gather.6.cloned.1.call-start = ((), (), s32[]{:S(2)}) async-start(), calls=%async_computation.3 | async-start | bytes 2621440 | tf_op jit(solution)/shard_map/all_gather | solution.py:74
  153.2 5.3 %collective-permute-start.5 = (bf16[3,16,256]{2,1,0:T(8,128)(2,1)S(1)}, bf16[3,16,256]{2,1,0:T(8,128)(2,1)S(1)}, u32[]{:S(2)}, u32[]{:S(2)}) collective-permute-start(bf16[3,16,256]{2,1,0:T(8,128)(2,1)S(1)} %get-tuple-element.14), channel_id=1, source_target_pairs={{16,0},{17,1},{18,2},{19,3},{20,4},{21,5},{22,6},{23,7},{24,8},{25... | collective-permute-start | bytes 73736 | tf_op jit(solution)/shard_map/ppermute | solution.py:22
  154.5 4.9 %collective-permute-start.4 = (bf16[3,16,256]{2,1,0:T(8,128)(2,1)S(1)}, bf16[3,16,256]{2,1,0:T(8,128)(2,1)S(1)}, u32[]{:S(2)}, u32[]{:S(2)}) collective-permute-start(bf16[3,16,256]{2,1,0:T(8,128)(2,1)S(1)} %get-tuple-element.13), channel_id=1, source_target_pairs={{0,16},{1,17},{2,18},{3,19},{4,20},{5,21},{6,22},{7,23},{8,24},{9,... | collective-permute-start | bytes 73736 | tf_op jit(solution)/shard_map/ppermute | solution.py:19
  159.4 27.6 %collective-permute-start.7 = (bf16[22,3,256]{2,1,0:T(4,128)(2,1)S(1)}, bf16[22,3,256]{2,1,0:T(4,128)(2,1)S(1)}, u32[]{:S(2)}, u32[]{:S(2)}) collective-permute-start(bf16[22,3,256]{2,1,0:T(4,128)(2,1)S(1)} %get-tuple-element.10), channel_id=1, source_target_pairs={{4,0},{8,4},{12,8},{5,1},{9,5},{13,9},{6,2},{10,6},{14,10},{7,3},{... | collective-permute-start | bytes 101384 | tf_op jit(solution)/shard_map/ppermute | solution.py:22
  167.6 19.4 %collective-permute-start.6 = (bf16[22,3,256]{2,1,0:T(4,128)(2,1)S(1)}, bf16[22,3,256]{2,1,0:T(4,128)(2,1)S(1)}, u32[]{:S(2)}, u32[]{:S(2)}) collective-permute-start(bf16[22,3,256]{2,1,0:T(4,128)(2,1)S(1)} %get-tuple-element.9), channel_id=1, source_target_pairs={{0,4},{4,8},{8,12},{1,5},{5,9},{9,13},{2,6},{6,10},{10,14},{3,7},{... | collective-permute-start | bytes 101384 | tf_op jit(solution)/shard_map/ppermute | solution.py:19
  184.0 3.1 %copy-start.1 = (bf16[16,16,256]{2,1,0:T(8,128)(2,1)S(1)}, bf16[16,16,256]{2,1,0:T(8,128)(2,1)}, u32[]{:S(2)}) copy-start(bf16[16,16,256]{2,1,0:T(8,128)(2,1)} %param.11) | copy-start | bytes 393220
Sparse Core Ops, SparseCore 0:
  9.6 25.0 all-gather.7
  36.2 23.0 all-gather.3
  61.6 51.5 reduce-scatter.2
  117.0 19.1 reduce-scatter.4
  137.7 46.2 all-gather.5
where the time goes:
time: 197 us; the launch traced here: 196 us
  waiting for transfers between devices  81.9 us (42%)
  blocking collectives  49.1 us (25%)
  starting transfers between devices  26.6 us (14%)
  matrix products  15.7 us (8%)
  between operations  14 us (7%)
  other arithmetic  7.88 us (4%)
    all_gather x1, waiting for transfers between devices, local(): lax.all_gather(w_out, 'row', axis=0, tiled=True)  26 us
    all_gather x1, blocking collectives, local(): features = lax.all_gather(scaled, 'col', axis=1, tiled=True)  20.2 us
    reduce_scatter x1, waiting for transfers between devices, local(): lax.psum_scatter(feature_terms.astype(jnp.bfloat16), 'col', scatter_dimen...  18.8 us
    reduce_scatter x1, waiting for transfers between devices, local(): lax.psum_scatter(hidden_terms.astype(jnp.bfloat16), 'col', scatter_dimens...  15.4 us
    psum x1, blocking collectives, local(): lax.psum((jnp.sum(mixed, axis=-1), jnp.sum(mixed * mixed, axis=-1)), 'col')  15.4 us
    ppermute x4, starting transfers between devices, extended(): lax.ppermute(lax.slice_in_dim(block, 0, width, axis=dim), axis, backward)  13.9 us
    psum x1, blocking collectives, local(): lax.psum((jnp.sum(normed_grad, axis=-1), jnp.sum(normed_grad * normed, ax...  13.5 us
    all_gather x1, waiting for transfers between devices, local(): hidden_all = lax.all_gather(hidden, 'col', axis=1, tiled=True)  13.4 us
  transfers between devices with their start and end apart: 13, of which 8 were waited for; matrix products, arithmetic and copies ran while one was open for 9% of the time, Pallas kernels for 0%

commit v1 on v0

v1 whole, which is shorter than its diff:
```python
import functools
import math

import jax
import jax.numpy as jnp
from jax import lax
from jax.experimental import pallas as pl
from jax.experimental.pallas import tpu as pltpu
from jax.sharding import PartitionSpec as P

KERNEL = 7
MARGIN = KERNEL // 2
EPSILON = 1e-06
BF16, F32 = jnp.bfloat16, jnp.float32
VMEM_LIMIT = 40 * 1024 * 1024


def round_up(value, to):
    return -(-value // to) * to


def bits_of(count):
    return [1 << b for b in range(count.bit_length() - 1)]


def swap(x, axis, bit):
    count = lax.axis_size(axis)
    return lax.ppermute(x, axis, [(i, i ^ bit) for i in range(count)])


def pairings(count):
    both = [
        [(i, i + 1) for i in range(first, count - 1, 2)] for first in range(2)
    ]
    return [p + [(b, a) for a, b in p] for p in both if p]


def faces_up(index, pairing):
    return (index + pairing) % 2 == 0


def halo_kinds(n_sec, n_row):
    secs, rows = range(len(pairings(n_sec))), range(len(pairings(n_row)))
    return (
        [(a, None) for a in secs]
        + [(None, b) for b in rows]
        + [(a, b) for a in secs for b in rows]
    )


def halo_rows(kind, height, breadth):
    if kind[1] is None:
        return MARGIN * breadth
    if kind[0] is None:
        return MARGIN * height
    return round_up(MARGIN * MARGIN, 16)


def halo_permute(strip, kind, n_sec, n_row):
    secs, rows = pairings(n_sec), pairings(n_row)
    if kind[1] is None:
        return lax.ppermute(strip, "section", secs[kind[0]])
    if kind[0] is None:
        return lax.ppermute(strip, "row", rows[kind[1]])
    pairs = [
        (a * n_row + c, b * n_row + d)
        for a, b in secs[kind[0]]
        for c, d in rows[kind[1]]
    ]
    return lax.ppermute(strip, ("section", "row"), pairs)


def emit_strips(cells, corner, outs, kinds, height, breadth):
    sec, row = lax.axis_index("section"), lax.axis_index("row")
    for lane in range(cells.shape[0]):
        block, lanes = cells.at[lane], slice(lane * 128, (lane + 1) * 128)
        for out, (a, b) in zip(outs, kinds):
            if b is None:
                up = faces_up(sec, a)
                size = MARGIN * breadth
                out[:, lanes] = jnp.where(
                    up, block[height * breadth - size :, :], block[:size, :]
                ).astype(BF16)
            elif a is None:
                up = faces_up(row, b)
                for j in range(MARGIN):
                    out[j * height : (j + 1) * height, lanes] = jnp.where(
                        up,
                        block[pl.ds(breadth - MARGIN + j, height, stride=breadth), :],
                        block[pl.ds(j, height, stride=breadth), :],
                    ).astype(BF16)
            else:
                up, right = faces_up(sec, a), faces_up(row, b)
                corner[...] = jnp.zeros_like(corner)
                for i in range(MARGIN):
                    sides = []
                    for start in ((height - MARGIN + i) * breadth, i * breadth):
                        sides.append(
                            jnp.where(
                                right,
                                block[start + breadth - MARGIN : start + breadth, :],
                                block[start : start + MARGIN, :],
                            )
                        )
                    corner[i * MARGIN : (i + 1) * MARGIN, :] = jnp.where(up, *sides)
                out[:, lanes] = corner[...].astype(BF16)


def low_high(index, received):
    if not received:
        return None, None
    first = received[0]
    second = received[1] if len(received) > 1 else jnp.zeros_like(first)
    odd = index % 2 == 1
    return jnp.where(odd, first, second), jnp.where(odd, second, first)


LEFT = 8


def padded_width(breadth):
    return round_up(LEFT + breadth + MARGIN, 8)


def fill_padded(pad, cells, halos, kinds, height, breadth):
    sec, row = lax.axis_index("section"), lax.axis_index("row")
    width = padded_width(breadth)
    got = dict(zip(kinds, halos))
    secs = sorted({a for a, b in kinds if b is None})
    rows = sorted({b for a, b in kinds if a is None})
    for lane in range(pad.shape[0]):
        block, lanes = pad.at[lane], slice(lane * 128, (lane + 1) * 128)

        def arrived(*kind):
            return got[kind][:, lanes].astype(F32)

        block[: MARGIN * width, :] = jnp.zeros((MARGIN * width, 128), F32)
        block[(MARGIN + height) * width :, :] = jnp.zeros((MARGIN * width, 128), F32)
        for i in range(height):
            start = (MARGIN + i) * width + LEFT
            block[start : start + breadth, :] = cells[i * breadth : (i + 1) * breadth, lanes].astype(F32)
        low, high = low_high(sec, [arrived(a, None) for a in secs])
        if low is not None:
            for i in range(MARGIN):
                for top, strip in ((i, low), (MARGIN + height + i, high)):
                    start = top * width + LEFT
                    block[start : start + breadth, :] = strip[i * breadth : (i + 1) * breadth, :]
        low, high = low_high(row, [arrived(None, b) for b in rows])
        for j in range(MARGIN):
            for column, strip in ((LEFT - MARGIN + j, low), (LEFT + breadth + j, high)):
                block[pl.ds(MARGIN * width + column, height, stride=width), :] = (
                    jnp.zeros((height, 128), F32)
                    if strip is None
                    else strip[j * height : (j + 1) * height, :]
                )
        if secs and rows:
            by_sec = [low_high(row, [arrived(a, b) for b in rows]) for a in secs]
            for column, k in ((LEFT - MARGIN, 0), (LEFT + breadth, 1)):
                low, high = low_high(sec, [pair[k] for pair in by_sec])
                for i in range(MARGIN):
                    for top, strip in ((i, low), (MARGIN + height + i, high)):
                        start = top * width + column
                        block[start : start + MARGIN, :] = strip[i * MARGIN : (i + 1) * MARGIN, :]


def convolve(pad, shifted, taps, height, breadth, flip, store):
    width = padded_width(breadth)
    tall = height + 2 * MARGIN
    step = 4 if height % 4 == 0 else 1
    for lane in range(pad.shape[0]):
        lanes = slice(lane * 128, (lane + 1) * 128)
        for b in range(KERNEL):
            for i in range(tall):
                start = i * width + LEFT - MARGIN + b
                shifted[b, i * breadth : (i + 1) * breadth, :] = pad[lane, start : start + breadth, :]
        for top in range(0, height, step):
            total = jnp.zeros((step * breadth, 128), F32)
            for a in range(KERNEL):
                for b in range(KERNEL):
                    p, q = (KERNEL - 1 - a, KERNEL - 1 - b) if flip else (a, b)
                    first = (top + a) * breadth
                    total += shifted[b, first : first + step * breadth, :] * taps[p, q, lanes][None, :]
            store(slice(top * breadth, (top + step) * breadth), lanes, total)


def strips_kernel(dims, kinds, image, *rest):
    outs, (cells, corner) = rest[: len(kinds)], rest[len(kinds) :]
    for lane in range(cells.shape[0]):
        cells[lane] = image[:, lane * 128 : (lane + 1) * 128].astype(F32)
    emit_strips(cells, corner, outs, kinds, *dims)


def split3(x):
    high = x.astype(BF16)
    left = x - high.astype(F32)
    mid = left.astype(BF16)
    return high, mid, (left - mid.astype(F32)).astype(BF16)


def message_rows(cells, channels):
    return cells + round_up(2 * (cells // channels) + 3, 16)


def forward_conv_kernel(dims, kinds, image, taps, gain, *rest):
    halos, (message, pad, shifted, mixed, tail) = rest[: len(kinds)], rest[len(kinds) :]
    height, breadth = dims
    cells, channels = image.shape
    fill_padded(pad, image, halos, kinds, height, breadth)

    def store(rows, lanes, total):
        mixed[rows, lanes] = total

    convolve(pad, shifted, taps, height, breadth, False, store)
    mean = jnp.sum(mixed[...], axis=1, keepdims=True) * (1.0 / channels)
    first = mean.astype(BF16).astype(F32)
    second = (mean - first).astype(BF16).astype(F32)
    message[:cells, :] = ((mixed[...] - first) - second).astype(BF16)
    tail[...] = jnp.zeros_like(tail)
    per = cells // channels
    for t, column in enumerate((first, second)):
        flat = jnp.broadcast_to(column, (cells, 128)).T
        for p in range(per):
            tail[t * per + p : t * per + p + 1, :] = flat[:1, p * channels : (p + 1) * channels]
    for t, part in enumerate(split3(gain[...])):
        tail[2 * per + t : 2 * per + t + 1, :] = part.astype(F32)
    message[cells:, :] = tail[...].astype(BF16)


def copy_pieces(pieces, refs, whole, sems):
    copies = []
    for n, (ref, (row_at, column_at)) in enumerate(zip(refs, pieces)):
        rows, columns = ref.shape
        row, column = row_at(), column_at()
        copy = pltpu.make_async_copy(
            ref,
            whole.at[
                pl.ds(row if isinstance(row, int) else pl.multiple_of(row, rows), rows),
                pl.ds(column if isinstance(column, int) else pl.multiple_of(column, columns), columns),
            ],
            sems.at[n],
        )
        copy.start()
        copies.append(copy)
    return copies


def hidden_grad_kernel(pieces, n_col, *refs):
    ups, refs = refs[:n_col], refs[n_col:]
    weights, (out, whole, sems) = refs[: len(pieces)], refs[len(pieces) :]
    copies = copy_pieces(pieces, weights, whole, sems)
    channels = ups[0].shape[1]
    for copy in copies:
        copy.wait()
    hidden = out.shape[1]
    tile = min(512, hidden)
    for start in range(0, hidden, tile):
        total = jnp.zeros((out.shape[0], tile), F32)
        for k in range(n_col):
            total += lax.dot_general(
                ups[k][...],
                whole[start : start + tile, k * channels : (k + 1) * channels],
                (((1,), (1,)), ((), ())),
                preferred_element_type=F32,
            )
        out[:, start : start + tile] = total


def mlp_kernel(pieces, n_col, hidden_grad, *refs):
    messages, refs = refs[:n_col], refs[n_col:]
    weights, refs = refs[: len(pieces)], refs[len(pieces) :]
    outs, refs = refs[:n_col], refs[n_col:]
    hidden, whole, normed, scaled, act_grad, sems = refs
    copies = copy_pieces(pieces, weights, whole, sems)
    cells, channels = outs[0].shape
    all_channels = n_col * channels
    per = cells // channels

    means, gains = [], []
    for message in messages:
        tail = message[cells:, :].astype(F32)
        flat = tail[:per, :] + tail[per : 2 * per, :]
        row = jnp.concatenate([flat[p : p + 1, :] for p in range(per)], axis=1)
        means.append(jnp.broadcast_to(row, (128, cells)).T[:, :1])
        gains.append(tail[2 * per : 2 * per + 1, :] + tail[2 * per + 1 : 2 * per + 2, :] + tail[2 * per + 2 : 2 * per + 3, :])
    centre = sum(means) * (1.0 / n_col)
    spread = jnp.zeros((cells, 1), F32)
    for k, message in enumerate(messages):
        centred = message[:cells, :].astype(F32) + (means[k] - centre)
        normed[k] = centred
        spread += jnp.sum(centred * centred, axis=1, keepdims=True)
    inv_std = lax.rsqrt(spread * (1.0 / all_channels) + EPSILON)
    for k in range(n_col):
        value = normed[k] * inv_std
        normed[k] = value
        scaled[:, k * channels : (k + 1) * channels] = (value * gains[k]).astype(BF16)
    for copy in copies:
        copy.wait()
    width = hidden.shape[1]
    tile = min(256, width)
    for start in range(0, width, tile):
        preact = jnp.dot(scaled[...], whole[:, start : start + tile], preferred_element_type=F32)
        phi = 0.5 * (1.0 + lax.erf(preact * math.sqrt(0.5)))
        hidden[:, start : start + tile] = (preact * phi).astype(BF16)
        slope = phi + preact * jnp.exp(-0.5 * preact * preact) * (1.0 / math.sqrt(2.0 * math.pi))
        act_grad[:, start : start + tile] = (hidden_grad[:, start : start + tile] * slope).astype(BF16)
    first, second = jnp.zeros((cells, 1), F32), jnp.zeros((cells, 1), F32)
    grads = []
    for k in range(n_col):
        grad = lax.dot_general(
            act_grad[...],
            whole[k * channels : (k + 1) * channels, :],
            (((1,), (1,)), ((), ())),
            preferred_element_type=F32,
        ) * gains[k]
        grads.append(grad)
        first += jnp.sum(grad, axis=1, keepdims=True)
        second += jnp.sum(grad * normed[k], axis=1, keepdims=True)
    first, second = first * (1.0 / all_channels), second * (1.0 / all_channels)
    for k in range(n_col):
        outs[k][...] = (inv_std * (grads[k] - first - normed[k] * second)).astype(BF16)


def branch_kernel(pieces, n_col, hidden, *refs):
    weights, refs = refs[: len(pieces)], refs[len(pieces) :]
    outs, (whole, sems) = refs[:n_col], refs[n_col:]
    copies = copy_pieces(pieces, weights, whole, sems)
    channels = outs[0].shape[1]
    for copy in copies:
        copy.wait()
    for k in range(n_col):
        outs[k][...] = jnp.dot(
            hidden[...], whole[:, k * channels : (k + 1) * channels], preferred_element_type=F32
        ).astype(BF16)


def grad_sum_kernel(dims, kinds, n_col, *refs):
    parts, refs = refs[:n_col], refs[n_col:]
    total, refs = refs[0], refs[1:]
    outs, (blocks, corner) = refs[: len(kinds)], refs[len(kinds) :]
    for lane in range(blocks.shape[0]):
        lanes = slice(lane * 128, (lane + 1) * 128)
        blocks[lane] = sum(part[:, lanes].astype(F32) for part in parts)
        total[:, lanes] = blocks[lane]
    emit_strips(blocks, corner, outs, kinds, *dims)


def backward_conv_kernel(dims, kinds, grad, taps, upstream, *rest):
    halos, (out, pad, shifted) = rest[: len(kinds)], rest[len(kinds) :]
    height, breadth = dims
    fill_padded(pad, grad, halos, kinds, height, breadth)

    def store(rows, lanes, total):
        out[rows, lanes] = total + upstream[rows, lanes].astype(F32)

    convolve(pad, shifted, taps, height, breadth, True, store)


def call(kernel, out_shape, in_specs, scratch, flops=0, bytes_accessed=1 << 20, transcendentals=0):
    return pl.pallas_call(
        kernel,
        out_shape=out_shape,
        in_specs=in_specs,
        out_specs=jax.tree.map(lambda _: pl.BlockSpec(memory_space=pltpu.VMEM), out_shape),
        scratch_shapes=scratch,
        compiler_params=pltpu.CompilerParams(vmem_limit_bytes=VMEM_LIMIT),
        cost_estimate=pl.CostEstimate(
            flops=flops, bytes_accessed=bytes_accessed, transcendentals=transcendentals
        ),
    )


IN_VMEM = pl.BlockSpec(memory_space=pltpu.VMEM)
ANYWHERE = pl.BlockSpec(memory_space=pl.ANY)


def spread_weights(w_in, w_out):
    n_sec, n_row, n_col = (lax.axis_size(a) for a in ("section", "row", "col"))
    channels, hidden = w_in.shape[0] * n_row // n_col, w_in.shape[1]
    if n_row != n_col or n_row & (n_row - 1) or n_sec & (n_sec - 1):
        order = jnp.arange(n_col) ^ lax.axis_index("col")
        whole_in = lax.all_gather(w_in, "row", axis=0, tiled=True)
        whole_in = whole_in.reshape(n_col, channels, hidden)[order].reshape(-1, hidden)
        whole_out = lax.all_gather(w_out, "row", axis=0, tiled=True)
        whole_out = lax.all_to_all(whole_out, "col", 0, 1, tiled=True)
        whole_out = whole_out.reshape(hidden, n_col, channels)[:, order].reshape(hidden, -1)
        none = (lambda: 0, lambda: 0)
        return [whole_in], [none], [whole_out], [none]

    section = lax.axis_index("section")
    share = hidden // n_sec

    def place(row_bits, sec_bits):
        block = lambda: ((lax.axis_index("row") ^ row_bits) ^ lax.axis_index("col")) * channels
        part = (lambda: 0) if sec_bits is None else (lambda: (lax.axis_index("section") ^ sec_bits) * share)
        return block, part

    mine_out = lax.dynamic_slice_in_dim(w_out, section * share, share, 0)
    mine_out = lax.ppermute(
        mine_out,
        ("row", "col"),
        [(r * n_col + z, z * n_col + r) for r in range(n_row) for z in range(n_col)],
    )
    far = [b for b in bits_of(n_row) if b > 1]
    mine_in = lax.dynamic_slice_in_dim(w_in, section * share, share, 1)

    def spread(piece, keep):
        got = {(0, 0): piece}
        for bit in far:
            got |= {(r ^ bit, s): swap(x, "row", bit) for (r, s), x in got.items()}
        for bit in bits_of(n_sec):
            got |= {
                (r, s ^ bit): swap(x, "section", bit)
                for (r, s), x in got.items()
                if keep or r > 0
            }
        return got

    got_in = {k: x for k, x in spread(mine_in, False).items() if k[0] > 0}
    got_in[0, None] = w_in
    got_out = spread(mine_out, True)
    for got in (got_in, got_out):
        for bit in bits_of(n_row)[:1]:
            got |= {(r ^ bit, s): swap(x, "row", bit) for (r, s), x in got.items()}
    return (
        list(got_in.values()),
        [place(*k) for k in got_in],
        list(got_out.values()),
        [place(*k)[::-1] for k in got_out],
    )


def local(image, conv_kernel, norm_gain, w_in, w_out, upstream):
    height, breadth, channels = image.shape
    dims = (height, breadth)
    cells = height * breadth
    n_sec, n_row, n_col = (lax.axis_size(a) for a in ("section", "row", "col"))
    all_channels, hidden = n_col * channels, w_in.shape[1]
    kinds = halo_kinds(n_sec, n_row)
    strips = [
        jax.ShapeDtypeStruct((halo_rows(k, height, breadth), channels), BF16) for k in kinds
    ]
    corner = pltpu.VMEM((round_up(MARGIN * MARGIN, 16), 128), F32)
    blocks = pltpu.VMEM((channels // 128, cells, 128), F32)
    padded = [
        pltpu.VMEM((channels // 128, (height + 2 * MARGIN) * padded_width(breadth), 128), F32),
        pltpu.VMEM((KERNEL, (height + 2 * MARGIN) * breadth, 128), F32),
    ]
    conv_cost = dict(flops=2 * KERNEL * KERNEL * cells * channels * 30)

    def exchange(sent):
        return [halo_permute(s, k, n_sec, n_row) for s, k in zip(sent, kinds)]

    def to_col(parts):
        return [p if k == 0 else swap(p, "col", k) for k, p in enumerate(parts)]

    flat_image = image.reshape(cells, channels)
    flat_up = upstream.reshape(cells, channels)
    sent = call(
        functools.partial(strips_kernel, dims, kinds),
        strips,
        [IN_VMEM],
        [blocks, corner],
    )(flat_image)
    halos = exchange(sent)
    in_refs, in_pieces, out_refs, out_pieces = spread_weights(w_in, w_out)
    ups = to_col([flat_up] * n_col)
    rows = message_rows(cells, channels)
    message = call(
        functools.partial(forward_conv_kernel, dims, kinds),
        jax.ShapeDtypeStruct((rows, channels), BF16),
        [IN_VMEM] * (3 + len(kinds)),
        padded + [pltpu.VMEM((cells, channels), F32), pltpu.VMEM((rows - cells, channels), F32)],
        **conv_cost,
    )(flat_image, conv_kernel, norm_gain.reshape(1, channels), *halos)
    messages = to_col([message] * n_col)

    product = 2 * cells * all_channels * hidden
    weight = pltpu.VMEM((all_channels, hidden), BF16)
    weight_t = pltpu.VMEM((hidden, all_channels), BF16)
    hidden_grad = call(
        functools.partial(hidden_grad_kernel, out_pieces, n_col),
        jax.ShapeDtypeStruct((cells, hidden), F32),
        [IN_VMEM] * n_col + [ANYWHERE] * len(out_refs),
        [weight_t, pltpu.SemaphoreType.DMA((len(out_refs),))],
        flops=product,
    )(*ups, *out_refs)
    part = jax.ShapeDtypeStruct((cells, channels), BF16)
    *grads, act = call(
        functools.partial(mlp_kernel, in_pieces, n_col),
        [part] * n_col + [jax.ShapeDtypeStruct((cells, hidden), BF16)],
        [IN_VMEM] * (1 + n_col) + [ANYWHERE] * len(in_refs),
        [
            weight,
            pltpu.VMEM((n_col, cells, channels), F32),
            pltpu.VMEM((cells, all_channels), BF16),
            pltpu.VMEM((cells, hidden), BF16),
            pltpu.SemaphoreType.DMA((len(in_refs),)),
        ],
        flops=2 * product,
        transcendentals=2 * cells * hidden,
    )(hidden_grad, *messages, *in_refs)
    grads = to_col(grads)
    branches = call(
        functools.partial(branch_kernel, out_pieces, n_col),
        [part] * n_col,
        [IN_VMEM] + [ANYWHERE] * len(out_refs),
        [weight_t, pltpu.SemaphoreType.DMA((len(out_refs),))],
        flops=product,
    )(act, *out_refs)
    branches = to_col(branches)
    mixed_grad, *sent = call(
        functools.partial(grad_sum_kernel, dims, kinds, n_col),
        [jax.ShapeDtypeStruct((cells, channels), F32)] + strips,
        [IN_VMEM] * n_col,
        [blocks, corner],
    )(*grads)
    halos = exchange(sent)
    image_grad = call(
        functools.partial(backward_conv_kernel, dims, kinds),
        jax.ShapeDtypeStruct((cells, channels), F32),
        [IN_VMEM] * (3 + len(kinds)),
        padded,
        **conv_cost,
    )(mixed_grad, conv_kernel, flat_up, *halos)
    output = (flat_image.astype(F32) + sum(b.astype(F32) for b in branches)).astype(BF16)
    return output.reshape(image.shape), image_grad.reshape(image.shape)


def solution(mesh):
    in_specs = (
        P("section", "row", "col"),
        P(None, None, "col"),
        P("col"),
        P("row", "col"),
        P("row", "col"),
        P("section", "row", "col"),
    )
    out_specs = (P("section", "row", "col"), P("section", "row", "col"))
    return jax.shard_map(local, mesh=mesh, in_specs=in_specs, out_specs=out_specs, check_vma=False)
```

time: 197 us -> 98.8 us (0.50)
  waiting for transfers between devices: 81.9 us -> 30.7 us
  blocking collectives: 49.1 us -> 0 us
  starting transfers between devices: 26.6 us -> 56.4 us
  matrix products: 15.7 us -> 0 us
  between operations: 14 us -> 0.85 us
  Pallas kernels: 0 us -> 8.81 us
  other arithmetic: 7.88 us -> 0.76 us
    all_gather x3 -> x0, waiting for transfers between devices: 39.3 us -> none  [the longest x1 26 us: local(): lax.all_gather(w_out, 'row', axis=0, tiled=True)]
    reduce_scatter x2 -> x0, waiting for transfers between devices: 34.2 us -> none  [the longest x1 18.8 us: local(): lax.psum_scatter(feature_terms.astype(jnp.bfloat16), 'col', scatter_dimen...]
    ppermute x8 -> x35, starting transfers between devices: 26.4 us -> 56.4 us  [the longest x24 26.3 us: swap(): return lax.ppermute(x, axis, [(i, i ^ bit) for i in range(count)])]
    psum x2 -> x0, blocking collectives: 28.9 us -> none  [the longest x1 15.4 us: local(): lax.psum((jnp.sum(mixed, axis=-1), jnp.sum(mixed * mixed, axis=-1)), 'col')]
    ppermute x8 -> x35, waiting for transfers between devices: 6.37 us -> 30.7 us  [the longest x24 23 us: swap(): return lax.ppermute(x, axis, [(i, i ^ bit) for i in range(count)])]
    all_gather x1 -> x0, blocking collectives: 20.2 us -> none  [local(): features = lax.all_gather(scaled, 'col', axis=1, tiled=True)]
    dot_general x4 -> x0, matrix products: 15.7 us -> none  [the longest x2 7.33 us: transposed(): lax.dot_general(left, right, (((1,), (1,)), ((), ())), preferred_element_...]
    pallas_call x0 -> x7, Pallas kernels: none -> 8.81 us  [the longest x1 3.17 us: local(): call(functools.partial(mlp_kernel, in_pieces, n_col), [part] * n_col + [j...]
  transfers between devices with their start and end apart: 13 -> 35, of which waited for: 8 -> 12; matrix products, arithmetic and copies ran while one was open for 9% -> 1% of each run, Pallas kernels for 0% -> 4%
where the time goes in v1:
time: 98.8 us; the launch traced here: 98.6 us
  starting transfers between devices  56.4 us (57%)
  waiting for transfers between devices  30.7 us (31%)
  Pallas kernels  8.81 us (9%)
  local copies, waits for them, and re-layouts  1.1 us (1%)
    ppermute x24, starting transfers between devices, swap(): return lax.ppermute(x, axis, [(i, i ^ bit) for i in range(count)])  26.3 us
    ppermute x24, waiting for transfers between devices, swap(): return lax.ppermute(x, axis, [(i, i ^ bit) for i in range(count)])  23 us
    ppermute x4, starting transfers between devices, halo_permute(): return lax.ppermute(strip, ('section', 'row'), pairs)  15.6 us
    ppermute x4, starting transfers between devices, halo_permute(): return lax.ppermute(strip, 'row', rows[kind[1]])  8.37 us
    ppermute x1, starting transfers between devices, spread_weights(): lax.ppermute(mine_out, ('row', 'col'), [(r * n_col + z, z * n_col + r) fo...  4.73 us
    ppermute x4, waiting for transfers between devices, halo_permute(): return lax.ppermute(strip, ('section', 'row'), pairs)  3.62 us
    pallas_call x1, Pallas kernels, local(): call(functools.partial(mlp_kernel, in_pieces, n_col), [part] * n_col + [j...  3.17 us
    ppermute x4, waiting for transfers between devices, halo_permute(): return lax.ppermute(strip, 'row', rows[kind[1]])  3.07 us
  transfers between devices with their start and end apart: 35, of which 12 were waited for; matrix products, arithmetic and copies ran while one was open for 1% of the time, Pallas kernels for 4%

profile of v1, /device:TPU:1, one launch (start us, length us, event | category | flops | bytes accessed | tf_op | source)
XLA Modules:
  0.0 98.6 jit_solution(652717976328525135)
XLA Ops:
  0.6 0.0 copy-start
  0.7 1.0 %copy-done = bf16[1024,256]{1,0:T(8,128)(2,1)S(1)} copy-done((bf16[1024,256]{1,0:T(8,128)(2,1)S(1)}, bf16[1024,256]{1,0:T(8,128)(2,1)}, u32[]{:S(2)}) %copy-start) | copy-done | bytes 524312
  1.7 0.0 copy-start.2
  1.7 4.7 %collective-permute-start.3 = (bf16[512,256]{1,0:T(8,128)(2,1)S(1)}, bf16[512,256]{1,0:T(8,128)(2,1)S(1)}, u32[]{:S(2)}, u32[]{:S(2)}) collective-permute-start(bf16[512,256]{1,0:T(8,128)(2,1)S(1)} %constant_dynamic-slice_fusion.1), channel_id=1, source_target_pairs={{0,0},{1,4},{2,8},{3,12},{4,1},{5,5},{6,9},{7,13},{8,2},{9,6},{10,... | collective-permute-start | bytes 786440 | tf_op jit(solution)/shard_map/ppermute | solution.py:398
  6.5 0.0 copy-start.4
  6.5 0.0 copy-start.1
  6.5 3.3 %collective-permute-start.19 = (bf16[256,512]{1,0:T(8,128)(2,1)S(1)}, bf16[256,512]{1,0:T(8,128)(2,1)S(1)}, u32[]{:S(2)}, u32[]{:S(2)}) collective-permute-start(bf16[256,512]{1,0:T(8,128)(2,1)S(1)} %constant_dynamic-slice_fusion), channel_id=1, source_target_pairs={{0,8},{4,12},{8,0},{12,4},{1,9},{5,13},{9,1},{13,5},{2,10},{6,14},... | collective-permute-start | bytes 786440 | tf_op jit(solution)/shard_map/ppermute | solution.py:28
  9.8 1.0 %collective-permute-done.3.refs_4_.refs_0_ = bf16[512,256]{1,0:T(8,128)(2,1)S(1)} collective-permute-done((bf16[512,256]{1,0:T(8,128)(2,1)S(1)}, bf16[512,256]{1,0:T(8,128)(2,1)S(1)}, u32[]{:S(2)}, u32[]{:S(2)}) %collective-permute-start.3) | collective-permute-done | bytes 262176 | tf_op jit(solution)/shard_map/ppermute | solution.py:398
  10.8 6.1 %collective-permute-start.4 = (bf16[512,256]{1,0:T(8,128)(2,1)S(1)}, bf16[512,256]{1,0:T(8,128)(2,1)S(1)}, u32[]{:S(2)}, u32[]{:S(2)}) collective-permute-start(bf16[512,256]{1,0:T(8,128)(2,1)S(1)} %collective-permute-done.3.refs_4_.refs_0_), channel_id=1, source_target_pairs={{0,8},{4,12},{8,0},{12,4},{1,9},{5,13},{9,1},{13,5},{2,10},{6,14},... | collective-permute-start | bytes 786440 | tf_op jit(solution)/shard_map/ppermute | solution.py:28
  16.9 0.1 shard_map.78
  16.9 7.2 %collective-permute-start.14 = (bf16[16,256]{1,0:T(8,128)(2,1)S(1)}, bf16[16,256]{1,0:T(8,128)(2,1)S(1)}, u32[]{:S(2)}, u32[]{:S(2)}) collective-permute-start(bf16[16,256]{1,0:T(8,128)(2,1)S(1)} %get-tuple-element.25), channel_id=1, source_target_pairs={{0,20},{8,28},{4,16},{12,24},{16,4},{24,12},{20,0},{28,8},{1,21},{... | collective-permute-start | bytes 24584 | tf_op jit(solution)/shard_map/ppermute | solution.py:70
  24.2 1.9 %collective-permute-start.15 = (bf16[16,256]{1,0:T(8,128)(2,1)S(1)}, bf16[16,256]{1,0:T(8,128)(2,1)S(1)}, u32[]{:S(2)}, u32[]{:S(2)}) collective-permute-start(bf16[16,256]{1,0:T(8,128)(2,1)S(1)} %get-tuple-element.26), channel_id=1, source_target_pairs={{4,24},{8,20},{20,8},{24,4},{5,25},{9,21},{21,9},{25,5},{6,26},{10... | collective-permute-start | bytes 24584 | tf_op jit(solution)/shard_map/ppermute | solution.py:70
  26.1 0.3 collective-permute-start.11
  26.4 0.0 collective-permute-done.14.rest_3_
  26.4 0.0 collective-permute-start.12
  26.4 3.6 %collective-permute-done.15.rest_4_ = bf16[16,256]{1,0:T(8,128)(2,1)S(1)} collective-permute-done((bf16[16,256]{1,0:T(8,128)(2,1)S(1)}, bf16[16,256]{1,0:T(8,128)(2,1)S(1)}, u32[]{:S(2)}, u32[]{:S(2)}) %collective-permute-start.15) | collective-permute-done | bytes 8224 | tf_op jit(solution)/shard_map/ppermute | solution.py:70
  30.0 1.9 %collective-permute-start.13 = (bf16[48,256]{1,0:T(8,128)(2,1)S(1)}, bf16[48,256]{1,0:T(8,128)(2,1)S(1)}, u32[]{:S(2)}, u32[]{:S(2)}) collective-permute-start(bf16[48,256]{1,0:T(8,128)(2,1)S(1)} %get-tuple-element.24), channel_id=1, source_target_pairs={{4,8},{8,4},{5,9},{9,5},{6,10},{10,6},{7,11},{11,7},{20,24},{24,20... | collective-permute-start | bytes 73736 | tf_op jit(solution)/shard_map/ppermute | solution.py:64
  32.0 0.0 copy-start.5
  32.0 1.9 %collective-permute-start.2 = (bf16[256,256]{1,0:T(8,128)(2,1)S(1)}, bf16[256,256]{1,0:T(8,128)(2,1)S(1)}, u32[]{:S(2)}, u32[]{:S(2)}) collective-permute-start(bf16[256,256]{1,0:T(8,128)(2,1)S(1)} %bitcast.6), channel_id=1, source_target_pairs={{0,3},{1,2},{2,1},{3,0},{4,7},{5,6},{6,5},{7,4},{8,11},{9,10},{10,... | collective-permute-start | bytes 393224 | tf_op jit(solution)/shard_map/ppermute | solution.py:28
  33.9 1.6 %collective-permute-done.13.rest_2_ = bf16[48,256]{1,0:T(8,128)(2,1)S(1)} collective-permute-done((bf16[48,256]{1,0:T(8,128)(2,1)S(1)}, bf16[48,256]{1,0:T(8,128)(2,1)S(1)}, u32[]{:S(2)}, u32[]{:S(2)}) %collective-permute-start.13) | collective-permute-done | bytes 24608 | tf_op jit(solution)/shard_map/ppermute | solution.py:64
  35.5 0.3 collective-permute-start.5
  35.7 0.0 collective-permute-done.19.refs_4_
  35.7 1.2 %collective-permute-start.20 = (bf16[256,512]{1,0:T(8,128)(2,1)S(1)}, bf16[256,512]{1,0:T(8,128)(2,1)S(1)}, u32[]{:S(2)}, u32[]{:S(2)}) collective-permute-start(bf16[256,512]{1,0:T(8,128)(2,1)S(1)} %collective-permute-done.19.refs_4_), channel_id=1, source_target_pairs={{0,16},{16,0},{1,17},{17,1},{2,18},{18,2},{3,19},{19,3},{4,20},{20... | collective-permute-start | bytes 786440 | tf_op jit(solution)/shard_map/ppermute | solution.py:28
  36.9 0.3 collective-permute-start.6
  37.2 1.6 %shard_map.79.refs_0_ = bf16[272,256]{1,0:T(8,128)(2,1)S(1)} custom-call(bf16[256,256]{1,0:T(8,128)(2,1)S(1)} %bitcast.12, f32[7,7,256]{2,1,0:T(8,128)S(1)} %copy-done.4, f32[1,256]{1,0:T(1,128)S(1)} %bitcast.13, bf16[48,256]{1,0:T(8,128)(2,1)S(1)} %collective-permute-done.11.rest_0_, bf16[48,256]{1,0:T(8,128)(2,1)S(1)} %collective-permute-done.12.rest_1_, ...), custom_call_target="tpu_custom_call" | custom-call | flops 192675840 | bytes 1048576 | tf_op jit(solution)/shard_map/pallas_call | solution.py:468
  38.8 0.0 collective-permute-done.2.refs_3_
  38.8 0.8 collective-permute-start.18
  39.5 7.0 %collective-permute-done.1.refs_2_ = bf16[256,256]{1,0:T(8,128)(2,1)S(1)} collective-permute-done((bf16[256,256]{1,0:T(8,128)(2,1)S(1)}, bf16[256,256]{1,0:T(8,128)(2,1)S(1)}, u32[]{:S(2)}, u32[]{:S(2)}) %collective-permute-start.1) | collective-permute-done | bytes 131104 | tf_op jit(solution)/shard_map/ppermute | solution.py:28
  46.5 0.3 collective-permute-start
  46.8 3.5 %collective-permute-done.refs_1_ = bf16[256,256]{1,0:T(8,128)(2,1)S(1)} collective-permute-done((bf16[256,256]{1,0:T(8,128)(2,1)S(1)}, bf16[256,256]{1,0:T(8,128)(2,1)S(1)}, u32[]{:S(2)}, u32[]{:S(2)}) %collective-permute-start) | collective-permute-done | bytes 131104 | tf_op jit(solution)/shard_map/ppermute | solution.py:28
  50.4 0.0 collective-permute-start.7
  50.4 0.0 collective-permute-done.5.refs_6_.refs_2_
  50.4 0.5 collective-permute-start.9
  50.9 0.1 collective-permute-start.23
  50.9 0.4 collective-permute-start.8
  51.4 0.1 collective-permute-start.10
  51.5 0.4 collective-permute-done.7.refs_8_.refs_4_
  51.9 0.1 collective-permute-start.21
  52.0 0.2 collective-permute-done.9.refs_10_.refs_6_
  52.3 0.1 collective-permute-start.22
  52.4 1.0 collective-permute-done.8.refs_9_.refs_5_
  53.4 1.6 %collective-permute-start.17 = (bf16[272,256]{1,0:T(8,128)(2,1)S(1)}, bf16[272,256]{1,0:T(8,128)(2,1)S(1)}, u32[]{:S(2)}, u32[]{:S(2)}) collective-permute-start(bf16[272,256]{1,0:T(8,128)(2,1)S(1)} %shard_map.79.refs_0_), channel_id=1, source_target_pairs={{0,2},{1,3},{2,0},{3,1},{4,6},{5,7},{6,4},{7,5},{8,10},{9,11},{10,... | collective-permute-start | bytes 417800 | tf_op jit(solution)/shard_map/ppermute | solution.py:28
  55.0 1.5 %collective-permute-start.16 = (bf16[272,256]{1,0:T(8,128)(2,1)S(1)}, bf16[272,256]{1,0:T(8,128)(2,1)S(1)}, u32[]{:S(2)}, u32[]{:S(2)}) collective-permute-start(bf16[272,256]{1,0:T(8,128)(2,1)S(1)} %shard_map.79.refs_0_), channel_id=1, source_target_pairs={{0,1},{1,0},{2,3},{3,2},{4,5},{5,4},{6,7},{7,6},{8,9},{9,8},{10,11... | collective-permute-start | bytes 417800 | tf_op jit(solution)/shard_map/ppermute | solution.py:28
  56.5 1.1 %shard_map.77.hidden_grad = f32[256,1024]{1,0:T(8,128)S(1)} custom-call(bf16[256,256]{1,0:T(8,128)(2,1)S(1)} %bitcast.9, bf16[256,256]{1,0:T(8,128)(2,1)S(1)} %collective-permute-done.refs_1_, bf16[256,256]{1,0:T(8,128)(2,1)S(1)} %collective-permute-done.1.refs_2_, bf16[256,256]{1,0:T(8,128)(2,1)S(1)} %collective-permute-done.2.refs_3_, ...), custom_call_target="tpu_custom_call" | custom-call | flops 536870912 | bytes 1048576 | tf_op jit(solution)/shard_map/pallas_call | solution.py:480
  57.6 5.0 %collective-permute-done.17.refs_2_ = bf16[272,256]{1,0:T(8,128)(2,1)S(1)} collective-permute-done((bf16[272,256]{1,0:T(8,128)(2,1)S(1)}, bf16[272,256]{1,0:T(8,128)(2,1)S(1)}, u32[]{:S(2)}, u32[]{:S(2)}) %collective-permute-start.17) | collective-permute-done | bytes 139296 | tf_op jit(solution)/shard_map/ppermute | solution.py:28
  62.6 3.2 %shard_map.80 = (bf16[256,256]{1,0:T(8,128)(2,1)S(1)}, bf16[256,256]{1,0:T(8,128)(2,1)S(1)}, bf16[256,256]{1,0:T(8,128)(2,1)S(1)}, bf16[256,256]{1,0:T(8,128)(2,1)S(1)}, bf16[256,1024]{1,0:T(8,128)(2,1)S(1)}) custom-call(f32[256,1024]{1,0:T(8,128)S(1)} %shard_map.77.hidden_grad, bf16[272,256]{1,0:T(8,128)(2,1)S(1)} %shard_map.79.refs_0_, ...), custom_call_target="tpu_custom_call" | custom-call | flops 1073741824 | bytes 1048576 | tf_op jit(solution)/shard_map/pallas_call | solution.py:488
  65.8 0.7 collective-permute-start.27
  66.4 2.6 %collective-permute-start.28 = (bf16[256,256]{1,0:T(8,128)(2,1)S(1)}, bf16[256,256]{1,0:T(8,128)(2,1)S(1)}, u32[]{:S(2)}, u32[]{:S(2)}) collective-permute-start(bf16[256,256]{1,0:T(8,128)(2,1)S(1)} %get-tuple-element.34), channel_id=1, source_target_pairs={{0,2},{1,3},{2,0},{3,1},{4,6},{5,7},{6,4},{7,5},{8,10},{9,11},{10,... | collective-permute-start | bytes 393224 | tf_op jit(solution)/shard_map/ppermute | solution.py:28
  69.0 0.4 collective-permute-start.29
  69.4 1.1 %shard_map.81 = (bf16[256,256]{1,0:T(8,128)(2,1)S(1)}, bf16[256,256]{1,0:T(8,128)(2,1)S(1)}, bf16[256,256]{1,0:T(8,128)(2,1)S(1)}, bf16[256,256]{1,0:T(8,128)(2,1)S(1)}) custom-call(bf16[256,1024]{1,0:T(8,128)(2,1)S(1)} %get-tuple-element.27.hidden, bf16[512,256]{1,0:T(8,128)(2,1)S(1)} %collective-permute-done.3.refs_4_.refs_0_, ...), custom_call_target="tpu_custom_call" | custom-call | flops 536870912 | bytes 1048576 | tf_op jit(solution)/shard_map/pallas_call | solution.py:503
  70.5 0.1 collective-permute-start.24
  70.5 3.1 %collective-permute-start.25 = (bf16[256,256]{1,0:T(8,128)(2,1)S(1)}, bf16[256,256]{1,0:T(8,128)(2,1)S(1)}, u32[]{:S(2)}, u32[]{:S(2)}) collective-permute-start(bf16[256,256]{1,0:T(8,128)(2,1)S(1)} %get-tuple-element.30), channel_id=1, source_target_pairs={{0,2},{1,3},{2,0},{3,1},{4,6},{5,7},{6,4},{7,5},{8,10},{9,11},{10,... | collective-permute-start | bytes 393224 | tf_op jit(solution)/shard_map/ppermute | solution.py:28
  73.7 1.1 %collective-permute-start.26 = (bf16[256,256]{1,0:T(8,128)(2,1)S(1)}, bf16[256,256]{1,0:T(8,128)(2,1)S(1)}, u32[]{:S(2)}, u32[]{:S(2)}) collective-permute-start(bf16[256,256]{1,0:T(8,128)(2,1)S(1)} %get-tuple-element.31), channel_id=1, source_target_pairs={{0,3},{1,2},{2,1},{3,0},{4,7},{5,6},{6,5},{7,4},{8,11},{9,10},{10,... | collective-permute-start | bytes 393224 | tf_op jit(solution)/shard_map/ppermute | solution.py:28
  74.7 3.1 %collective-permute-done.29.refs_3_ = bf16[256,256]{1,0:T(8,128)(2,1)S(1)} collective-permute-done((bf16[256,256]{1,0:T(8,128)(2,1)S(1)}, bf16[256,256]{1,0:T(8,128)(2,1)S(1)}, u32[]{:S(2)}, u32[]{:S(2)}) %collective-permute-start.29) | collective-permute-done | bytes 131104 | tf_op jit(solution)/shard_map/ppermute | solution.py:28
  77.8 0.1 shard_map.82
  78.0 3.0 %collective-permute-start.33 = (bf16[16,256]{1,0:T(8,128)(2,1)S(1)}, bf16[16,256]{1,0:T(8,128)(2,1)S(1)}, u32[]{:S(2)}, u32[]{:S(2)}) collective-permute-start(bf16[16,256]{1,0:T(8,128)(2,1)S(1)} %get-tuple-element.40), channel_id=1, source_target_pairs={{0,20},{8,28},{4,16},{12,24},{16,4},{24,12},{20,0},{28,8},{1,21},{... | collective-permute-start | bytes 24584 | tf_op jit(solution)/shard_map/ppermute | solution.py:70
  81.0 3.4 %collective-permute-start.34 = (bf16[16,256]{1,0:T(8,128)(2,1)S(1)}, bf16[16,256]{1,0:T(8,128)(2,1)S(1)}, u32[]{:S(2)}, u32[]{:S(2)}) collective-permute-start(bf16[16,256]{1,0:T(8,128)(2,1)S(1)} %get-tuple-element.41), channel_id=1, source_target_pairs={{4,24},{8,20},{20,8},{24,4},{5,25},{9,21},{21,9},{25,5},{6,26},{10... | collective-permute-start | bytes 24584 | tf_op jit(solution)/shard_map/ppermute | solution.py:70
  84.4 1.1 %collective-permute-start.30 = (bf16[48,256]{1,0:T(8,128)(2,1)S(1)}, bf16[48,256]{1,0:T(8,128)(2,1)S(1)}, u32[]{:S(2)}, u32[]{:S(2)}) collective-permute-start(bf16[48,256]{1,0:T(8,128)(2,1)S(1)} %get-tuple-element.37), channel_id=1, source_target_pairs={{0,16},{16,0},{1,17},{17,1},{2,18},{18,2},{3,19},{19,3},{4,20},{20... | collective-permute-start | bytes 73736 | tf_op jit(solution)/shard_map/ppermute | solution.py:62
  85.5 2.7 %collective-permute-done.25 = bf16[256,256]{1,0:T(8,128)(2,1)S(1)} collective-permute-done((bf16[256,256]{1,0:T(8,128)(2,1)S(1)}, bf16[256,256]{1,0:T(8,128)(2,1)S(1)}, u32[]{:S(2)}, u32[]{:S(2)}) %collective-permute-start.25) | collective-permute-done | bytes 131104 | tf_op jit(solution)/shard_map/ppermute | solution.py:28
  88.1 3.6 %collective-permute-start.31 = (bf16[48,256]{1,0:T(8,128)(2,1)S(1)}, bf16[48,256]{1,0:T(8,128)(2,1)S(1)}, u32[]{:S(2)}, u32[]{:S(2)}) collective-permute-start(bf16[48,256]{1,0:T(8,128)(2,1)S(1)} %get-tuple-element.38), channel_id=1, source_target_pairs={{0,4},{8,12},{4,0},{12,8},{1,5},{9,13},{5,1},{13,9},{2,6},{10,14},... | collective-permute-start | bytes 73736 | tf_op jit(solution)/shard_map/ppermute | solution.py:64
  91.8 2.8 %collective-permute-start.32 = (bf16[48,256]{1,0:T(8,128)(2,1)S(1)}, bf16[48,256]{1,0:T(8,128)(2,1)S(1)}, u32[]{:S(2)}, u32[]{:S(2)}) collective-permute-start(bf16[48,256]{1,0:T(8,128)(2,1)S(1)} %get-tuple-element.39), channel_id=1, source_target_pairs={{4,8},{8,4},{5,9},{9,5},{6,10},{10,6},{7,11},{11,7},{20,24},{24,20... | collective-permute-start | bytes 73736 | tf_op jit(solution)/shard_map/ppermute | solution.py:64
  94.6 0.8 add_convert_fusion
  95.4 1.5 %collective-permute-done.32.rest_2_ = bf16[48,256]{1,0:T(8,128)(2,1)S(1)} collective-permute-done((bf16[48,256]{1,0:T(8,128)(2,1)S(1)}, bf16[48,256]{1,0:T(8,128)(2,1)S(1)}, u32[]{:S(2)}, u32[]{:S(2)}) %collective-permute-start.32) | collective-permute-done | bytes 24608 | tf_op jit(solution)/shard_map/ppermute | solution.py:64
  96.9 1.7 %shard_map.83 = f32[256,256]{1,0:T(8,128)} custom-call(f32[256,256]{1,0:T(8,128)S(1)} %get-tuple-element.36.grad, f32[7,7,256]{2,1,0:T(8,128)S(1)} %copy-done.4, bf16[256,256]{1,0:T(8,128)(2,1)S(1)} %bitcast.10, bf16[48,256]{1,0:T(8,128)(2,1)S(1)} %collective-permute-done.30.rest_0_, bf16[48,256]{1,0:T(8,128)(2,1)S(1)} %collective-permute-done.31.rest_1_, ...), custom_call_target="tpu_custom_call" | custom-call | flops 192675840 | bytes 1048576 | tf_op jit(solution)/shard_map/pallas_call | solution.py:518
  (28 shorter events, 0.1 us)
Async XLA Ops:
  0.6 1.0 %copy-start = (bf16[1024,256]{1,0:T(8,128)(2,1)S(1)}, bf16[1024,256]{1,0:T(8,128)(2,1)}, u32[]{:S(2)}) copy-start(bf16[1024,256]{1,0:T(8,128)(2,1)} %param.10) | copy-start | bytes 1572868
  0.6 5.8 %copy-start.3 = (bf16[256,1024]{1,0:T(8,128)(2,1)S(1)}, bf16[256,1024]{1,0:T(8,128)(2,1)}, u32[]{:S(2)}) copy-start(bf16[256,1024]{1,0:T(8,128)(2,1)} %refs_6_.1) | copy-start | bytes 1572868
  1.7 15.2 %copy-start.2 = (bf16[16,16,256]{2,1,0:T(8,128)(2,1)S(1)}, bf16[16,16,256]{2,1,0:T(8,128)(2,1)}, u32[]{:S(2)}) copy-start(bf16[16,16,256]{2,1,0:T(8,128)(2,1)} %param.6) | copy-start | bytes 393220
  1.7 9.1 %collective-permute-start.3 = (bf16[512,256]{1,0:T(8,128)(2,1)S(1)}, bf16[512,256]{1,0:T(8,128)(2,1)S(1)}, u32[]{:S(2)}, u32[]{:S(2)}) collective-permute-start(bf16[512,256]{1,0:T(8,128)(2,1)S(1)} %constant_dynamic-slice_fusion.1), channel_id=1, source_target_pairs={{0,0},{1,4},{2,8},{3,12},{4,1},{5,5},{6,9},{7,13},{8,2},{9,6},{10,... | collective-permute-start | bytes 786440 | tf_op jit(solution)/shard_map/ppermute | solution.py:398
  6.5 30.7 %copy-start.4 = (f32[7,7,256]{2,1,0:T(8,128)S(1)}, f32[7,7,256]{2,1,0:T(8,128)}, u32[]{:S(2)}) copy-start(f32[7,7,256]{2,1,0:T(8,128)} %taps.3) | copy-start | bytes 150532
  6.5 25.5 %copy-start.1 = (bf16[16,16,256]{2,1,0:T(8,128)(2,1)S(1)}, bf16[16,16,256]{2,1,0:T(8,128)(2,1)}, u32[]{:S(2)}) copy-start(bf16[16,16,256]{2,1,0:T(8,128)(2,1)} %param.11) | copy-start | bytes 393220
  6.5 29.2 %collective-permute-start.19 = (bf16[256,512]{1,0:T(8,128)(2,1)S(1)}, bf16[256,512]{1,0:T(8,128)(2,1)S(1)}, u32[]{:S(2)}, u32[]{:S(2)}) collective-permute-start(bf16[256,512]{1,0:T(8,128)(2,1)S(1)} %constant_dynamic-slice_fusion), channel_id=1, source_target_pairs={{0,8},{4,12},{8,0},{12,4},{1,9},{5,13},{9,1},{13,5},{2,10},{6,14},... | collective-permute-start | bytes 786440 | tf_op jit(solution)/shard_map/ppermute | solution.py:28
  10.8 26.1 %collective-permute-start.4 = (bf16[512,256]{1,0:T(8,128)(2,1)S(1)}, bf16[512,256]{1,0:T(8,128)(2,1)S(1)}, u32[]{:S(2)}, u32[]{:S(2)}) collective-permute-start(bf16[512,256]{1,0:T(8,128)(2,1)S(1)} %collective-permute-done.3.refs_4_.refs_0_), channel_id=1, source_target_pairs={{0,8},{4,12},{8,0},{12,4},{1,9},{5,13},{9,1},{13,5},{2,10},{6,14},... | collective-permute-start | bytes 786440 | tf_op jit(solution)/shard_map/ppermute | solution.py:28
  16.9 9.5 %collective-permute-start.14 = (bf16[16,256]{1,0:T(8,128)(2,1)S(1)}, bf16[16,256]{1,0:T(8,128)(2,1)S(1)}, u32[]{:S(2)}, u32[]{:S(2)}) collective-permute-start(bf16[16,256]{1,0:T(8,128)(2,1)S(1)} %get-tuple-element.25), channel_id=1, source_target_pairs={{0,20},{8,28},{4,16},{12,24},{16,4},{24,12},{20,0},{28,8},{1,21},{... | collective-permute-start | bytes 24584 | tf_op jit(solution)/shard_map/ppermute | solution.py:70
  24.2 5.9 %collective-permute-start.15 = (bf16[16,256]{1,0:T(8,128)(2,1)S(1)}, bf16[16,256]{1,0:T(8,128)(2,1)S(1)}, u32[]{:S(2)}, u32[]{:S(2)}) collective-permute-start(bf16[16,256]{1,0:T(8,128)(2,1)S(1)} %get-tuple-element.26), channel_id=1, source_target_pairs={{4,24},{8,20},{20,8},{24,4},{5,25},{9,21},{21,9},{25,5},{6,26},{10... | collective-permute-start | bytes 24584 | tf_op jit(solution)/shard_map/ppermute | solution.py:70
  26.1 5.9 %collective-permute-start.11 = (bf16[48,256]{1,0:T(8,128)(2,1)S(1)}, bf16[48,256]{1,0:T(8,128)(2,1)S(1)}, u32[]{:S(2)}, u32[]{:S(2)}) collective-permute-start(bf16[48,256]{1,0:T(8,128)(2,1)S(1)} %get-tuple-element.22), channel_id=1, source_target_pairs={{0,16},{16,0},{1,17},{17,1},{2,18},{18,2},{3,19},{19,3},{4,20},{20... | collective-permute-start | bytes 73736 | tf_op jit(solution)/shard_map/ppermute | solution.py:62
  26.4 7.5 %collective-permute-start.12 = (bf16[48,256]{1,0:T(8,128)(2,1)S(1)}, bf16[48,256]{1,0:T(8,128)(2,1)S(1)}, u32[]{:S(2)}, u32[]{:S(2)}) collective-permute-start(bf16[48,256]{1,0:T(8,128)(2,1)S(1)} %get-tuple-element.23), channel_id=1, source_target_pairs={{0,4},{8,12},{4,0},{12,8},{1,5},{9,13},{5,1},{13,9},{2,6},{10,14},... | collective-permute-start | bytes 73736 | tf_op jit(solution)/shard_map/ppermute | solution.py:64
  30.0 5.4 %collective-permute-start.13 = (bf16[48,256]{1,0:T(8,128)(2,1)S(1)}, bf16[48,256]{1,0:T(8,128)(2,1)S(1)}, u32[]{:S(2)}, u32[]{:S(2)}) collective-permute-start(bf16[48,256]{1,0:T(8,128)(2,1)S(1)} %get-tuple-element.24), channel_id=1, source_target_pairs={{4,8},{8,4},{5,9},{9,5},{6,10},{10,6},{7,11},{11,7},{20,24},{24,20... | collective-permute-start | bytes 73736 | tf_op jit(solution)/shard_map/ppermute | solution.py:64
  32.0 5.2 %copy-start.5 = (f32[256]{0:T(256)S(1)}, f32[256]{0:T(256)}, u32[]{:S(2)}) copy-start(f32[256]{0:T(256)} %param.8) | copy-start | bytes 3076
  32.0 6.8 %collective-permute-start.2 = (bf16[256,256]{1,0:T(8,128)(2,1)S(1)}, bf16[256,256]{1,0:T(8,128)(2,1)S(1)}, u32[]{:S(2)}, u32[]{:S(2)}) collective-permute-start(bf16[256,256]{1,0:T(8,128)(2,1)S(1)} %bitcast.6), channel_id=1, source_target_pairs={{0,3},{1,2},{2,1},{3,0},{4,7},{5,6},{6,5},{7,4},{8,11},{9,10},{10,... | collective-permute-start | bytes 393224 | tf_op jit(solution)/shard_map/ppermute | solution.py:28
  33.9 12.6 %collective-permute-start.1 = (bf16[256,256]{1,0:T(8,128)(2,1)S(1)}, bf16[256,256]{1,0:T(8,128)(2,1)S(1)}, u32[]{:S(2)}, u32[]{:S(2)}) collective-permute-start(bf16[256,256]{1,0:T(8,128)(2,1)S(1)} %bitcast.7), channel_id=1, source_target_pairs={{0,2},{1,3},{2,0},{3,1},{4,6},{5,7},{6,4},{7,5},{8,10},{9,11},{10,... | collective-permute-start | bytes 393224 | tf_op jit(solution)/shard_map/ppermute | solution.py:28
  35.5 14.9 %collective-permute-start.5 = (bf16[512,256]{1,0:T(8,128)(2,1)S(1)}, bf16[512,256]{1,0:T(8,128)(2,1)S(1)}, u32[]{:S(2)}, u32[]{:S(2)}) collective-permute-start(bf16[512,256]{1,0:T(8,128)(2,1)S(1)} %collective-permute-done.3.refs_4_.refs_0_), channel_id=1, source_target_pairs={{0,16},{16,0},{1,17},{17,1},{2,18},{18,2},{3,19},{19,3},{4,20},{20... | collective-permute-start | bytes 786440 | tf_op jit(solution)/shard_map/ppermute | solution.py:28
  35.7 15.2 %collective-permute-start.20 = (bf16[256,512]{1,0:T(8,128)(2,1)S(1)}, bf16[256,512]{1,0:T(8,128)(2,1)S(1)}, u32[]{:S(2)}, u32[]{:S(2)}) collective-permute-start(bf16[256,512]{1,0:T(8,128)(2,1)S(1)} %collective-permute-done.19.refs_4_), channel_id=1, source_target_pairs={{0,16},{16,0},{1,17},{17,1},{2,18},{18,2},{3,19},{19,3},{4,20},{20... | collective-permute-start | bytes 786440 | tf_op jit(solution)/shard_map/ppermute | solution.py:28
  36.9 14.5 %collective-permute-start.6 = (bf16[512,256]{1,0:T(8,128)(2,1)S(1)}, bf16[512,256]{1,0:T(8,128)(2,1)S(1)}, u32[]{:S(2)}, u32[]{:S(2)}) collective-permute-start(bf16[512,256]{1,0:T(8,128)(2,1)S(1)} %collective-permute-done.4.refs_5_.refs_1_), channel_id=1, source_target_pairs={{0,16},{16,0},{1,17},{17,1},{2,18},{18,2},{3,19},{19,3},{4,20},{20... | collective-permute-start | bytes 786440 | tf_op jit(solution)/shard_map/ppermute | solution.py:28
  38.8 12.1 %collective-permute-start.18 = (bf16[272,256]{1,0:T(8,128)(2,1)S(1)}, bf16[272,256]{1,0:T(8,128)(2,1)S(1)}, u32[]{:S(2)}, u32[]{:S(2)}) collective-permute-start(bf16[272,256]{1,0:T(8,128)(2,1)S(1)} %shard_map.79.refs_0_), channel_id=1, source_target_pairs={{0,3},{1,2},{2,1},{3,0},{4,7},{5,6},{6,5},{7,4},{8,11},{9,10},{10,... | collective-permute-start | bytes 417800 | tf_op jit(solution)/shard_map/ppermute | solution.py:28
  46.5 3.8 %collective-permute-start = (bf16[256,256]{1,0:T(8,128)(2,1)S(1)}, bf16[256,256]{1,0:T(8,128)(2,1)S(1)}, u32[]{:S(2)}, u32[]{:S(2)}) collective-permute-start(bf16[256,256]{1,0:T(8,128)(2,1)S(1)} %bitcast.8), channel_id=1, source_target_pairs={{0,1},{1,0},{2,3},{3,2},{4,5},{5,4},{6,7},{7,6},{8,9},{9,8},{10,11... | collective-permute-start | bytes 393224 | tf_op jit(solution)/shard_map/ppermute | solution.py:28
  50.4 1.5 %collective-permute-start.7 = (bf16[512,256]{1,0:T(8,128)(2,1)S(1)}, bf16[512,256]{1,0:T(8,128)(2,1)S(1)}, u32[]{:S(2)}, u32[]{:S(2)}) collective-permute-start(bf16[512,256]{1,0:T(8,128)(2,1)S(1)} %collective-permute-done.3.refs_4_.refs_0_), channel_id=1, source_target_pairs={{0,4},{4,0},{8,12},{12,8},{1,5},{5,1},{9,13},{13,9},{2,6},{6,2},{1... | collective-permute-start | bytes 786440 | tf_op jit(solution)/shard_map/ppermute | solution.py:28
  50.4 1.9 %collective-permute-start.9 = (bf16[512,256]{1,0:T(8,128)(2,1)S(1)}, bf16[512,256]{1,0:T(8,128)(2,1)S(1)}, u32[]{:S(2)}, u32[]{:S(2)}) collective-permute-start(bf16[512,256]{1,0:T(8,128)(2,1)S(1)} %collective-permute-done.5.refs_6_.refs_2_), channel_id=1, source_target_pairs={{0,4},{4,0},{8,12},{12,8},{1,5},{5,1},{9,13},{13,9},{2,6},{6,2},{1... | collective-permute-start | bytes 786440 | tf_op jit(solution)/shard_map/ppermute | solution.py:28
  50.9 11.7 %collective-permute-start.23 = (bf16[256,1024]{1,0:T(8,128)(2,1)S(1)}, bf16[256,1024]{1,0:T(8,128)(2,1)S(1)}, u32[]{:S(2)}, u32[]{:S(2)}) collective-permute-start(bf16[256,1024]{1,0:T(8,128)(2,1)S(1)} %copy-done.3), channel_id=1, source_target_pairs={{0,4},{4,0},{8,12},{12,8},{1,5},{5,1},{9,13},{13,9},{2,6},{6,2},{1... | collective-permute-start | bytes 1572872 | tf_op jit(solution)/shard_map/ppermute | solution.py:28
  50.9 2.4 %collective-permute-start.8 = (bf16[512,256]{1,0:T(8,128)(2,1)S(1)}, bf16[512,256]{1,0:T(8,128)(2,1)S(1)}, u32[]{:S(2)}, u32[]{:S(2)}) collective-permute-start(bf16[512,256]{1,0:T(8,128)(2,1)S(1)} %collective-permute-done.4.refs_5_.refs_1_), channel_id=1, source_target_pairs={{0,4},{4,0},{8,12},{12,8},{1,5},{5,1},{9,13},{13,9},{2,6},{6,2},{1... | collective-permute-start | bytes 786440 | tf_op jit(solution)/shard_map/ppermute | solution.py:28
  51.4 3.6 %collective-permute-start.10 = (bf16[512,256]{1,0:T(8,128)(2,1)S(1)}, bf16[512,256]{1,0:T(8,128)(2,1)S(1)}, u32[]{:S(2)}, u32[]{:S(2)}) collective-permute-start(bf16[512,256]{1,0:T(8,128)(2,1)S(1)} %collective-permute-done.6.refs_7_.refs_3_), channel_id=1, source_target_pairs={{0,4},{4,0},{8,12},{12,8},{1,5},{5,1},{9,13},{13,9},{2,6},{6,2},{1... | collective-permute-start | bytes 786440 | tf_op jit(solution)/shard_map/ppermute | solution.py:28
  51.9 10.7 %collective-permute-start.21 = (bf16[256,512]{1,0:T(8,128)(2,1)S(1)}, bf16[256,512]{1,0:T(8,128)(2,1)S(1)}, u32[]{:S(2)}, u32[]{:S(2)}) collective-permute-start(bf16[256,512]{1,0:T(8,128)(2,1)S(1)} %collective-permute-done.19.refs_4_), channel_id=1, source_target_pairs={{0,4},{4,0},{8,12},{12,8},{1,5},{5,1},{9,13},{13,9},{2,6},{6,2},{1... | collective-permute-start | bytes 786440 | tf_op jit(solution)/shard_map/ppermute | solution.py:28
  52.3 10.3 %collective-permute-start.22 = (bf16[256,512]{1,0:T(8,128)(2,1)S(1)}, bf16[256,512]{1,0:T(8,128)(2,1)S(1)}, u32[]{:S(2)}, u32[]{:S(2)}) collective-permute-start(bf16[256,512]{1,0:T(8,128)(2,1)S(1)} %collective-permute-done.20.refs_5_), channel_id=1, source_target_pairs={{0,4},{4,0},{8,12},{12,8},{1,5},{5,1},{9,13},{13,9},{2,6},{6,2},{1... | collective-permute-start | bytes 786440 | tf_op jit(solution)/shard_map/ppermute | solution.py:28
  53.4 9.2 %collective-permute-start.17 = (bf16[272,256]{1,0:T(8,128)(2,1)S(1)}, bf16[272,256]{1,0:T(8,128)(2,1)S(1)}, u32[]{:S(2)}, u32[]{:S(2)}) collective-permute-start(bf16[272,256]{1,0:T(8,128)(2,1)S(1)} %shard_map.79.refs_0_), channel_id=1, source_target_pairs={{0,2},{1,3},{2,0},{3,1},{4,6},{5,7},{6,4},{7,5},{8,10},{9,11},{10,... | collective-permute-start | bytes 417800 | tf_op jit(solution)/shard_map/ppermute | solution.py:28
  55.0 7.6 %collective-permute-start.16 = (bf16[272,256]{1,0:T(8,128)(2,1)S(1)}, bf16[272,256]{1,0:T(8,128)(2,1)S(1)}, u32[]{:S(2)}, u32[]{:S(2)}) collective-permute-start(bf16[272,256]{1,0:T(8,128)(2,1)S(1)} %shard_map.79.refs_0_), channel_id=1, source_target_pairs={{0,1},{1,0},{2,3},{3,2},{4,5},{5,4},{6,7},{7,6},{8,9},{9,8},{10,11... | collective-permute-start | bytes 417800 | tf_op jit(solution)/shard_map/ppermute | solution.py:28
  65.8 7.9 %collective-permute-start.27 = (bf16[256,256]{1,0:T(8,128)(2,1)S(1)}, bf16[256,256]{1,0:T(8,128)(2,1)S(1)}, u32[]{:S(2)}, u32[]{:S(2)}) collective-permute-start(bf16[256,256]{1,0:T(8,128)(2,1)S(1)} %get-tuple-element.33), channel_id=1, source_target_pairs={{0,1},{1,0},{2,3},{3,2},{4,5},{5,4},{6,7},{7,6},{8,9},{9,8},{10,11... | collective-permute-start | bytes 393224 | tf_op jit(solution)/shard_map/ppermute | solution.py:28
  66.4 8.3 %collective-permute-start.28 = (bf16[256,256]{1,0:T(8,128)(2,1)S(1)}, bf16[256,256]{1,0:T(8,128)(2,1)S(1)}, u32[]{:S(2)}, u32[]{:S(2)}) collective-permute-start(bf16[256,256]{1,0:T(8,128)(2,1)S(1)} %get-tuple-element.34), channel_id=1, source_target_pairs={{0,2},{1,3},{2,0},{3,1},{4,6},{5,7},{6,4},{7,5},{8,10},{9,11},{10,... | collective-permute-start | bytes 393224 | tf_op jit(solution)/shard_map/ppermute | solution.py:28
  69.0 8.9 %collective-permute-start.29 = (bf16[256,256]{1,0:T(8,128)(2,1)S(1)}, bf16[256,256]{1,0:T(8,128)(2,1)S(1)}, u32[]{:S(2)}, u32[]{:S(2)}) collective-permute-start(bf16[256,256]{1,0:T(8,128)(2,1)S(1)} %get-tuple-element.35), channel_id=1, source_target_pairs={{0,3},{1,2},{2,1},{3,0},{4,7},{5,6},{6,5},{7,4},{8,11},{9,10},{10,... | collective-permute-start | bytes 393224 | tf_op jit(solution)/shard_map/ppermute | solution.py:28
  70.5 13.9 %collective-permute-start.24 = (bf16[256,256]{1,0:T(8,128)(2,1)S(1)}, bf16[256,256]{1,0:T(8,128)(2,1)S(1)}, u32[]{:S(2)}, u32[]{:S(2)}) collective-permute-start(bf16[256,256]{1,0:T(8,128)(2,1)S(1)} %get-tuple-element.29), channel_id=1, source_target_pairs={{0,1},{1,0},{2,3},{3,2},{4,5},{5,4},{6,7},{7,6},{8,9},{9,8},{10,11... | collective-permute-start | bytes 393224 | tf_op jit(solution)/shard_map/ppermute | solution.py:28
  70.5 17.6 %collective-permute-start.25 = (bf16[256,256]{1,0:T(8,128)(2,1)S(1)}, bf16[256,256]{1,0:T(8,128)(2,1)S(1)}, u32[]{:S(2)}, u32[]{:S(2)}) collective-permute-start(bf16[256,256]{1,0:T(8,128)(2,1)S(1)} %get-tuple-element.30), channel_id=1, source_target_pairs={{0,2},{1,3},{2,0},{3,1},{4,6},{5,7},{6,4},{7,5},{8,10},{9,11},{10,... | collective-permute-start | bytes 393224 | tf_op jit(solution)/shard_map/ppermute | solution.py:28
  73.7 18.1 %collective-permute-start.26 = (bf16[256,256]{1,0:T(8,128)(2,1)S(1)}, bf16[256,256]{1,0:T(8,128)(2,1)S(1)}, u32[]{:S(2)}, u32[]{:S(2)}) collective-permute-start(bf16[256,256]{1,0:T(8,128)(2,1)S(1)} %get-tuple-element.31), channel_id=1, source_target_pairs={{0,3},{1,2},{2,1},{3,0},{4,7},{5,6},{6,5},{7,4},{8,11},{9,10},{10,... | collective-permute-start | bytes 393224 | tf_op jit(solution)/shard_map/ppermute | solution.py:28
  78.0 17.4 %collective-permute-start.33 = (bf16[16,256]{1,0:T(8,128)(2,1)S(1)}, bf16[16,256]{1,0:T(8,128)(2,1)S(1)}, u32[]{:S(2)}, u32[]{:S(2)}) collective-permute-start(bf16[16,256]{1,0:T(8,128)(2,1)S(1)} %get-tuple-element.40), channel_id=1, source_target_pairs={{0,20},{8,28},{4,16},{12,24},{16,4},{24,12},{20,0},{28,8},{1,21},{... | collective-permute-start | bytes 24584 | tf_op jit(solution)/shard_map/ppermute | solution.py:70
  81.0 14.4 %collective-permute-start.34 = (bf16[16,256]{1,0:T(8,128)(2,1)S(1)}, bf16[16,256]{1,0:T(8,128)(2,1)S(1)}, u32[]{:S(2)}, u32[]{:S(2)}) collective-permute-start(bf16[16,256]{1,0:T(8,128)(2,1)S(1)} %get-tuple-element.41), channel_id=1, source_target_pairs={{4,24},{8,20},{20,8},{24,4},{5,25},{9,21},{21,9},{25,5},{6,26},{10... | collective-permute-start | bytes 24584 | tf_op jit(solution)/shard_map/ppermute | solution.py:70
  84.4 11.0 %collective-permute-start.30 = (bf16[48,256]{1,0:T(8,128)(2,1)S(1)}, bf16[48,256]{1,0:T(8,128)(2,1)S(1)}, u32[]{:S(2)}, u32[]{:S(2)}) collective-permute-start(bf16[48,256]{1,0:T(8,128)(2,1)S(1)} %get-tuple-element.37), channel_id=1, source_target_pairs={{0,16},{16,0},{1,17},{17,1},{2,18},{18,2},{3,19},{19,3},{4,20},{20... | collective-permute-start | bytes 73736 | tf_op jit(solution)/shard_map/ppermute | solution.py:62
  88.1 7.2 %collective-permute-start.31 = (bf16[48,256]{1,0:T(8,128)(2,1)S(1)}, bf16[48,256]{1,0:T(8,128)(2,1)S(1)}, u32[]{:S(2)}, u32[]{:S(2)}) collective-permute-start(bf16[48,256]{1,0:T(8,128)(2,1)S(1)} %get-tuple-element.38), channel_id=1, source_target_pairs={{0,4},{8,12},{4,0},{12,8},{1,5},{9,13},{5,1},{13,9},{2,6},{10,14},... | collective-permute-start | bytes 73736 | tf_op jit(solution)/shard_map/ppermute | solution.py:64
  91.8 5.1 %collective-permute-start.32 = (bf16[48,256]{1,0:T(8,128)(2,1)S(1)}, bf16[48,256]{1,0:T(8,128)(2,1)S(1)}, u32[]{:S(2)}, u32[]{:S(2)}) collective-permute-start(bf16[48,256]{1,0:T(8,128)(2,1)S(1)} %get-tuple-element.39), channel_id=1, source_target_pairs={{4,8},{8,4},{5,9},{9,5},{6,10},{10,6},{7,11},{11,7},{20,24},{24,20... | collective-permute-start | bytes 73736 | tf_op jit(solution)/shard_map/ppermute | solution.py:64

commit v2 on v1

v2 whole, which is shorter than its diff:
```python
import functools
import math

import jax
import jax.numpy as jnp
from jax import lax
from jax.experimental import pallas as pl
from jax.experimental.pallas import tpu as pltpu
from jax.sharding import PartitionSpec as P

KERNEL = 7
MARGIN = KERNEL // 2
EPSILON = 1e-06
BF16, F32 = jnp.bfloat16, jnp.float32
MIB = 1024 * 1024


def round_up(value, to):
    return -(-value // to) * to


def bits_of(count):
    return [1 << b for b in range(count.bit_length() - 1)]


def swap(x, axis, bit, name=None):
    count = lax.axis_size(axis)
    with jax.named_scope(name or f"{axis}_{bit}"):
        return lax.ppermute(x, axis, [(i, i ^ bit) for i in range(count)])


def pairings(count):
    both = [[(i, i + 1) for i in range(first, count - 1, 2)] for first in range(2)]
    return [p + [(b, a) for a, b in p] for p in both if p]


def faces_up(index, pairing):
    return (index + pairing) % 2 == 0


def meet(strips, axis, name):
    with jax.named_scope(name):
        return [
            lax.ppermute(strip, axis, pairs)
            for strip, pairs in zip(strips, pairings(lax.axis_size(axis)))
        ]


def low_high(index, received):
    if not received:
        return None, None
    first = received[0]
    second = received[1] if len(received) > 1 else jnp.zeros_like(first)
    odd = index % 2 == 1
    return jnp.where(odd, first, second), jnp.where(odd, second, first)


def side_rows(height):
    return round_up(MARGIN * (height + 2 * MARGIN), 16)


def emit_top(cells, outs, height, breadth):
    size = MARGIN * breadth
    for pairing, out in enumerate(outs):
        up = faces_up(lax.axis_index("section"), pairing)
        for lane in range(cells.shape[0]):
            out[:, lane * 128 : (lane + 1) * 128] = jnp.where(
                up, cells[lane, height * breadth - size :, :], cells[lane, :size, :]
            ).astype(BF16)


def sides_kernel(dims, n_top, cells, *refs):
    height, breadth = dims
    tops, (*outs, blocks) = refs[:n_top], refs[n_top:]
    size = MARGIN * breadth
    tall = height + 2 * MARGIN
    for lane in range(blocks.shape[0]):
        lanes = slice(lane * 128, (lane + 1) * 128)
        block = blocks.at[lane]
        low, high = low_high(lax.axis_index("section"), [top[:, lanes].astype(F32) for top in tops])
        block[:size, :] = jnp.zeros((size, 128), F32) if low is None else low
        block[size : size + height * breadth, :] = cells[:, lanes].astype(F32)
        block[size + height * breadth :, :] = jnp.zeros((size, 128), F32) if high is None else high
        for pairing, out in enumerate(outs):
            up = faces_up(lax.axis_index("row"), pairing)
            columns = [
                jnp.where(
                    up,
                    block[pl.ds(breadth - MARGIN + j, tall, stride=breadth), :],
                    block[pl.ds(j, tall, stride=breadth), :],
                )
                for j in range(MARGIN)
            ]
            spare = out.shape[0] - MARGIN * tall
            if spare:
                columns.append(jnp.zeros((spare, 128), F32))
            out[:, lanes] = jnp.concatenate(columns, axis=0).astype(BF16)


LEFT = 8


def padded_width(breadth):
    return round_up(LEFT + breadth + MARGIN, 8)


def fill_padded(pad, cells, tops, columns, height, breadth):
    width = padded_width(breadth)
    tall = height + 2 * MARGIN
    for lane in range(pad.shape[0]):
        block, lanes = pad.at[lane], slice(lane * 128, (lane + 1) * 128)
        for i in range(height):
            start = (MARGIN + i) * width + LEFT
            block[start : start + breadth, :] = cells[i * breadth : (i + 1) * breadth, lanes].astype(F32)
        low, high = low_high(lax.axis_index("section"), [top[:, lanes].astype(F32) for top in tops])
        for i in range(MARGIN):
            for row, strip in ((i, low), (MARGIN + height + i, high)):
                start = row * width + LEFT
                block[start : start + breadth, :] = (
                    jnp.zeros((breadth, 128), F32)
                    if strip is None
                    else strip[i * breadth : (i + 1) * breadth, :]
                )
        low, high = low_high(lax.axis_index("row"), [c[:, lanes].astype(F32) for c in columns])
        for j in range(MARGIN):
            for column, strip in ((LEFT - MARGIN + j, low), (LEFT + breadth + j, high)):
                block[pl.ds(column, tall, stride=width), :] = (
                    jnp.zeros((tall, 128), F32)
                    if strip is None
                    else strip[j * tall : (j + 1) * tall, :]
                )


def convolve(pad, shifted, taps, height, breadth, flip, store):
    width = padded_width(breadth)
    tall = height + 2 * MARGIN
    step = 4 if height % 4 == 0 else 1
    for lane in range(pad.shape[0]):
        lanes = slice(lane * 128, (lane + 1) * 128)
        for b in range(KERNEL):
            for i in range(tall):
                start = i * width + LEFT - MARGIN + b
                shifted[b, i * breadth : (i + 1) * breadth, :] = pad[lane, start : start + breadth, :]
        for top in range(0, height, step):
            total = jnp.zeros((step * breadth, 128), F32)
            for a in range(KERNEL):
                for b in range(KERNEL):
                    p, q = (KERNEL - 1 - a, KERNEL - 1 - b) if flip else (a, b)
                    first = (top + a) * breadth
                    total += shifted[b, first : first + step * breadth, :] * taps[p, q, lanes][None, :]
            store(slice(top * breadth, (top + step) * breadth), lanes, total)


def split3(x):
    high = x.astype(BF16)
    left = x - high.astype(F32)
    mid = left.astype(BF16)
    return high, mid, (left - mid.astype(F32)).astype(BF16)


def message_rows(cells, channels):
    return 2 * cells + round_up(2 * (cells // channels) + 3, 16)


def forward_conv_kernel(dims, n_top, n_side, image, taps, gain, upstream, *refs):
    tops, columns, refs = refs[:n_top], refs[n_top : n_top + n_side], refs[n_top + n_side :]
    message, pad, shifted, mixed, tail = refs
    height, breadth = dims
    cells, channels = image.shape
    fill_padded(pad, image, tops, columns, height, breadth)

    def store(rows, lanes, total):
        mixed[rows, lanes] = total

    convolve(pad, shifted, taps, height, breadth, False, store)
    mean = jnp.sum(mixed[...], axis=1, keepdims=True) * (1.0 / channels)
    first = mean.astype(BF16).astype(F32)
    second = (mean - first).astype(BF16).astype(F32)
    message[:cells, :] = ((mixed[...] - first) - second).astype(BF16)
    tail[...] = jnp.zeros_like(tail)
    per = cells // channels
    for t, column in enumerate((first, second)):
        flat = jnp.broadcast_to(column, (cells, 128)).T
        for p in range(per):
            tail[t * per + p : t * per + p + 1, :] = flat[:1, p * channels : (p + 1) * channels]
    for t, part in enumerate(split3(gain[...])):
        tail[2 * per + t : 2 * per + t + 1, :] = part.astype(F32)
    message[cells : message.shape[0] - cells, :] = tail[...].astype(BF16)
    message[message.shape[0] - cells :, :] = upstream[...]


def copy_pieces(pieces, refs, whole, sems):
    copies = []
    for n, (ref, (row_at, column_at)) in enumerate(zip(refs, pieces)):
        rows, columns = ref.shape
        row, column = row_at(), column_at()
        copy = pltpu.make_async_copy(
            ref,
            whole.at[
                pl.ds(row if isinstance(row, int) else pl.multiple_of(row, rows), rows),
                pl.ds(column if isinstance(column, int) else pl.multiple_of(column, columns), columns),
            ],
            sems.at[n],
        )
        copy.start()
        copies.append(copy)
    return copies


def mlp_kernel(in_pieces, out_pieces, n_col, *refs):
    messages, refs = refs[:n_col], refs[n_col:]
    in_refs, refs = refs[: len(in_pieces)], refs[len(in_pieces) :]
    out_refs, refs = refs[: len(out_pieces)], refs[len(out_pieces) :]
    outs, refs = refs[:n_col], refs[n_col:]
    hidden, whole, whole_out, normed, scaled, act_grad, in_sems, out_sems = refs
    copies = copy_pieces(in_pieces, in_refs, whole, in_sems)
    out_copies = copy_pieces(out_pieces, out_refs, whole_out, out_sems)
    cells, channels = outs[0].shape
    up_at = messages[0].shape[0] - cells
    all_channels = n_col * channels
    per = cells // channels

    means, gains = [], []
    for message in messages:
        tail = message[cells:up_at, :].astype(F32)
        flat = tail[:per, :] + tail[per : 2 * per, :]
        row = jnp.concatenate([flat[p : p + 1, :] for p in range(per)], axis=1)
        means.append(jnp.broadcast_to(row, (128, cells)).T[:, :1])
        gains.append(tail[2 * per : 2 * per + 1, :] + tail[2 * per + 1 : 2 * per + 2, :] + tail[2 * per + 2 : 2 * per + 3, :])
    centre = sum(means) * (1.0 / n_col)
    spread = jnp.zeros((cells, 1), F32)
    for k, message in enumerate(messages):
        centred = message[:cells, :].astype(F32) + (means[k] - centre)
        normed[k] = centred
        spread += jnp.sum(centred * centred, axis=1, keepdims=True)
    inv_std = lax.rsqrt(spread * (1.0 / all_channels) + EPSILON)
    for k in range(n_col):
        value = normed[k] * inv_std
        normed[k] = value
        scaled[:, k * channels : (k + 1) * channels] = (value * gains[k]).astype(BF16)
    for copy in copies:
        copy.wait()
    for copy in out_copies:
        copy.wait()
    width = hidden.shape[1]
    tile = min(256, width)
    for start in range(0, width, tile):
        hidden_grad = jnp.zeros((cells, tile), F32)
        for k, message in enumerate(messages):
            hidden_grad += lax.dot_general(
                message[up_at:, :],
                whole_out[start : start + tile, k * channels : (k + 1) * channels],
                (((1,), (1,)), ((), ())),
                preferred_element_type=F32,
            )
        preact = jnp.dot(scaled[...], whole[:, start : start + tile], preferred_element_type=F32)
        phi = 0.5 * (1.0 + lax.erf(preact * math.sqrt(0.5)))
        hidden[:, start : start + tile] = (preact * phi).astype(BF16)
        slope = phi + preact * jnp.exp(-0.5 * preact * preact) * (1.0 / math.sqrt(2.0 * math.pi))
        act_grad[:, start : start + tile] = (hidden_grad * slope).astype(BF16)
    first, second = jnp.zeros((cells, 1), F32), jnp.zeros((cells, 1), F32)
    grads = []
    for k in range(n_col):
        grad = lax.dot_general(
            act_grad[...],
            whole[k * channels : (k + 1) * channels, :],
            (((1,), (1,)), ((), ())),
            preferred_element_type=F32,
        ) * gains[k]
        grads.append(grad)
        first += jnp.sum(grad, axis=1, keepdims=True)
        second += jnp.sum(grad * normed[k], axis=1, keepdims=True)
    first, second = first * (1.0 / all_channels), second * (1.0 / all_channels)
    for k in range(n_col):
        outs[k][...] = (inv_std * (grads[k] - first - normed[k] * second)).astype(BF16)


def branch_kernel(pieces, n_col, hidden, *refs):
    weights, refs = refs[: len(pieces)], refs[len(pieces) :]
    outs, (whole, sems) = refs[:n_col], refs[n_col:]
    copies = copy_pieces(pieces, weights, whole, sems)
    channels = outs[0].shape[1]
    for copy in copies:
        copy.wait()
    for k in range(n_col):
        outs[k][...] = jnp.dot(
            hidden[...], whole[:, k * channels : (k + 1) * channels], preferred_element_type=F32
        ).astype(BF16)


def grad_sum_kernel(dims, n_col, *refs):
    parts, (total, *outs, blocks) = refs[:n_col], refs[n_col:]
    for lane in range(blocks.shape[0]):
        lanes = slice(lane * 128, (lane + 1) * 128)
        blocks[lane] = sum(part[:, lanes].astype(F32) for part in parts)
        total[:, lanes] = blocks[lane]
    emit_top(blocks, outs, *dims)


def backward_conv_kernel(dims, n_top, n_side, grad, taps, upstream, *refs):
    tops, columns, refs = refs[:n_top], refs[n_top : n_top + n_side], refs[n_top + n_side :]
    out, pad, shifted = refs
    height, breadth = dims
    fill_padded(pad, grad, tops, columns, height, breadth)

    def store(rows, lanes, total):
        out[rows, lanes] = total + upstream[rows, lanes].astype(F32)

    convolve(pad, shifted, taps, height, breadth, True, store)


def call(name, vmem, kernel, out_shape, in_specs, scratch, flops=0, bytes_accessed=1 << 20, transcendentals=0):
    return pl.pallas_call(
        kernel,
        name=name,
        out_shape=out_shape,
        in_specs=in_specs,
        out_specs=jax.tree.map(lambda _: pl.BlockSpec(memory_space=pltpu.VMEM), out_shape),
        scratch_shapes=scratch,
        compiler_params=pltpu.CompilerParams(vmem_limit_bytes=vmem),
        cost_estimate=pl.CostEstimate(
            flops=flops, bytes_accessed=bytes_accessed, transcendentals=transcendentals
        ),
    )


IN_VMEM = pl.BlockSpec(memory_space=pltpu.VMEM)
ANYWHERE = pl.BlockSpec(memory_space=pl.ANY)


def tie(x, *others):
    return lax.optimization_barrier((x, others))[0]


def exchangeable():
    n_sec, n_row, n_col = (lax.axis_size(a) for a in ("section", "row", "col"))
    return n_row == n_col and not n_row & (n_row - 1) and not n_sec & (n_sec - 1)


def weights_begin(w_in, w_out):
    n_sec, n_row, n_col = (lax.axis_size(a) for a in ("section", "row", "col"))
    if not exchangeable():
        return None, None, []
    share = w_in.shape[1] // n_sec
    mine_out = lax.dynamic_slice_in_dim(w_out, lax.axis_index("section") * share, share, 0)
    with jax.named_scope("w_out_transposed"):
        mine_out = lax.ppermute(
            mine_out,
            ("row", "col"),
            [(r * n_col + z, z * n_col + r) for r in range(n_row) for z in range(n_col)],
        )
    early = {(0, None): w_in}
    for bit in bits_of(n_row)[1:]:
        early |= {(r ^ bit, None): swap(x, "row", bit, "w_in_row") for (r, _), x in early.items()}
    return mine_out, early, [swap(w_in, "row", bit, "w_in_core") for bit in bits_of(n_row)[:1]]


def weights_finish(w_in, w_out, mine_out, got_in, core_in, message, messages):
    n_sec, n_row, n_col = (lax.axis_size(a) for a in ("section", "row", "col"))
    channels, hidden = w_in.shape[0] * n_row // n_col, w_in.shape[1]
    if not exchangeable():
        order = jnp.arange(n_col) ^ lax.axis_index("col")
        whole_in = lax.all_gather(w_in, "row", axis=0, tiled=True)
        whole_in = whole_in.reshape(n_col, channels, hidden)[order].reshape(-1, hidden)
        whole_out = lax.all_gather(w_out, "row", axis=0, tiled=True)
        whole_out = lax.all_to_all(whole_out, "col", 0, 1, tiled=True)
        whole_out = whole_out.reshape(hidden, n_col, channels)[:, order].reshape(hidden, -1)
        none = (lambda: 0, lambda: 0)
        return [whole_in], [none], [whole_out], [none]

    share = hidden // n_sec

    def place(row_bits, sec_bits):
        block = lambda: ((lax.axis_index("row") ^ row_bits) ^ lax.axis_index("col")) * channels
        part = (lambda: 0) if sec_bits is None else (lambda: (lax.axis_index("section") ^ sec_bits) * share)
        return block, part

    far, core = [b for b in bits_of(n_row) if b > 1], bits_of(n_row)[:1]
    got_out = {(0, 0): tie(mine_out, message, list(got_in.values()))}
    for bit in far:
        got_out |= {(r ^ bit, s): swap(x, "row", bit, "w_out_row") for (r, s), x in got_out.items()}
    for bit in bits_of(n_sec):
        got_out |= {
            (r, s ^ bit): swap(x, "section", bit, f"w_out_section_{r}") for (r, s), x in got_out.items()
        }
    for bit in core:
        got_in |= {
            (r ^ bit, s): core_in[0] if r == 0 else swap(tie(x, messages), "row", bit, f"w_in_core_{r}")
            for (r, s), x in got_in.items()
        }
        first = {
            (r ^ bit, s): swap(tie(x, messages), "row", bit, f"w_out_core_{r}_{s}")
            for (r, s), x in got_out.items()
            if not (r and s)
        }
        got_out |= first | {
            (r ^ bit, s): swap(tie(x, list(first.values())), "row", bit, f"w_out_core_{r}_{s}")
            for (r, s), x in got_out.items()
            if r and s
        }
    return (
        list(got_in.values()),
        [place(*k) for k in got_in],
        list(got_out.values()),
        [place(*k)[::-1] for k in got_out],
    )


def local(image, conv_kernel, norm_gain, w_in, w_out, upstream):
    height, breadth, channels = image.shape
    dims = (height, breadth)
    cells = height * breadth
    n_sec, n_row, n_col = (lax.axis_size(a) for a in ("section", "row", "col"))
    all_channels, hidden = n_col * channels, w_in.shape[1]
    top = jax.ShapeDtypeStruct((MARGIN * breadth, channels), BF16)
    side = jax.ShapeDtypeStruct((side_rows(height), channels), BF16)
    n_top, n_side = len(pairings(n_sec)), len(pairings(n_row))
    padded = [
        pltpu.VMEM((channels // 128, (height + 2 * MARGIN) * padded_width(breadth), 128), F32),
        pltpu.VMEM((KERNEL, (height + 2 * MARGIN) * breadth, 128), F32),
    ]
    conv_cost = dict(flops=2 * KERNEL * KERNEL * cells * channels * 30)

    def columns_of(cell_values, tops, name):
        sent = call(
            name,
            4 * MIB,
            functools.partial(sides_kernel, dims, n_top),
            [side] * n_side,
            [IN_VMEM] * (1 + n_top),
            [pltpu.VMEM((channels // 128, (height + 2 * MARGIN) * breadth, 128), F32)],
        )(cell_values, *tops)
        return meet(sent, "row", name)

    def to_col(parts, name):
        with jax.named_scope(name):
            return [p if k == 0 else swap(p, "col", k) for k, p in enumerate(parts)]

    flat_image = image.reshape(cells, channels)
    flat_up = upstream.reshape(cells, channels)
    mine_out, early_in, core_in = weights_begin(w_in, w_out)
    size = MARGIN * breadth
    sent = [
        lax.dynamic_slice_in_dim(
            flat_image, jnp.where(faces_up(lax.axis_index("section"), p), cells - size, 0), size, 0
        )
        for p in range(n_top)
    ]
    tops = meet(sent, "section", "image_rows")
    columns = columns_of(flat_image, tops, "image_columns")
    rows = message_rows(cells, channels)
    message = call(
        "forward_conv",
        8 * MIB,
        functools.partial(forward_conv_kernel, dims, n_top, n_side),
        jax.ShapeDtypeStruct((rows, channels), BF16),
        [IN_VMEM] * (4 + n_top + n_side),
        padded + [pltpu.VMEM((cells, channels), F32), pltpu.VMEM((rows - 2 * cells, channels), F32)],
        **conv_cost,
    )(tie(flat_image, core_in), conv_kernel, norm_gain.reshape(1, channels), flat_up, *tops, *columns)

    messages = to_col([message] * n_col, "features")
    in_refs, in_pieces, out_refs, out_pieces = weights_finish(
        w_in, w_out, mine_out, early_in, core_in, message, messages
    )

    product = 2 * cells * all_channels * hidden
    weight = pltpu.VMEM((all_channels, hidden), BF16)
    weight_t = pltpu.VMEM((hidden, all_channels), BF16)
    part = jax.ShapeDtypeStruct((cells, channels), BF16)
    *grads, act = call(
        "mlp",
        20 * MIB,
        functools.partial(mlp_kernel, in_pieces, out_pieces, n_col),
        [part] * n_col + [jax.ShapeDtypeStruct((cells, hidden), BF16)],
        [IN_VMEM] * n_col + [ANYWHERE] * (len(in_refs) + len(out_refs)),
        [
            weight,
            weight_t,
            pltpu.VMEM((n_col, cells, channels), F32),
            pltpu.VMEM((cells, all_channels), BF16),
            pltpu.VMEM((cells, hidden), BF16),
            pltpu.SemaphoreType.DMA((len(in_refs),)),
            pltpu.SemaphoreType.DMA((len(out_refs),)),
        ],
        flops=3 * product,
        transcendentals=2 * cells * hidden,
    )(*messages, *in_refs, *out_refs)
    grads = to_col(grads, "grad_sums")
    act = tie(act, grads[1:3])
    branches = call(
        "branch",
        8 * MIB,
        functools.partial(branch_kernel, out_pieces, n_col),
        [part] * n_col,
        [IN_VMEM] + [ANYWHERE] * len(out_refs),
        [weight_t, pltpu.SemaphoreType.DMA((len(out_refs),))],
        flops=product,
    )(act, *out_refs)
    branches = to_col(branches, "branch_sums")
    mixed_grad, *sent = call(
        "grad_sum",
        4 * MIB,
        functools.partial(grad_sum_kernel, dims, n_col),
        [jax.ShapeDtypeStruct((cells, channels), F32)] + [top] * n_top,
        [IN_VMEM] * n_col,
        [pltpu.VMEM((channels // 128, cells, 128), F32)],
    )(*grads)
    tops = meet(sent, "section", "grad_rows")
    columns = columns_of(mixed_grad, tops, "grad_columns")
    image_grad = call(
        "backward_conv",
        8 * MIB,
        functools.partial(backward_conv_kernel, dims, n_top, n_side),
        jax.ShapeDtypeStruct((cells, channels), F32),
        [IN_VMEM] * (3 + n_top + n_side),
        padded,
        **conv_cost,
    )(mixed_grad, conv_kernel, flat_up, *tops, *columns)
    branches = tie(branches, image_grad)
    output = (flat_image.astype(F32) + sum(b.astype(F32) for b in branches)).astype(BF16)
    return output.reshape(image.shape), image_grad.reshape(image.shape)


def solution(mesh):
    in_specs = (
        P("section", "row", "col"),
        P(None, None, "col"),
        P("col"),
        P("row", "col"),
        P("row", "col"),
        P("section", "row", "col"),
    )
    out_specs = (P("section", "row", "col"), P("section", "row", "col"))
    return jax.shard_map(local, mesh=mesh, in_specs=in_specs, out_specs=out_specs, check_vma=False)
```

time: 98.8 us -> 82.9 us (0.84)
  starting transfers between devices: 56.4 us -> 36.8 us
  waiting for transfers between devices: 30.7 us -> 35.9 us
  local copies, waits for them, and re-layouts: 1.1 us -> 0.07 us
    ppermute x11 -> x7, starting transfers between devices: 30.1 us -> 18.3 us  [the longest x6 14.7 us: meet(): lax.ppermute(strip, axis, pairs)]
    ppermute x24 -> x19, starting transfers between devices: 26.3 us -> 18.5 us  [swap(): return lax.ppermute(x, axis, [(i, i ^ bit) for i in range(count)])]
    ppermute x24 -> x19, waiting for transfers between devices: 23 us -> 25.7 us  [swap(): return lax.ppermute(x, axis, [(i, i ^ bit) for i in range(count)])]
    ppermute x11 -> x7, waiting for transfers between devices: 7.7 us -> 10.1 us  [the longest x6 10.1 us: meet(): lax.ppermute(strip, axis, pairs)]
    unnamed x12, local copies, waits for them, and re-layouts: 1.05 us -> 0.04 us
  transfers between devices with their start and end apart: 35 -> 26, of which waited for: 12 -> 13; matrix products, arithmetic and copies ran while one was open for 1% -> 0% of each run, Pallas kernels for 4% -> 6%
where the time goes in v2:
time: 82.9 us; the launch traced here: 82.7 us
  starting transfers between devices  36.8 us (44%)
  waiting for transfers between devices  35.9 us (43%)
  Pallas kernels  8.39 us (10%)
  between operations  0.84 us (1%)
    ppermute x19, waiting for transfers between devices, swap(): return lax.ppermute(x, axis, [(i, i ^ bit) for i in range(count)])  25.7 us
    ppermute x19, starting transfers between devices, swap(): return lax.ppermute(x, axis, [(i, i ^ bit) for i in range(count)])  18.5 us
    ppermute x6, starting transfers between devices, meet(): lax.ppermute(strip, axis, pairs)  14.7 us
    ppermute x6, waiting for transfers between devices, meet(): lax.ppermute(strip, axis, pairs)  10.1 us
    pallas_call x1, Pallas kernels, local(): call('mlp', 20 * MIB, functools.partial(mlp_kernel, in_pieces, out_pieces...  3.78 us
    ppermute x1, starting transfers between devices, weights_begin(): lax.ppermute(mine_out, ('row', 'col'), [(r * n_col + z, z * n_col + r) fo...  3.57 us
    pallas_call x1, Pallas kernels, local(): call('backward_conv', 8 * MIB, functools.partial(backward_conv_kernel, di...  1.69 us
  transfers between devices with their start and end apart: 26, of which 13 were waited for; matrix products, arithmetic and copies ran while one was open for 0% of the time, Pallas kernels for 6%

profile of v2, /device:TPU:1, one launch (start us, length us, event | category | flops | bytes accessed | tf_op | source)
XLA Modules:
  0.0 82.7 jit_solution(7062978986435836327)
XLA Ops:
  0.6 0.0 copy-start
  0.6 0.1 collective-permute-start
  0.8 2.7 %collective-permute-start.7 = (bf16[256,1024]{1,0:T(8,128)(2,1)}, bf16[256,1024]{1,0:T(8,128)(2,1)S(1)}, u32[]{:S(2)}, u32[]{:S(2)}) collective-permute-start(bf16[256,1024]{1,0:T(8,128)(2,1)} %refs_4_.1), channel_id=1, source_target_pairs={{0,8},{4,12},{8,0},{12,4},{1,9},{5,13},{9,1},{13,5},{2,10},{6,14},... | collective-permute-start | bytes 1572872 | tf_op jit(solution)/shard_map/w_in_row/ppermute | solution.py:29
  3.5 0.0 copy-start.2
  3.5 3.6 %collective-permute-start.9 = (bf16[512,256]{1,0:T(8,128)(2,1)S(1)}, bf16[512,256]{1,0:T(8,128)(2,1)S(1)}, u32[]{:S(2)}, u32[]{:S(2)}) collective-permute-start(bf16[512,256]{1,0:T(8,128)(2,1)S(1)} %constant_dynamic-slice_fusion), channel_id=1, source_target_pairs={{0,0},{1,4},{2,8},{3,12},{4,1},{5,5},{6,9},{7,13},{8,2},{9,6},{10,... | collective-permute-start | bytes 786440 | tf_op jit(solution)/shard_map/w_out_transposed/ppermute | solution.py:347
  7.1 0.0 copy-start.5
  7.1 0.0 copy-start.3
  7.1 0.0 copy-start.4
  7.2 1.3 %collective-permute-start.1 = (bf16[48,256]{1,0:T(8,128)(2,1)S(1)}, bf16[48,256]{1,0:T(8,128)(2,1)S(1)}, u32[]{:S(2)}, u32[]{:S(2)}) collective-permute-start(bf16[48,256]{1,0:T(8,128)(2,1)S(1)} %constant_dynamic-slice_fusion.1), channel_id=1, source_target_pairs={{0,16},{16,0},{1,17},{17,1},{2,18},{18,2},{3,19},{19,3},{4,20},{20... | collective-permute-start | bytes 73736 | tf_op jit(solution)/shard_map/image_rows/ppermute | solution.py:44
  8.4 1.8 %collective-permute-done.1.refs_0_ = bf16[48,256]{1,0:T(8,128)(2,1)S(1)} collective-permute-done((bf16[48,256]{1,0:T(8,128)(2,1)S(1)}, bf16[48,256]{1,0:T(8,128)(2,1)S(1)}, u32[]{:S(2)}, u32[]{:S(2)}) %collective-permute-start.1) | collective-permute-done | bytes 24608 | tf_op jit(solution)/shard_map/image_rows/ppermute | solution.py:44
  10.2 0.1 image_columns.1
  10.3 0.1 collective-permute-start.2
  10.4 5.6 %collective-permute-start.3 = (bf16[80,256]{1,0:T(8,128)(2,1)S(1)}, bf16[80,256]{1,0:T(8,128)(2,1)S(1)}, u32[]{:S(2)}, u32[]{:S(2)}) collective-permute-start(bf16[80,256]{1,0:T(8,128)(2,1)S(1)} %get-tuple-element.31), channel_id=1, source_target_pairs={{4,8},{8,4},{5,9},{9,5},{6,10},{10,6},{7,11},{11,7},{20,24},{24,20... | collective-permute-start | bytes 122888 | tf_op jit(solution)/shard_map/image_columns/ppermute | solution.py:44
  16.0 0.0 collective-permute-done.refs_6_
  16.0 0.0 collective-permute-done.2.refs_1_
  16.0 4.0 %collective-permute-done.3.refs_2_ = bf16[80,256]{1,0:T(8,128)(2,1)S(1)} collective-permute-done((bf16[80,256]{1,0:T(8,128)(2,1)S(1)}, bf16[80,256]{1,0:T(8,128)(2,1)S(1)}, u32[]{:S(2)}, u32[]{:S(2)}) %collective-permute-start.3) | collective-permute-done | bytes 40992 | tf_op jit(solution)/shard_map/image_columns/ppermute | solution.py:44
  20.0 1.6 %forward_conv.1.refs_0_ = bf16[528,256]{1,0:T(8,128)(2,1)S(1)} custom-call(bf16[256,256]{1,0:T(8,128)(2,1)S(1)} %bitcast.8, f32[7,7,256]{2,1,0:T(8,128)S(1)} %copy-done.3, f32[1,256]{1,0:T(1,128)S(1)} %bitcast.11, bf16[256,256]{1,0:T(8,128)(2,1)S(1)} %bitcast.9, bf16[48,256]{1,0:T(8,128)(2,1)S(1)} %collective-permute-done.1.refs_0_, ...), custom_call_target="tpu_custom_call" | custom-call | flops 192675840 | bytes 1048576 | tf_op jit(solution)/shard_map/forward_conv/pallas_call | solution.py:452
  21.6 4.0 %collective-permute-start.6 = (bf16[528,256]{1,0:T(8,128)(2,1)S(1)}, bf16[528,256]{1,0:T(8,128)(2,1)S(1)}, u32[]{:S(2)}, u32[]{:S(2)}) collective-permute-start(bf16[528,256]{1,0:T(8,128)(2,1)S(1)} %forward_conv.1.refs_0_), channel_id=1, source_target_pairs={{0,3},{1,2},{2,1},{3,0},{4,7},{5,6},{6,5},{7,4},{8,11},{9,10},{10,... | collective-permute-start | bytes 811016 | tf_op jit(solution)/shard_map/features/col_3/ppermute | solution.py:29
  25.6 0.0 collective-permute-start.5
  25.6 0.4 collective-permute-start.4
  26.0 0.0 collective-permute-done.9.refs_8_.refs_0_
  26.0 0.0 collective-permute-done.7.refs_5_
  26.0 0.0 collective-permute-start.10
  26.0 1.3 %collective-permute-start.11 = (bf16[512,256]{1,0:T(8,128)(2,1)S(1)}, bf16[512,256]{1,0:T(8,128)(2,1)S(1)}, u32[]{:S(2)}, u32[]{:S(2)}) collective-permute-start(bf16[512,256]{1,0:T(8,128)(2,1)S(1)} %collective-permute-done.9.refs_8_.refs_0_), channel_id=1, source_target_pairs={{0,16},{16,0},{1,17},{17,1},{2,18},{18,2},{3,19},{19,3},{4,20},{20... | collective-permute-start | bytes 786440 | tf_op jit(solution)/shard_map/w_out_section_0/ppermute | solution.py:29
  27.3 5.3 %collective-permute-done.10.refs_9_.refs_1_ = bf16[512,256]{1,0:T(8,128)(2,1)S(1)} collective-permute-done((bf16[512,256]{1,0:T(8,128)(2,1)S(1)}, bf16[512,256]{1,0:T(8,128)(2,1)S(1)}, u32[]{:S(2)}, u32[]{:S(2)}) %collective-permute-start.10) | collective-permute-done | bytes 262176 | tf_op jit(solution)/shard_map/w_out_row/ppermute | solution.py:29
  32.6 1.2 %collective-permute-start.12 = (bf16[512,256]{1,0:T(8,128)(2,1)S(1)}, bf16[512,256]{1,0:T(8,128)(2,1)S(1)}, u32[]{:S(2)}, u32[]{:S(2)}) collective-permute-start(bf16[512,256]{1,0:T(8,128)(2,1)S(1)} %collective-permute-done.10.refs_9_.refs_1_), channel_id=1, source_target_pairs={{0,16},{16,0},{1,17},{17,1},{2,18},{18,2},{3,19},{19,3},{4,20},{20... | collective-permute-start | bytes 786440 | tf_op jit(solution)/shard_map/w_out_section_2/ppermute | solution.py:29
  33.8 0.0 collective-permute-done.11.refs_10_.refs_2_
  33.8 0.0 collective-permute-done.6.refs_3_
  33.8 10.1 %collective-permute-done.5.refs_2_ = bf16[528,256]{1,0:T(8,128)(2,1)S(1)} collective-permute-done((bf16[528,256]{1,0:T(8,128)(2,1)S(1)}, bf16[528,256]{1,0:T(8,128)(2,1)S(1)}, u32[]{:S(2)}, u32[]{:S(2)}) %collective-permute-start.5) | collective-permute-done | bytes 270368 | tf_op jit(solution)/shard_map/features/col_2/ppermute | solution.py:29
  43.9 0.0 collective-permute-done.4.refs_1_
  43.9 0.8 collective-permute-start.13
  44.6 0.0 collective-permute-start.14
  44.6 0.5 collective-permute-start.15
  45.1 0.0 collective-permute-start.8
  45.1 0.0 collective-permute-done.12.refs_11_.refs_3_
  45.1 0.6 collective-permute-done.13.refs_12_.refs_4_
  45.8 0.4 collective-permute-done.14.refs_13_.refs_5_
  46.2 0.4 collective-permute-done.15.refs_14_.refs_6_
  46.5 0.4 collective-permute-start.16
  46.9 0.4 collective-permute-done.8.refs_7_
  47.3 0.8 collective-permute-done.16.refs_15_.refs_7_
  48.1 3.8 %mlp.1 = (bf16[256,256]{1,0:T(8,128)(2,1)S(1)}, bf16[256,256]{1,0:T(8,128)(2,1)S(1)}, bf16[256,256]{1,0:T(8,128)(2,1)S(1)}, bf16[256,256]{1,0:T(8,128)(2,1)S(1)}, bf16[256,1024]{1,0:T(8,128)(2,1)S(1)}) custom-call(bf16[528,256]{1,0:T(8,128)(2,1)S(1)} %forward_conv.1.refs_0_, bf16[528,256]{1,0:T(8,128)(2,1)S(1)} %collective-permute-done.4.refs_1_, ...), custom_call_target="tpu_custom_call" | custom-call | flops 1610612736 | bytes 1048576 | tf_op jit(solution)/shard_map/mlp/pallas_call | solution.py:471
  51.9 0.1 collective-permute-start.17
  51.9 0.4 collective-permute-start.18
  52.3 3.1 %collective-permute-start.22 = (bf16[256,256]{1,0:T(8,128)(2,1)S(1)}, bf16[256,256]{1,0:T(8,128)(2,1)S(1)}, u32[]{:S(2)}, u32[]{:S(2)}) collective-permute-start(bf16[256,256]{1,0:T(8,128)(2,1)S(1)} %get-tuple-element.47), channel_id=1, source_target_pairs={{0,3},{1,2},{2,1},{3,0},{4,7},{5,6},{6,5},{7,4},{8,11},{9,10},{10,... | collective-permute-start | bytes 393224 | tf_op jit(solution)/shard_map/grad_sums/col_3/ppermute | solution.py:29
  55.5 2.3 %collective-permute-done.17.refs_1_ = bf16[256,256]{1,0:T(8,128)(2,1)S(1)} collective-permute-done((bf16[256,256]{1,0:T(8,128)(2,1)S(1)}, bf16[256,256]{1,0:T(8,128)(2,1)S(1)}, u32[]{:S(2)}, u32[]{:S(2)}) %collective-permute-start.17) | collective-permute-done | bytes 131104 | tf_op jit(solution)/shard_map/grad_sums/col_1/ppermute | solution.py:29
  57.8 5.5 %collective-permute-done.18.refs_2_ = bf16[256,256]{1,0:T(8,128)(2,1)S(1)} collective-permute-done((bf16[256,256]{1,0:T(8,128)(2,1)S(1)}, bf16[256,256]{1,0:T(8,128)(2,1)S(1)}, u32[]{:S(2)}, u32[]{:S(2)}) %collective-permute-start.18) | collective-permute-done | bytes 131104 | tf_op jit(solution)/shard_map/grad_sums/col_2/ppermute | solution.py:29
  63.3 1.1 %branch.1 = (bf16[256,256]{1,0:T(8,128)(2,1)S(1)}, bf16[256,256]{1,0:T(8,128)(2,1)S(1)}, bf16[256,256]{1,0:T(8,128)(2,1)S(1)}, bf16[256,256]{1,0:T(8,128)(2,1)S(1)}) custom-call(bf16[256,1024]{1,0:T(8,128)(2,1)S(1)} %get-tuple-element.41.hidden, bf16[512,256]{1,0:T(8,128)(2,1)S(1)} %collective-permute-done.9.refs_8_.refs_0_, ...), custom_call_target="tpu_custom_call" | custom-call | flops 536870912 | bytes 1048576 | tf_op jit(solution)/shard_map/branch/pallas_call | solution.py:491
  64.3 0.1 collective-permute-start.19
  64.4 0.1 collective-permute-start.20
  64.5 3.5 %collective-permute-start.21 = (bf16[256,256]{1,0:T(8,128)(2,1)S(1)}, bf16[256,256]{1,0:T(8,128)(2,1)S(1)}, u32[]{:S(2)}, u32[]{:S(2)}) collective-permute-start(bf16[256,256]{1,0:T(8,128)(2,1)S(1)} %get-tuple-element.45), channel_id=1, source_target_pairs={{0,3},{1,2},{2,1},{3,0},{4,7},{5,6},{6,5},{7,4},{8,11},{9,10},{10,... | collective-permute-start | bytes 393224 | tf_op jit(solution)/shard_map/branch_sums/col_3/ppermute | solution.py:29
  68.0 0.0 collective-permute-done.22.refs_3_
  68.0 0.1 grad_sum.1
  68.0 1.3 %collective-permute-start.23 = (bf16[48,256]{1,0:T(8,128)(2,1)S(1)}, bf16[48,256]{1,0:T(8,128)(2,1)S(1)}, u32[]{:S(2)}, u32[]{:S(2)}) collective-permute-start(bf16[48,256]{1,0:T(8,128)(2,1)S(1)} %get-tuple-element.49), channel_id=1, source_target_pairs={{0,16},{16,0},{1,17},{17,1},{2,18},{18,2},{3,19},{19,3},{4,20},{20... | collective-permute-start | bytes 73736 | tf_op jit(solution)/shard_map/grad_rows/ppermute | solution.py:44
  69.3 1.7 %collective-permute-done.23.refs_0_ = bf16[48,256]{1,0:T(8,128)(2,1)S(1)} collective-permute-done((bf16[48,256]{1,0:T(8,128)(2,1)S(1)}, bf16[48,256]{1,0:T(8,128)(2,1)S(1)}, u32[]{:S(2)}, u32[]{:S(2)}) %collective-permute-start.23) | collective-permute-done | bytes 24608 | tf_op jit(solution)/shard_map/grad_rows/ppermute | solution.py:44
  71.1 0.1 grad_columns.1
  71.1 3.8 %collective-permute-start.24 = (bf16[80,256]{1,0:T(8,128)(2,1)S(1)}, bf16[80,256]{1,0:T(8,128)(2,1)S(1)}, u32[]{:S(2)}, u32[]{:S(2)}) collective-permute-start(bf16[80,256]{1,0:T(8,128)(2,1)S(1)} %get-tuple-element.50), channel_id=1, source_target_pairs={{0,4},{8,12},{4,0},{12,8},{1,5},{9,13},{5,1},{13,9},{2,6},{10,14},... | collective-permute-start | bytes 122888 | tf_op jit(solution)/shard_map/grad_columns/ppermute | solution.py:44
  75.0 2.7 %collective-permute-start.25 = (bf16[80,256]{1,0:T(8,128)(2,1)S(1)}, bf16[80,256]{1,0:T(8,128)(2,1)S(1)}, u32[]{:S(2)}, u32[]{:S(2)}) collective-permute-start(bf16[80,256]{1,0:T(8,128)(2,1)S(1)} %get-tuple-element.51), channel_id=1, source_target_pairs={{4,8},{8,4},{5,9},{9,5},{6,10},{10,6},{7,11},{11,7},{20,24},{24,20... | collective-permute-start | bytes 122888 | tf_op jit(solution)/shard_map/grad_columns/ppermute | solution.py:44
  77.6 0.0 collective-permute-done.24.refs_1_
  77.6 2.6 %collective-permute-done.25.refs_2_ = bf16[80,256]{1,0:T(8,128)(2,1)S(1)} collective-permute-done((bf16[80,256]{1,0:T(8,128)(2,1)S(1)}, bf16[80,256]{1,0:T(8,128)(2,1)S(1)}, u32[]{:S(2)}, u32[]{:S(2)}) %collective-permute-start.25) | collective-permute-done | bytes 40992 | tf_op jit(solution)/shard_map/grad_columns/ppermute | solution.py:44
  80.3 1.7 %backward_conv.1 = f32[256,256]{1,0:T(8,128)} custom-call(f32[256,256]{1,0:T(8,128)S(1)} %get-tuple-element.48.cells.grad, f32[7,7,256]{2,1,0:T(8,128)S(1)} %copy-done.3, bf16[256,256]{1,0:T(8,128)(2,1)S(1)} %bitcast.10, bf16[48,256]{1,0:T(8,128)(2,1)S(1)} %collective-permute-done.23.refs_0_, bf16[80,256]{1,0:T(8,128)(2,1)S(1)} %collective-permute-done.24.refs_1_, ...), custom_call_target="tpu_custom_call" | custom-call | flops 192675840 | bytes 1048576 | tf_op jit(solution)/shard_map/backward_conv/pallas_call | solution.py:511
  82.0 0.0 collective-permute-done.19
  82.0 0.0 collective-permute-done.20
  82.0 0.7 add_convert_fusion
  (10 shorter events, 0.0 us)
Async XLA Ops:
  0.6 2.8 %copy-start = (bf16[1024,256]{1,0:T(8,128)(2,1)S(1)}, bf16[1024,256]{1,0:T(8,128)(2,1)}, u32[]{:S(2)}) copy-start(bf16[1024,256]{1,0:T(8,128)(2,1)} %param.10) | copy-start | bytes 1572868
  0.6 15.3 %collective-permute-start = (bf16[256,1024]{1,0:T(8,128)(2,1)}, bf16[256,1024]{1,0:T(8,128)(2,1)S(1)}, u32[]{:S(2)}, u32[]{:S(2)}) collective-permute-start(bf16[256,1024]{1,0:T(8,128)(2,1)} %refs_4_.1), channel_id=1, source_target_pairs={{0,4},{4,0},{8,12},{12,8},{1,5},{5,1},{9,13},{13,9},{2,6},{6,2},{1... | collective-permute-start | bytes 1572872 | tf_op jit(solution)/shard_map/w_in_core/ppermute | solution.py:29
  0.8 25.2 %collective-permute-start.7 = (bf16[256,1024]{1,0:T(8,128)(2,1)}, bf16[256,1024]{1,0:T(8,128)(2,1)S(1)}, u32[]{:S(2)}, u32[]{:S(2)}) collective-permute-start(bf16[256,1024]{1,0:T(8,128)(2,1)} %refs_4_.1), channel_id=1, source_target_pairs={{0,8},{4,12},{8,0},{12,4},{1,9},{5,13},{9,1},{13,5},{2,10},{6,14},... | collective-permute-start | bytes 1572872 | tf_op jit(solution)/shard_map/w_in_row/ppermute | solution.py:29
  3.5 3.6 %copy-start.1 = (bf16[16,16,256]{2,1,0:T(8,128)(2,1)S(1)}, bf16[16,16,256]{2,1,0:T(8,128)(2,1)}, u32[]{:S(2)}) copy-start(bf16[16,16,256]{2,1,0:T(8,128)(2,1)} %param.6) | copy-start | bytes 393220
  3.5 16.5 %copy-start.2 = (bf16[16,16,256]{2,1,0:T(8,128)(2,1)S(1)}, bf16[16,16,256]{2,1,0:T(8,128)(2,1)}, u32[]{:S(2)}) copy-start(bf16[16,16,256]{2,1,0:T(8,128)(2,1)} %param.11) | copy-start | bytes 393220
  3.5 22.5 %collective-permute-start.9 = (bf16[512,256]{1,0:T(8,128)(2,1)S(1)}, bf16[512,256]{1,0:T(8,128)(2,1)S(1)}, u32[]{:S(2)}, u32[]{:S(2)}) collective-permute-start(bf16[512,256]{1,0:T(8,128)(2,1)S(1)} %constant_dynamic-slice_fusion), channel_id=1, source_target_pairs={{0,0},{1,4},{2,8},{3,12},{4,1},{5,5},{6,9},{7,13},{8,2},{9,6},{10,... | collective-permute-start | bytes 786440 | tf_op jit(solution)/shard_map/w_out_transposed/ppermute | solution.py:347
  7.1 12.9 %copy-start.5 = (f32[256]{0:T(256)S(1)}, f32[256]{0:T(256)}, u32[]{:S(2)}) copy-start(f32[256]{0:T(256)} %param.8) | copy-start | bytes 3076
  7.1 12.9 %copy-start.3 = (f32[7,7,256]{2,1,0:T(8,128)S(1)}, f32[7,7,256]{2,1,0:T(8,128)}, u32[]{:S(2)}) copy-start(f32[7,7,256]{2,1,0:T(8,128)} %taps.3) | copy-start | bytes 150532
  7.1 40.9 %copy-start.4 = (bf16[256,1024]{1,0:T(8,128)(2,1)S(1)}, bf16[256,1024]{1,0:T(8,128)(2,1)}, u32[]{:S(2)}) copy-start(bf16[256,1024]{1,0:T(8,128)(2,1)} %refs_4_.1) | copy-start | bytes 1572868
  7.2 3.0 %collective-permute-start.1 = (bf16[48,256]{1,0:T(8,128)(2,1)S(1)}, bf16[48,256]{1,0:T(8,128)(2,1)S(1)}, u32[]{:S(2)}, u32[]{:S(2)}) collective-permute-start(bf16[48,256]{1,0:T(8,128)(2,1)S(1)} %constant_dynamic-slice_fusion.1), channel_id=1, source_target_pairs={{0,16},{16,0},{1,17},{17,1},{2,18},{18,2},{3,19},{19,3},{4,20},{20... | collective-permute-start | bytes 73736 | tf_op jit(solution)/shard_map/image_rows/ppermute | solution.py:44
  10.3 5.7 %collective-permute-start.2 = (bf16[80,256]{1,0:T(8,128)(2,1)S(1)}, bf16[80,256]{1,0:T(8,128)(2,1)S(1)}, u32[]{:S(2)}, u32[]{:S(2)}) collective-permute-start(bf16[80,256]{1,0:T(8,128)(2,1)S(1)} %get-tuple-element.30), channel_id=1, source_target_pairs={{0,4},{8,12},{4,0},{12,8},{1,5},{9,13},{5,1},{13,9},{2,6},{10,14},... | collective-permute-start | bytes 122888 | tf_op jit(solution)/shard_map/image_columns/ppermute | solution.py:44
  10.4 9.6 %collective-permute-start.3 = (bf16[80,256]{1,0:T(8,128)(2,1)S(1)}, bf16[80,256]{1,0:T(8,128)(2,1)S(1)}, u32[]{:S(2)}, u32[]{:S(2)}) collective-permute-start(bf16[80,256]{1,0:T(8,128)(2,1)S(1)} %get-tuple-element.31), channel_id=1, source_target_pairs={{4,8},{8,4},{5,9},{9,5},{6,10},{10,6},{7,11},{11,7},{20,24},{24,20... | collective-permute-start | bytes 122888 | tf_op jit(solution)/shard_map/image_columns/ppermute | solution.py:44
  21.6 12.2 %collective-permute-start.6 = (bf16[528,256]{1,0:T(8,128)(2,1)S(1)}, bf16[528,256]{1,0:T(8,128)(2,1)S(1)}, u32[]{:S(2)}, u32[]{:S(2)}) collective-permute-start(bf16[528,256]{1,0:T(8,128)(2,1)S(1)} %forward_conv.1.refs_0_), channel_id=1, source_target_pairs={{0,3},{1,2},{2,1},{3,0},{4,7},{5,6},{6,5},{7,4},{8,11},{9,10},{10,... | collective-permute-start | bytes 811016 | tf_op jit(solution)/shard_map/features/col_3/ppermute | solution.py:29
  25.6 18.2 %collective-permute-start.5 = (bf16[528,256]{1,0:T(8,128)(2,1)S(1)}, bf16[528,256]{1,0:T(8,128)(2,1)S(1)}, u32[]{:S(2)}, u32[]{:S(2)}) collective-permute-start(bf16[528,256]{1,0:T(8,128)(2,1)S(1)} %forward_conv.1.refs_0_), channel_id=1, source_target_pairs={{0,2},{1,3},{2,0},{3,1},{4,6},{5,7},{6,4},{7,5},{8,10},{9,11},{10,... | collective-permute-start | bytes 811016 | tf_op jit(solution)/shard_map/features/col_2/ppermute | solution.py:29
  25.6 18.2 %collective-permute-start.4 = (bf16[528,256]{1,0:T(8,128)(2,1)S(1)}, bf16[528,256]{1,0:T(8,128)(2,1)S(1)}, u32[]{:S(2)}, u32[]{:S(2)}) collective-permute-start(bf16[528,256]{1,0:T(8,128)(2,1)S(1)} %forward_conv.1.refs_0_), channel_id=1, source_target_pairs={{0,1},{1,0},{2,3},{3,2},{4,5},{5,4},{6,7},{7,6},{8,9},{9,8},{10,11... | collective-permute-start | bytes 811016 | tf_op jit(solution)/shard_map/features/col_1/ppermute | solution.py:29
  26.0 6.6 %collective-permute-start.10 = (bf16[512,256]{1,0:T(8,128)(2,1)S(1)}, bf16[512,256]{1,0:T(8,128)(2,1)S(1)}, u32[]{:S(2)}, u32[]{:S(2)}) collective-permute-start(bf16[512,256]{1,0:T(8,128)(2,1)S(1)} %collective-permute-done.9.refs_8_.refs_0_), channel_id=1, source_target_pairs={{0,8},{4,12},{8,0},{12,4},{1,9},{5,13},{9,1},{13,5},{2,10},{6,14},... | collective-permute-start | bytes 786440 | tf_op jit(solution)/shard_map/w_out_row/ppermute | solution.py:29
  26.0 7.8 %collective-permute-start.11 = (bf16[512,256]{1,0:T(8,128)(2,1)S(1)}, bf16[512,256]{1,0:T(8,128)(2,1)S(1)}, u32[]{:S(2)}, u32[]{:S(2)}) collective-permute-start(bf16[512,256]{1,0:T(8,128)(2,1)S(1)} %collective-permute-done.9.refs_8_.refs_0_), channel_id=1, source_target_pairs={{0,16},{16,0},{1,17},{17,1},{2,18},{18,2},{3,19},{19,3},{4,20},{20... | collective-permute-start | bytes 786440 | tf_op jit(solution)/shard_map/w_out_section_0/ppermute | solution.py:29
  32.6 12.6 %collective-permute-start.12 = (bf16[512,256]{1,0:T(8,128)(2,1)S(1)}, bf16[512,256]{1,0:T(8,128)(2,1)S(1)}, u32[]{:S(2)}, u32[]{:S(2)}) collective-permute-start(bf16[512,256]{1,0:T(8,128)(2,1)S(1)} %collective-permute-done.10.refs_9_.refs_1_), channel_id=1, source_target_pairs={{0,16},{16,0},{1,17},{17,1},{2,18},{18,2},{3,19},{19,3},{4,20},{20... | collective-permute-start | bytes 786440 | tf_op jit(solution)/shard_map/w_out_section_2/ppermute | solution.py:29
  43.9 1.9 %collective-permute-start.13 = (bf16[512,256]{1,0:T(8,128)(2,1)S(1)}, bf16[512,256]{1,0:T(8,128)(2,1)S(1)}, u32[]{:S(2)}, u32[]{:S(2)}) collective-permute-start(bf16[512,256]{1,0:T(8,128)(2,1)S(1)} %collective-permute-done.9.refs_8_.refs_0_), channel_id=1, source_target_pairs={{0,4},{4,0},{8,12},{12,8},{1,5},{5,1},{9,13},{13,9},{2,6},{6,2},{1... | collective-permute-start | bytes 786440 | tf_op jit(solution)/shard_map/w_out_core_0_0/ppermute | solution.py:29
  44.6 1.5 %collective-permute-start.14 = (bf16[512,256]{1,0:T(8,128)(2,1)S(1)}, bf16[512,256]{1,0:T(8,128)(2,1)S(1)}, u32[]{:S(2)}, u32[]{:S(2)}) collective-permute-start(bf16[512,256]{1,0:T(8,128)(2,1)S(1)} %collective-permute-done.10.refs_9_.refs_1_), channel_id=1, source_target_pairs={{0,4},{4,0},{8,12},{12,8},{1,5},{5,1},{9,13},{13,9},{2,6},{6,2},{1... | collective-permute-start | bytes 786440 | tf_op jit(solution)/shard_map/w_out_core_2_0/ppermute | solution.py:29
  44.6 1.9 %collective-permute-start.15 = (bf16[512,256]{1,0:T(8,128)(2,1)S(1)}, bf16[512,256]{1,0:T(8,128)(2,1)S(1)}, u32[]{:S(2)}, u32[]{:S(2)}) collective-permute-start(bf16[512,256]{1,0:T(8,128)(2,1)S(1)} %collective-permute-done.11.refs_10_.refs_2_), channel_id=1, source_target_pairs={{0,4},{4,0},{8,12},{12,8},{1,5},{5,1},{9,13},{13,9},{2,6},{6,2},{1... | collective-permute-start | bytes 786440 | tf_op jit(solution)/shard_map/w_out_core_0_1/ppermute | solution.py:29
  45.1 2.2 %collective-permute-start.8 = (bf16[256,1024]{1,0:T(8,128)(2,1)S(1)}, bf16[256,1024]{1,0:T(8,128)(2,1)S(1)}, u32[]{:S(2)}, u32[]{:S(2)}) collective-permute-start(bf16[256,1024]{1,0:T(8,128)(2,1)S(1)} %collective-permute-done.7.refs_5_), channel_id=1, source_target_pairs={{0,4},{4,0},{8,12},{12,8},{1,5},{5,1},{9,13},{13,9},{2,6},{6,2},{1... | collective-permute-start | bytes 1572872 | tf_op jit(solution)/shard_map/w_in_core_2/ppermute | solution.py:29
  46.5 1.5 %collective-permute-start.16 = (bf16[512,256]{1,0:T(8,128)(2,1)S(1)}, bf16[512,256]{1,0:T(8,128)(2,1)S(1)}, u32[]{:S(2)}, u32[]{:S(2)}) collective-permute-start(bf16[512,256]{1,0:T(8,128)(2,1)S(1)} %collective-permute-done.12.refs_11_.refs_3_), channel_id=1, source_target_pairs={{0,4},{4,0},{8,12},{12,8},{1,5},{5,1},{9,13},{13,9},{2,6},{6,2},{1... | collective-permute-start | bytes 786440 | tf_op jit(solution)/shard_map/w_out_core_2_1/ppermute | solution.py:29
  51.9 5.9 %collective-permute-start.17 = (bf16[256,256]{1,0:T(8,128)(2,1)S(1)}, bf16[256,256]{1,0:T(8,128)(2,1)S(1)}, u32[]{:S(2)}, u32[]{:S(2)}) collective-permute-start(bf16[256,256]{1,0:T(8,128)(2,1)S(1)} %get-tuple-element.39), channel_id=1, source_target_pairs={{0,1},{1,0},{2,3},{3,2},{4,5},{5,4},{6,7},{7,6},{8,9},{9,8},{10,11... | collective-permute-start | bytes 393224 | tf_op jit(solution)/shard_map/grad_sums/col_1/ppermute | solution.py:29
  51.9 11.3 %collective-permute-start.18 = (bf16[256,256]{1,0:T(8,128)(2,1)S(1)}, bf16[256,256]{1,0:T(8,128)(2,1)S(1)}, u32[]{:S(2)}, u32[]{:S(2)}) collective-permute-start(bf16[256,256]{1,0:T(8,128)(2,1)S(1)} %get-tuple-element.40), channel_id=1, source_target_pairs={{0,2},{1,3},{2,0},{3,1},{4,6},{5,7},{6,4},{7,5},{8,10},{9,11},{10,... | collective-permute-start | bytes 393224 | tf_op jit(solution)/shard_map/grad_sums/col_2/ppermute | solution.py:29
  52.3 15.6 %collective-permute-start.22 = (bf16[256,256]{1,0:T(8,128)(2,1)S(1)}, bf16[256,256]{1,0:T(8,128)(2,1)S(1)}, u32[]{:S(2)}, u32[]{:S(2)}) collective-permute-start(bf16[256,256]{1,0:T(8,128)(2,1)S(1)} %get-tuple-element.47), channel_id=1, source_target_pairs={{0,3},{1,2},{2,1},{3,0},{4,7},{5,6},{6,5},{7,4},{8,11},{9,10},{10,... | collective-permute-start | bytes 393224 | tf_op jit(solution)/shard_map/grad_sums/col_3/ppermute | solution.py:29
  64.3 17.6 %collective-permute-start.19 = (bf16[256,256]{1,0:T(8,128)(2,1)S(1)}, bf16[256,256]{1,0:T(8,128)(2,1)S(1)}, u32[]{:S(2)}, u32[]{:S(2)}) collective-permute-start(bf16[256,256]{1,0:T(8,128)(2,1)S(1)} %get-tuple-element.43), channel_id=1, source_target_pairs={{0,1},{1,0},{2,3},{3,2},{4,5},{5,4},{6,7},{7,6},{8,9},{9,8},{10,11... | collective-permute-start | bytes 393224 | tf_op jit(solution)/shard_map/branch_sums/col_1/ppermute | solution.py:29
  64.4 17.5 %collective-permute-start.20 = (bf16[256,256]{1,0:T(8,128)(2,1)S(1)}, bf16[256,256]{1,0:T(8,128)(2,1)S(1)}, u32[]{:S(2)}, u32[]{:S(2)}) collective-permute-start(bf16[256,256]{1,0:T(8,128)(2,1)S(1)} %get-tuple-element.44), channel_id=1, source_target_pairs={{0,2},{1,3},{2,0},{3,1},{4,6},{5,7},{6,4},{7,5},{8,10},{9,11},{10,... | collective-permute-start | bytes 393224 | tf_op jit(solution)/shard_map/branch_sums/col_2/ppermute | solution.py:29
  64.5 17.5 %collective-permute-start.21 = (bf16[256,256]{1,0:T(8,128)(2,1)S(1)}, bf16[256,256]{1,0:T(8,128)(2,1)S(1)}, u32[]{:S(2)}, u32[]{:S(2)}) collective-permute-start(bf16[256,256]{1,0:T(8,128)(2,1)S(1)} %get-tuple-element.45), channel_id=1, source_target_pairs={{0,3},{1,2},{2,1},{3,0},{4,7},{5,6},{6,5},{7,4},{8,11},{9,10},{10,... | collective-permute-start | bytes 393224 | tf_op jit(solution)/shard_map/branch_sums/col_3/ppermute | solution.py:29
  68.0 3.0 %collective-permute-start.23 = (bf16[48,256]{1,0:T(8,128)(2,1)S(1)}, bf16[48,256]{1,0:T(8,128)(2,1)S(1)}, u32[]{:S(2)}, u32[]{:S(2)}) collective-permute-start(bf16[48,256]{1,0:T(8,128)(2,1)S(1)} %get-tuple-element.49), channel_id=1, source_target_pairs={{0,16},{16,0},{1,17},{17,1},{2,18},{18,2},{3,19},{19,3},{4,20},{20... | collective-permute-start | bytes 73736 | tf_op jit(solution)/shard_map/grad_rows/ppermute | solution.py:44
  71.1 6.5 %collective-permute-start.24 = (bf16[80,256]{1,0:T(8,128)(2,1)S(1)}, bf16[80,256]{1,0:T(8,128)(2,1)S(1)}, u32[]{:S(2)}, u32[]{:S(2)}) collective-permute-start(bf16[80,256]{1,0:T(8,128)(2,1)S(1)} %get-tuple-element.50), channel_id=1, source_target_pairs={{0,4},{8,12},{4,0},{12,8},{1,5},{9,13},{5,1},{13,9},{2,6},{10,14},... | collective-permute-start | bytes 122888 | tf_op jit(solution)/shard_map/grad_columns/ppermute | solution.py:44
  75.0 5.3 %collective-permute-start.25 = (bf16[80,256]{1,0:T(8,128)(2,1)S(1)}, bf16[80,256]{1,0:T(8,128)(2,1)S(1)}, u32[]{:S(2)}, u32[]{:S(2)}) collective-permute-start(bf16[80,256]{1,0:T(8,128)(2,1)S(1)} %get-tuple-element.51), channel_id=1, source_target_pairs={{4,8},{8,4},{5,9},{9,5},{6,10},{10,6},{7,11},{11,7},{20,24},{24,20... | collective-permute-start | bytes 122888 | tf_op jit(solution)/shard_map/grad_columns/ppermute | solution.py:44

commit v3 on v2

--- a/solution.py
+++ b/solution.py
@@ -355,7 +355,20 @@
     return mine_out, early, [swap(w_in, "row", bit, "w_in_core") for bit in bits_of(n_row)[:1]]
 
 
-def weights_finish(w_in, w_out, mine_out, got_in, core_in, message, messages):
+def weights_far(mine_out, others):
+    if not exchangeable():
+        return None, []
+    got = {(0, 0): tie(mine_out, others)}
+    for bit in bits_of(lax.axis_size("row"))[1:]:
+        got |= {(r ^ bit, s): swap(x, "row", bit, "w_out_row") for (r, s), x in got.items()}
+    for bit in bits_of(lax.axis_size("section")):
+        got |= {
+            (0, s ^ bit): swap(x, "section", bit, "w_out_section") for (r, s), x in got.items() if r == 0
+        }
+    return got, list(got.values())
+
+
+def weights_finish(w_in, w_out, got_out, got_in, core_in, messages):
     n_sec, n_row, n_col = (lax.axis_size(a) for a in ("section", "row", "col"))
     channels, hidden = w_in.shape[0] * n_row // n_col, w_in.shape[1]
     if not exchangeable():
@@ -375,28 +388,21 @@
         part = (lambda: 0) if sec_bits is None else (lambda: (lax.axis_index("section") ^ sec_bits) * share)
         return block, part
 
-    far, core = [b for b in bits_of(n_row) if b > 1], bits_of(n_row)[:1]
-    got_out = {(0, 0): tie(mine_out, message, list(got_in.values()))}
-    for bit in far:
-        got_out |= {(r ^ bit, s): swap(x, "row", bit, "w_out_row") for (r, s), x in got_out.items()}
+    core = bits_of(n_row)[:1]
     for bit in bits_of(n_sec):
         got_out |= {
-            (r, s ^ bit): swap(x, "section", bit, f"w_out_section_{r}") for (r, s), x in got_out.items()
+            (r, s ^ bit): swap(x, "section", bit, "w_out_both") for (r, s), x in got_out.items() if r and s < bit
         }
     for bit in core:
         got_in |= {
-            (r ^ bit, s): core_in[0] if r == 0 else swap(tie(x, messages), "row", bit, f"w_in_core_{r}")
+            (r ^ bit, s): core_in[0] if r == 0 else swap(x, "row", bit, f"w_in_core_{r}")
             for (r, s), x in got_in.items()
         }
-        first = {
-            (r ^ bit, s): swap(tie(x, messages), "row", bit, f"w_out_core_{r}_{s}")
+        gate = swap(tie(got_out[0, 0], messages), "row", bit, "w_out_core_0_0")
+        got_out |= {(bit, 0): gate} | {
+            (r ^ bit, s): swap(tie(x, gate) if r and s else x, "row", bit, f"w_out_core_{r}_{s}")
             for (r, s), x in got_out.items()
-            if not (r and s)
-        }
-        got_out |= first | {
-            (r ^ bit, s): swap(tie(x, list(first.values())), "row", bit, f"w_out_core_{r}_{s}")
-            for (r, s), x in got_out.items()
-            if r and s
+            if r or s
         }
     return (
         list(got_in.values()),
@@ -435,6 +441,25 @@
     def to_col(parts, name):
         with jax.named_scope(name):
             return [p if k == 0 else swap(p, "col", k) for k, p in enumerate(parts)]
+
+    def gather_col(part, name, others):
+        got = {0: part}
+        with jax.named_scope(name):
+            for bit in reversed(bits_of(n_col)):
+                got |= {k ^ bit: swap(tie(x, others) if k else x, "col", bit) for k, x in got.items()}
+        return [got[k] for k in range(n_col)]
+
+    def scatter_col(parts, name, others):
+        terms = [[p] for p in parts]
+        with jax.named_scope(name):
+            for bit in bits_of(n_col):
+                for k in range(bit, n_col, 2 * bit):
+                    far, *more = terms[k]
+                    if more:
+                        more = tie(more, others)
+                        far = sum((m.astype(F32) for m in more), far.astype(F32)).astype(BF16)
+                    terms[k ^ bit].append(swap(far, "col", bit))
+        return terms[0]
 
     flat_image = image.reshape(cells, channels)
     flat_up = upstream.reshape(cells, channels)
@@ -459,9 +484,11 @@
         **conv_cost,
     )(tie(flat_image, core_in), conv_kernel, norm_gain.reshape(1, channels), flat_up, *tops, *columns)
 
-    messages = to_col([message] * n_col, "features")
+    early = [] if early_in is None else list(early_in.values())
+    got_out, rows_done = weights_far(mine_out, [message, early])
+    messages = gather_col(message, "features", rows_done)
     in_refs, in_pieces, out_refs, out_pieces = weights_finish(
-        w_in, w_out, mine_out, early_in, core_in, message, messages
+        w_in, w_out, got_out, early_in, core_in, messages
     )
 
     product = 2 * cells * all_channels * hidden
@@ -487,7 +514,7 @@
         transcendentals=2 * cells * hidden,
     )(*messages, *in_refs, *out_refs)
     grads = to_col(grads, "grad_sums")
-    act = tie(act, grads[1:3])
+    act = tie(act, grads[1])
     branches = call(
         "branch",
         8 * MIB,
@@ -497,7 +524,6 @@
         [weight_t, pltpu.SemaphoreType.DMA((len(out_refs),))],
         flops=product,
     )(act, *out_refs)
-    branches = to_col(branches, "branch_sums")
     mixed_grad, *sent = call(
         "grad_sum",
         4 * MIB,
@@ -507,6 +533,7 @@
         [pltpu.VMEM((channels // 128, cells, 128), F32)],
     )(*grads)
     tops = meet(sent, "section", "grad_rows")
+    branches = scatter_col(branches, "branch_sums", tops)
     columns = columns_of(mixed_grad, tops, "grad_columns")
     image_grad = call(
         "backward_conv",

time: 82.9 us -> 79.3 us (0.957)
  waiting for transfers between devices: 35.9 us -> 29.6 us
  starting transfers between devices: 36.8 us -> 39.5 us
    ppermute x19, starting transfers between devices: 18.5 us -> 22.2 us  [swap(): return lax.ppermute(x, axis, [(i, i ^ bit) for i in range(count)])]
    ppermute x19, waiting for transfers between devices: 25.7 us -> 22.2 us  [swap(): return lax.ppermute(x, axis, [(i, i ^ bit) for i in range(count)])]
    ppermute x6, waiting for transfers between devices: 10.1 us -> 7.38 us  [meet(): lax.ppermute(strip, axis, pairs)]
    ppermute x6, starting transfers between devices: 14.7 us -> 13.8 us  [meet(): lax.ppermute(strip, axis, pairs)]
  transfers between devices with their start and end apart: 26 -> 26, of which waited for: 13 -> 14; matrix products, arithmetic and copies ran while one was open for 0% -> 0% of each run, Pallas kernels for 6% -> 6%
where the time goes in v3:
time: 79.3 us; the launch traced here: 79.1 us
  starting transfers between devices  39.5 us (50%)
  waiting for transfers between devices  29.6 us (37%)
  Pallas kernels  8.39 us (11%)
  between operations  0.82 us (1%)
    ppermute x19, waiting for transfers between devices, swap(): return lax.ppermute(x, axis, [(i, i ^ bit) for i in range(count)])  22.2 us
    ppermute x19, starting transfers between devices, swap(): return lax.ppermute(x, axis, [(i, i ^ bit) for i in range(count)])  22.2 us
    ppermute x6, starting transfers between devices, meet(): lax.ppermute(strip, axis, pairs)  13.8 us
    ppermute x6, waiting for transfers between devices, meet(): lax.ppermute(strip, axis, pairs)  7.38 us
    pallas_call x1, Pallas kernels, local(): call('mlp', 20 * MIB, functools.partial(mlp_kernel, in_pieces, out_pieces...  3.77 us
    ppermute x1, starting transfers between devices, weights_begin(): lax.ppermute(mine_out, ('row', 'col'), [(r * n_col + z, z * n_col + r) fo...  3.57 us
    pallas_call x1, Pallas kernels, local(): call('backward_conv', 8 * MIB, functools.partial(backward_conv_kernel, di...  1.69 us
    pallas_call x1, Pallas kernels, local(): call('forward_conv', 8 * MIB, functools.partial(forward_conv_kernel, dims...  1.62 us
  transfers between devices with their start and end apart: 26, of which 14 were waited for; matrix products, arithmetic and copies ran while one was open for 0% of the time, Pallas kernels for 6%

profile of v3, /device:TPU:1, one launch (start us, length us, event | category | flops | bytes accessed | tf_op | source)
XLA Modules:
  0.0 79.1 jit_solution(12219017525137793782)
XLA Ops:
  0.6 0.0 copy-start
  0.6 0.1 collective-permute-start
  0.8 2.7 %collective-permute-start.7 = (bf16[256,1024]{1,0:T(8,128)(2,1)}, bf16[256,1024]{1,0:T(8,128)(2,1)S(1)}, u32[]{:S(2)}, u32[]{:S(2)}) collective-permute-start(bf16[256,1024]{1,0:T(8,128)(2,1)} %refs_4_.1), channel_id=1, source_target_pairs={{0,8},{4,12},{8,0},{12,4},{1,9},{5,13},{9,1},{13,5},{2,10},{6,14},... | collective-permute-start | bytes 1572872 | tf_op jit(solution)/shard_map/w_in_row/ppermute | solution.py:29
  3.5 0.0 copy-start.2
  3.5 3.6 %collective-permute-start.6 = (bf16[512,256]{1,0:T(8,128)(2,1)S(1)}, bf16[512,256]{1,0:T(8,128)(2,1)S(1)}, u32[]{:S(2)}, u32[]{:S(2)}) collective-permute-start(bf16[512,256]{1,0:T(8,128)(2,1)S(1)} %constant_dynamic-slice_fusion), channel_id=1, source_target_pairs={{0,0},{1,4},{2,8},{3,12},{4,1},{5,5},{6,9},{7,13},{8,2},{9,6},{10,... | collective-permute-start | bytes 786440 | tf_op jit(solution)/shard_map/w_out_transposed/ppermute | solution.py:347
  7.1 0.0 copy-start.5
  7.1 0.0 copy-start.3
  7.1 0.0 copy-start.4
  7.2 1.3 %collective-permute-start.1 = (bf16[48,256]{1,0:T(8,128)(2,1)S(1)}, bf16[48,256]{1,0:T(8,128)(2,1)S(1)}, u32[]{:S(2)}, u32[]{:S(2)}) collective-permute-start(bf16[48,256]{1,0:T(8,128)(2,1)S(1)} %constant_dynamic-slice_fusion.1), channel_id=1, source_target_pairs={{0,16},{16,0},{1,17},{17,1},{2,18},{18,2},{3,19},{19,3},{4,20},{20... | collective-permute-start | bytes 73736 | tf_op jit(solution)/shard_map/image_rows/ppermute | solution.py:44
  8.4 1.8 %collective-permute-done.1.refs_0_ = bf16[48,256]{1,0:T(8,128)(2,1)S(1)} collective-permute-done((bf16[48,256]{1,0:T(8,128)(2,1)S(1)}, bf16[48,256]{1,0:T(8,128)(2,1)S(1)}, u32[]{:S(2)}, u32[]{:S(2)}) %collective-permute-start.1) | collective-permute-done | bytes 24608 | tf_op jit(solution)/shard_map/image_rows/ppermute | solution.py:44
  10.2 0.1 image_columns.1
  10.3 0.1 collective-permute-start.2
  10.4 5.6 %collective-permute-start.3 = (bf16[80,256]{1,0:T(8,128)(2,1)S(1)}, bf16[80,256]{1,0:T(8,128)(2,1)S(1)}, u32[]{:S(2)}, u32[]{:S(2)}) collective-permute-start(bf16[80,256]{1,0:T(8,128)(2,1)S(1)} %get-tuple-element.29), channel_id=1, source_target_pairs={{4,8},{8,4},{5,9},{9,5},{6,10},{10,6},{7,11},{11,7},{20,24},{24,20... | collective-permute-start | bytes 122888 | tf_op jit(solution)/shard_map/image_columns/ppermute | solution.py:44
  16.0 0.0 collective-permute-done.refs_6_
  16.0 0.0 collective-permute-done.2.refs_1_
  16.0 3.9 %collective-permute-done.3.refs_2_ = bf16[80,256]{1,0:T(8,128)(2,1)S(1)} collective-permute-done((bf16[80,256]{1,0:T(8,128)(2,1)S(1)}, bf16[80,256]{1,0:T(8,128)(2,1)S(1)}, u32[]{:S(2)}, u32[]{:S(2)}) %collective-permute-start.3) | collective-permute-done | bytes 40992 | tf_op jit(solution)/shard_map/image_columns/ppermute | solution.py:44
  19.9 1.6 %forward_conv.1.refs_0_ = bf16[528,256]{1,0:T(8,128)(2,1)S(1)} custom-call(bf16[256,256]{1,0:T(8,128)(2,1)S(1)} %bitcast.8, f32[7,7,256]{2,1,0:T(8,128)S(1)} %copy-done.3, f32[1,256]{1,0:T(1,128)S(1)} %bitcast.11, bf16[256,256]{1,0:T(8,128)(2,1)S(1)} %bitcast.9, bf16[48,256]{1,0:T(8,128)(2,1)S(1)} %collective-permute-done.1.refs_0_, ...), custom_call_target="tpu_custom_call" | custom-call | flops 192675840 | bytes 1048576 | tf_op jit(solution)/shard_map/forward_conv/pallas_call | solution.py:477
  21.6 3.5 %collective-permute-start.5 = (bf16[528,256]{1,0:T(8,128)(2,1)S(1)}, bf16[528,256]{1,0:T(8,128)(2,1)S(1)}, u32[]{:S(2)}, u32[]{:S(2)}) collective-permute-start(bf16[528,256]{1,0:T(8,128)(2,1)S(1)} %forward_conv.1.refs_0_), channel_id=1, source_target_pairs={{0,2},{1,3},{2,0},{3,1},{4,6},{5,7},{6,4},{7,5},{8,10},{9,11},{10,... | collective-permute-start | bytes 811016 | tf_op jit(solution)/shard_map/features/col_2/ppermute | solution.py:29
  25.1 0.0 collective-permute-done.6.refs_8_.refs_0_
  25.1 0.0 collective-permute-done.7.refs_5_
  25.1 1.2 %collective-permute-start.9 = (bf16[512,256]{1,0:T(8,128)(2,1)S(1)}, bf16[512,256]{1,0:T(8,128)(2,1)S(1)}, u32[]{:S(2)}, u32[]{:S(2)}) collective-permute-start(bf16[512,256]{1,0:T(8,128)(2,1)S(1)} %collective-permute-done.6.refs_8_.refs_0_), channel_id=1, source_target_pairs={{0,16},{16,0},{1,17},{17,1},{2,18},{18,2},{3,19},{19,3},{4,20},{20... | collective-permute-start | bytes 786440 | tf_op jit(solution)/shard_map/w_out_section/ppermute | solution.py:29
  26.3 0.0 collective-permute-start.8
  26.3 1.0 %collective-permute-start.4 = (bf16[528,256]{1,0:T(8,128)(2,1)S(1)}, bf16[528,256]{1,0:T(8,128)(2,1)S(1)}, u32[]{:S(2)}, u32[]{:S(2)}) collective-permute-start(bf16[528,256]{1,0:T(8,128)(2,1)S(1)} %forward_conv.1.refs_0_), channel_id=1, source_target_pairs={{0,1},{1,0},{2,3},{3,2},{4,5},{5,4},{6,7},{7,6},{8,9},{9,8},{10,11... | collective-permute-start | bytes 811016 | tf_op jit(solution)/shard_map/features/col_1/ppermute | solution.py:29
  27.3 3.3 %collective-permute-done.9.refs_10_.refs_2_ = bf16[512,256]{1,0:T(8,128)(2,1)S(1)} collective-permute-done((bf16[512,256]{1,0:T(8,128)(2,1)S(1)}, bf16[512,256]{1,0:T(8,128)(2,1)S(1)}, u32[]{:S(2)}, u32[]{:S(2)}) %collective-permute-start.9) | collective-permute-done | bytes 262176 | tf_op jit(solution)/shard_map/w_out_section/ppermute | solution.py:29
  30.6 3.5 %collective-permute-done.8.refs_9_.refs_1_ = bf16[512,256]{1,0:T(8,128)(2,1)S(1)} collective-permute-done((bf16[512,256]{1,0:T(8,128)(2,1)S(1)}, bf16[512,256]{1,0:T(8,128)(2,1)S(1)}, u32[]{:S(2)}, u32[]{:S(2)}) %collective-permute-start.8) | collective-permute-done | bytes 262176 | tf_op jit(solution)/shard_map/w_out_row/ppermute | solution.py:29
  34.1 0.0 collective-permute-done.5.refs_2_
  34.1 1.5 %collective-permute-start.10 = (bf16[528,256]{1,0:T(8,128)(2,1)S(1)}, bf16[528,256]{1,0:T(8,128)(2,1)S(1)}, u32[]{:S(2)}, u32[]{:S(2)}) collective-permute-start(bf16[528,256]{1,0:T(8,128)(2,1)S(1)} %collective-permute-done.5.refs_2_), channel_id=1, source_target_pairs={{0,1},{1,0},{2,3},{3,2},{4,5},{5,4},{6,7},{7,6},{8,9},{9,8},{10,11... | collective-permute-start | bytes 811016 | tf_op jit(solution)/shard_map/features/col_1/ppermute | solution.py:29
  35.6 0.3 collective-permute-start.12
  35.8 0.1 collective-permute-done.4.refs_1_
  35.9 6.8 %collective-permute-done.10.refs_3_ = bf16[528,256]{1,0:T(8,128)(2,1)S(1)} collective-permute-done((bf16[528,256]{1,0:T(8,128)(2,1)S(1)}, bf16[528,256]{1,0:T(8,128)(2,1)S(1)}, u32[]{:S(2)}, u32[]{:S(2)}) %collective-permute-start.10) | collective-permute-done | bytes 270368 | tf_op jit(solution)/shard_map/features/col_1/ppermute | solution.py:29
  42.7 0.8 collective-permute-start.13
  43.4 0.0 collective-permute-start.11
  43.4 0.5 collective-permute-start.15
  44.0 0.0 collective-permute-start.14
  44.0 0.0 collective-permute-done.12.refs_11_.refs_3_
  44.0 0.6 collective-permute-done.13.refs_12_.refs_4_
  44.6 0.4 collective-permute-start.16
  45.0 0.4 collective-permute-done.11.refs_7_
  45.4 0.4 collective-permute-done.15.refs_14_.refs_6_
  45.7 0.4 collective-permute-done.14.refs_13_.refs_5_
  46.1 0.4 collective-permute-done.16.refs_15_.refs_7_
  46.5 3.8 %mlp.1 = (bf16[256,256]{1,0:T(8,128)(2,1)S(1)}, bf16[256,256]{1,0:T(8,128)(2,1)S(1)}, bf16[256,256]{1,0:T(8,128)(2,1)S(1)}, bf16[256,256]{1,0:T(8,128)(2,1)S(1)}, bf16[256,1024]{1,0:T(8,128)(2,1)S(1)}) custom-call(bf16[528,256]{1,0:T(8,128)(2,1)S(1)} %forward_conv.1.refs_0_, bf16[528,256]{1,0:T(8,128)(2,1)S(1)} %collective-permute-done.4.refs_1_, ...), custom_call_target="tpu_custom_call" | custom-call | flops 1610612736 | bytes 1048576 | tf_op jit(solution)/shard_map/mlp/pallas_call | solution.py:498
  50.3 1.1 %collective-permute-start.17 = (bf16[256,256]{1,0:T(8,128)(2,1)S(1)}, bf16[256,256]{1,0:T(8,128)(2,1)S(1)}, u32[]{:S(2)}, u32[]{:S(2)}) collective-permute-start(bf16[256,256]{1,0:T(8,128)(2,1)S(1)} %get-tuple-element.35), channel_id=1, source_target_pairs={{0,1},{1,0},{2,3},{3,2},{4,5},{5,4},{6,7},{7,6},{8,9},{9,8},{10,11... | collective-permute-start | bytes 393224 | tf_op jit(solution)/shard_map/grad_sums/col_1/ppermute | solution.py:29
  51.4 1.1 %collective-permute-start.20 = (bf16[256,256]{1,0:T(8,128)(2,1)S(1)}, bf16[256,256]{1,0:T(8,128)(2,1)S(1)}, u32[]{:S(2)}, u32[]{:S(2)}) collective-permute-start(bf16[256,256]{1,0:T(8,128)(2,1)S(1)} %get-tuple-element.42), channel_id=1, source_target_pairs={{0,2},{1,3},{2,0},{3,1},{4,6},{5,7},{6,4},{7,5},{8,10},{9,11},{10,... | collective-permute-start | bytes 393224 | tf_op jit(solution)/shard_map/grad_sums/col_2/ppermute | solution.py:29
  52.5 1.4 %collective-permute-start.21 = (bf16[256,256]{1,0:T(8,128)(2,1)S(1)}, bf16[256,256]{1,0:T(8,128)(2,1)S(1)}, u32[]{:S(2)}, u32[]{:S(2)}) collective-permute-start(bf16[256,256]{1,0:T(8,128)(2,1)S(1)} %get-tuple-element.43), channel_id=1, source_target_pairs={{0,3},{1,2},{2,1},{3,0},{4,7},{5,6},{6,5},{7,4},{8,11},{9,10},{10,... | collective-permute-start | bytes 393224 | tf_op jit(solution)/shard_map/grad_sums/col_3/ppermute | solution.py:29
  53.9 1.2 %collective-permute-done.17.refs_1_ = bf16[256,256]{1,0:T(8,128)(2,1)S(1)} collective-permute-done((bf16[256,256]{1,0:T(8,128)(2,1)S(1)}, bf16[256,256]{1,0:T(8,128)(2,1)S(1)}, u32[]{:S(2)}, u32[]{:S(2)}) %collective-permute-start.17) | collective-permute-done | bytes 131104 | tf_op jit(solution)/shard_map/grad_sums/col_1/ppermute | solution.py:29
  55.0 1.1 %branch.1 = (bf16[256,256]{1,0:T(8,128)(2,1)S(1)}, bf16[256,256]{1,0:T(8,128)(2,1)S(1)}, bf16[256,256]{1,0:T(8,128)(2,1)S(1)}, bf16[256,256]{1,0:T(8,128)(2,1)S(1)}) custom-call(bf16[256,1024]{1,0:T(8,128)(2,1)S(1)} %get-tuple-element.36.hidden, bf16[512,256]{1,0:T(8,128)(2,1)S(1)} %collective-permute-done.6.refs_8_.refs_0_, ...), custom_call_target="tpu_custom_call" | custom-call | flops 536870912 | bytes 1048576 | tf_op jit(solution)/shard_map/branch/pallas_call | solution.py:518
  56.1 1.1 %collective-permute-start.19 = (bf16[256,256]{1,0:T(8,128)(2,1)S(1)}, bf16[256,256]{1,0:T(8,128)(2,1)S(1)}, u32[]{:S(2)}, u32[]{:S(2)}) collective-permute-start(bf16[256,256]{1,0:T(8,128)(2,1)S(1)} %get-tuple-element.40), channel_id=1, source_target_pairs={{0,1},{1,0},{2,3},{3,2},{4,5},{5,4},{6,7},{7,6},{8,9},{9,8},{10,11... | collective-permute-start | bytes 393224 | tf_op jit(solution)/shard_map/branch_sums/col_1/ppermute | solution.py:29
  57.2 5.3 %collective-permute-done.20.refs_2_ = bf16[256,256]{1,0:T(8,128)(2,1)S(1)} collective-permute-done((bf16[256,256]{1,0:T(8,128)(2,1)S(1)}, bf16[256,256]{1,0:T(8,128)(2,1)S(1)}, u32[]{:S(2)}, u32[]{:S(2)}) %collective-permute-start.20) | collective-permute-done | bytes 131104 | tf_op jit(solution)/shard_map/grad_sums/col_2/ppermute | solution.py:29
  62.5 0.1 grad_sum.1
  62.6 0.3 collective-permute-start.22
  62.9 3.1 %collective-permute-start.18 = (bf16[256,256]{1,0:T(8,128)(2,1)S(1)}, bf16[256,256]{1,0:T(8,128)(2,1)S(1)}, u32[]{:S(2)}, u32[]{:S(2)}) collective-permute-start(bf16[256,256]{1,0:T(8,128)(2,1)S(1)} %get-tuple-element.38), channel_id=1, source_target_pairs={{0,1},{1,0},{2,3},{3,2},{4,5},{5,4},{6,7},{7,6},{8,9},{9,8},{10,11... | collective-permute-start | bytes 393224 | tf_op jit(solution)/shard_map/branch_sums/col_1/ppermute | solution.py:29
  65.9 0.0 collective-permute-done.22.refs_0_
  65.9 0.0 collective-permute-done.19
  66.0 2.4 %collective-permute-start.23 = (bf16[256,256]{1,0:T(8,128)(2,1)S(1)}, bf16[256,256]{1,0:T(8,128)(2,1)S(1)}, u32[]{:S(2)}, u32[]{:S(2)}) collective-permute-start(bf16[256,256]{1,0:T(8,128)(2,1)S(1)} %add_convert_fusion.1), channel_id=1, source_target_pairs={{0,2},{1,3},{2,0},{3,1},{4,6},{5,7},{6,4},{7,5},{8,10},{9,11},{10,... | collective-permute-start | bytes 393224 | tf_op jit(solution)/shard_map/branch_sums/col_2/ppermute | solution.py:29
  68.4 0.1 grad_columns.1
  68.5 2.7 %collective-permute-start.24 = (bf16[80,256]{1,0:T(8,128)(2,1)S(1)}, bf16[80,256]{1,0:T(8,128)(2,1)S(1)}, u32[]{:S(2)}, u32[]{:S(2)}) collective-permute-start(bf16[80,256]{1,0:T(8,128)(2,1)S(1)} %get-tuple-element.47), channel_id=1, source_target_pairs={{0,4},{8,12},{4,0},{12,8},{1,5},{9,13},{5,1},{13,9},{2,6},{10,14},... | collective-permute-start | bytes 122888 | tf_op jit(solution)/shard_map/grad_columns/ppermute | solution.py:44
  71.1 3.9 %collective-permute-start.25 = (bf16[80,256]{1,0:T(8,128)(2,1)S(1)}, bf16[80,256]{1,0:T(8,128)(2,1)S(1)}, u32[]{:S(2)}, u32[]{:S(2)}) collective-permute-start(bf16[80,256]{1,0:T(8,128)(2,1)S(1)} %get-tuple-element.48), channel_id=1, source_target_pairs={{4,8},{8,4},{5,9},{9,5},{6,10},{10,6},{7,11},{11,7},{20,24},{24,20... | collective-permute-start | bytes 122888 | tf_op jit(solution)/shard_map/grad_columns/ppermute | solution.py:44
  75.0 0.0 collective-permute-done.24.refs_1_
  75.0 1.7 %collective-permute-done.25.refs_2_ = bf16[80,256]{1,0:T(8,128)(2,1)S(1)} collective-permute-done((bf16[80,256]{1,0:T(8,128)(2,1)S(1)}, bf16[80,256]{1,0:T(8,128)(2,1)S(1)}, u32[]{:S(2)}, u32[]{:S(2)}) %collective-permute-start.25) | collective-permute-done | bytes 40992 | tf_op jit(solution)/shard_map/grad_columns/ppermute | solution.py:44
  76.7 1.7 %backward_conv.1 = f32[256,256]{1,0:T(8,128)} custom-call(f32[256,256]{1,0:T(8,128)S(1)} %get-tuple-element.46.cells.grad, f32[7,7,256]{2,1,0:T(8,128)S(1)} %copy-done.3, bf16[256,256]{1,0:T(8,128)(2,1)S(1)} %bitcast.10, bf16[48,256]{1,0:T(8,128)(2,1)S(1)} %collective-permute-done.22.refs_0_, bf16[80,256]{1,0:T(8,128)(2,1)S(1)} %collective-permute-done.24.refs_1_, ...), custom_call_target="tpu_custom_call" | custom-call | flops 192675840 | bytes 1048576 | tf_op jit(solution)/shard_map/backward_conv/pallas_call | solution.py:538
  78.4 0.0 collective-permute-done.18
  78.4 0.0 collective-permute-done.23
  78.4 0.7 add_convert_fusion
  (11 shorter events, 0.1 us)
Async XLA Ops:
  0.6 2.8 %copy-start = (bf16[1024,256]{1,0:T(8,128)(2,1)S(1)}, bf16[1024,256]{1,0:T(8,128)(2,1)}, u32[]{:S(2)}) copy-start(bf16[1024,256]{1,0:T(8,128)(2,1)} %param.10) | copy-start | bytes 1572868
  0.6 15.3 %collective-permute-start = (bf16[256,1024]{1,0:T(8,128)(2,1)}, bf16[256,1024]{1,0:T(8,128)(2,1)S(1)}, u32[]{:S(2)}, u32[]{:S(2)}) collective-permute-start(bf16[256,1024]{1,0:T(8,128)(2,1)} %refs_4_.1), channel_id=1, source_target_pairs={{0,4},{4,0},{8,12},{12,8},{1,5},{5,1},{9,13},{13,9},{2,6},{6,2},{1... | collective-permute-start | bytes 1572872 | tf_op jit(solution)/shard_map/w_in_core/ppermute | solution.py:29
  0.8 24.3 %collective-permute-start.7 = (bf16[256,1024]{1,0:T(8,128)(2,1)}, bf16[256,1024]{1,0:T(8,128)(2,1)S(1)}, u32[]{:S(2)}, u32[]{:S(2)}) collective-permute-start(bf16[256,1024]{1,0:T(8,128)(2,1)} %refs_4_.1), channel_id=1, source_target_pairs={{0,8},{4,12},{8,0},{12,4},{1,9},{5,13},{9,1},{13,5},{2,10},{6,14},... | collective-permute-start | bytes 1572872 | tf_op jit(solution)/shard_map/w_in_row/ppermute | solution.py:29
  3.5 3.6 %copy-start.1 = (bf16[16,16,256]{2,1,0:T(8,128)(2,1)S(1)}, bf16[16,16,256]{2,1,0:T(8,128)(2,1)}, u32[]{:S(2)}) copy-start(bf16[16,16,256]{2,1,0:T(8,128)(2,1)} %param.6) | copy-start | bytes 393220
  3.5 16.4 %copy-start.2 = (bf16[16,16,256]{2,1,0:T(8,128)(2,1)S(1)}, bf16[16,16,256]{2,1,0:T(8,128)(2,1)}, u32[]{:S(2)}) copy-start(bf16[16,16,256]{2,1,0:T(8,128)(2,1)} %param.11) | copy-start | bytes 393220
  3.5 21.6 %collective-permute-start.6 = (bf16[512,256]{1,0:T(8,128)(2,1)S(1)}, bf16[512,256]{1,0:T(8,128)(2,1)S(1)}, u32[]{:S(2)}, u32[]{:S(2)}) collective-permute-start(bf16[512,256]{1,0:T(8,128)(2,1)S(1)} %constant_dynamic-slice_fusion), channel_id=1, source_target_pairs={{0,0},{1,4},{2,8},{3,12},{4,1},{5,5},{6,9},{7,13},{8,2},{9,6},{10,... | collective-permute-start | bytes 786440 | tf_op jit(solution)/shard_map/w_out_transposed/ppermute | solution.py:347
  7.1 12.8 %copy-start.5 = (f32[256]{0:T(256)S(1)}, f32[256]{0:T(256)}, u32[]{:S(2)}) copy-start(f32[256]{0:T(256)} %param.8) | copy-start | bytes 3076
  7.1 12.8 %copy-start.3 = (f32[7,7,256]{2,1,0:T(8,128)S(1)}, f32[7,7,256]{2,1,0:T(8,128)}, u32[]{:S(2)}) copy-start(f32[7,7,256]{2,1,0:T(8,128)} %taps.3) | copy-start | bytes 150532
  7.1 39.3 %copy-start.4 = (bf16[256,1024]{1,0:T(8,128)(2,1)S(1)}, bf16[256,1024]{1,0:T(8,128)(2,1)}, u32[]{:S(2)}) copy-start(bf16[256,1024]{1,0:T(8,128)(2,1)} %refs_4_.1) | copy-start | bytes 1572868
  7.2 3.0 %collective-permute-start.1 = (bf16[48,256]{1,0:T(8,128)(2,1)S(1)}, bf16[48,256]{1,0:T(8,128)(2,1)S(1)}, u32[]{:S(2)}, u32[]{:S(2)}) collective-permute-start(bf16[48,256]{1,0:T(8,128)(2,1)S(1)} %constant_dynamic-slice_fusion.1), channel_id=1, source_target_pairs={{0,16},{16,0},{1,17},{17,1},{2,18},{18,2},{3,19},{19,3},{4,20},{20... | collective-permute-start | bytes 73736 | tf_op jit(solution)/shard_map/image_rows/ppermute | solution.py:44
  10.3 5.7 %collective-permute-start.2 = (bf16[80,256]{1,0:T(8,128)(2,1)S(1)}, bf16[80,256]{1,0:T(8,128)(2,1)S(1)}, u32[]{:S(2)}, u32[]{:S(2)}) collective-permute-start(bf16[80,256]{1,0:T(8,128)(2,1)S(1)} %get-tuple-element.28), channel_id=1, source_target_pairs={{0,4},{8,12},{4,0},{12,8},{1,5},{9,13},{5,1},{13,9},{2,6},{10,14},... | collective-permute-start | bytes 122888 | tf_op jit(solution)/shard_map/image_columns/ppermute | solution.py:44
  10.4 9.6 %collective-permute-start.3 = (bf16[80,256]{1,0:T(8,128)(2,1)S(1)}, bf16[80,256]{1,0:T(8,128)(2,1)S(1)}, u32[]{:S(2)}, u32[]{:S(2)}) collective-permute-start(bf16[80,256]{1,0:T(8,128)(2,1)S(1)} %get-tuple-element.29), channel_id=1, source_target_pairs={{4,8},{8,4},{5,9},{9,5},{6,10},{10,6},{7,11},{11,7},{20,24},{24,20... | collective-permute-start | bytes 122888 | tf_op jit(solution)/shard_map/image_columns/ppermute | solution.py:44
  21.6 12.5 %collective-permute-start.5 = (bf16[528,256]{1,0:T(8,128)(2,1)S(1)}, bf16[528,256]{1,0:T(8,128)(2,1)S(1)}, u32[]{:S(2)}, u32[]{:S(2)}) collective-permute-start(bf16[528,256]{1,0:T(8,128)(2,1)S(1)} %forward_conv.1.refs_0_), channel_id=1, source_target_pairs={{0,2},{1,3},{2,0},{3,1},{4,6},{5,7},{6,4},{7,5},{8,10},{9,11},{10,... | collective-permute-start | bytes 811016 | tf_op jit(solution)/shard_map/features/col_2/ppermute | solution.py:29
  25.1 5.5 %collective-permute-start.9 = (bf16[512,256]{1,0:T(8,128)(2,1)S(1)}, bf16[512,256]{1,0:T(8,128)(2,1)S(1)}, u32[]{:S(2)}, u32[]{:S(2)}) collective-permute-start(bf16[512,256]{1,0:T(8,128)(2,1)S(1)} %collective-permute-done.6.refs_8_.refs_0_), channel_id=1, source_target_pairs={{0,16},{16,0},{1,17},{17,1},{2,18},{18,2},{3,19},{19,3},{4,20},{20... | collective-permute-start | bytes 786440 | tf_op jit(solution)/shard_map/w_out_section/ppermute | solution.py:29
  26.3 7.8 %collective-permute-start.8 = (bf16[512,256]{1,0:T(8,128)(2,1)S(1)}, bf16[512,256]{1,0:T(8,128)(2,1)S(1)}, u32[]{:S(2)}, u32[]{:S(2)}) collective-permute-start(bf16[512,256]{1,0:T(8,128)(2,1)S(1)} %collective-permute-done.6.refs_8_.refs_0_), channel_id=1, source_target_pairs={{0,8},{4,12},{8,0},{12,4},{1,9},{5,13},{9,1},{13,5},{2,10},{6,14},... | collective-permute-start | bytes 786440 | tf_op jit(solution)/shard_map/w_out_row/ppermute | solution.py:29
  26.3 9.6 %collective-permute-start.4 = (bf16[528,256]{1,0:T(8,128)(2,1)S(1)}, bf16[528,256]{1,0:T(8,128)(2,1)S(1)}, u32[]{:S(2)}, u32[]{:S(2)}) collective-permute-start(bf16[528,256]{1,0:T(8,128)(2,1)S(1)} %forward_conv.1.refs_0_), channel_id=1, source_target_pairs={{0,1},{1,0},{2,3},{3,2},{4,5},{5,4},{6,7},{7,6},{8,9},{9,8},{10,11... | collective-permute-start | bytes 811016 | tf_op jit(solution)/shard_map/features/col_1/ppermute | solution.py:29
  34.1 8.6 %collective-permute-start.10 = (bf16[528,256]{1,0:T(8,128)(2,1)S(1)}, bf16[528,256]{1,0:T(8,128)(2,1)S(1)}, u32[]{:S(2)}, u32[]{:S(2)}) collective-permute-start(bf16[528,256]{1,0:T(8,128)(2,1)S(1)} %collective-permute-done.5.refs_2_), channel_id=1, source_target_pairs={{0,1},{1,0},{2,3},{3,2},{4,5},{5,4},{6,7},{7,6},{8,9},{9,8},{10,11... | collective-permute-start | bytes 811016 | tf_op jit(solution)/shard_map/features/col_1/ppermute | solution.py:29
  35.6 8.4 %collective-permute-start.12 = (bf16[512,256]{1,0:T(8,128)(2,1)S(1)}, bf16[512,256]{1,0:T(8,128)(2,1)S(1)}, u32[]{:S(2)}, u32[]{:S(2)}) collective-permute-start(bf16[512,256]{1,0:T(8,128)(2,1)S(1)} %collective-permute-done.8.refs_9_.refs_1_), channel_id=1, source_target_pairs={{0,16},{16,0},{1,17},{17,1},{2,18},{18,2},{3,19},{19,3},{4,20},{20... | collective-permute-start | bytes 786440 | tf_op jit(solution)/shard_map/w_out_both/ppermute | solution.py:29
  42.7 1.9 %collective-permute-start.13 = (bf16[512,256]{1,0:T(8,128)(2,1)S(1)}, bf16[512,256]{1,0:T(8,128)(2,1)S(1)}, u32[]{:S(2)}, u32[]{:S(2)}) collective-permute-start(bf16[512,256]{1,0:T(8,128)(2,1)S(1)} %collective-permute-done.6.refs_8_.refs_0_), channel_id=1, source_target_pairs={{0,4},{4,0},{8,12},{12,8},{1,5},{5,1},{9,13},{13,9},{2,6},{6,2},{1... | collective-permute-start | bytes 786440 | tf_op jit(solution)/shard_map/w_out_core_0_0/ppermute | solution.py:29
  43.4 1.9 %collective-permute-start.11 = (bf16[256,1024]{1,0:T(8,128)(2,1)S(1)}, bf16[256,1024]{1,0:T(8,128)(2,1)S(1)}, u32[]{:S(2)}, u32[]{:S(2)}) collective-permute-start(bf16[256,1024]{1,0:T(8,128)(2,1)S(1)} %collective-permute-done.7.refs_5_), channel_id=1, source_target_pairs={{0,4},{4,0},{8,12},{12,8},{1,5},{5,1},{9,13},{13,9},{2,6},{6,2},{1... | collective-permute-start | bytes 1572872 | tf_op jit(solution)/shard_map/w_in_core_2/ppermute | solution.py:29
  43.4 2.3 %collective-permute-start.15 = (bf16[512,256]{1,0:T(8,128)(2,1)S(1)}, bf16[512,256]{1,0:T(8,128)(2,1)S(1)}, u32[]{:S(2)}, u32[]{:S(2)}) collective-permute-start(bf16[512,256]{1,0:T(8,128)(2,1)S(1)} %collective-permute-done.9.refs_10_.refs_2_), channel_id=1, source_target_pairs={{0,4},{4,0},{8,12},{12,8},{1,5},{5,1},{9,13},{13,9},{2,6},{6,2},{1... | collective-permute-start | bytes 786440 | tf_op jit(solution)/shard_map/w_out_core_0_1/ppermute | solution.py:29
  44.0 2.2 %collective-permute-start.14 = (bf16[512,256]{1,0:T(8,128)(2,1)S(1)}, bf16[512,256]{1,0:T(8,128)(2,1)S(1)}, u32[]{:S(2)}, u32[]{:S(2)}) collective-permute-start(bf16[512,256]{1,0:T(8,128)(2,1)S(1)} %collective-permute-done.8.refs_9_.refs_1_), channel_id=1, source_target_pairs={{0,4},{4,0},{8,12},{12,8},{1,5},{5,1},{9,13},{13,9},{2,6},{6,2},{1... | collective-permute-start | bytes 786440 | tf_op jit(solution)/shard_map/w_out_core_2_0/ppermute | solution.py:29
  44.6 1.9 %collective-permute-start.16 = (bf16[512,256]{1,0:T(8,128)(2,1)S(1)}, bf16[512,256]{1,0:T(8,128)(2,1)S(1)}, u32[]{:S(2)}, u32[]{:S(2)}) collective-permute-start(bf16[512,256]{1,0:T(8,128)(2,1)S(1)} %collective-permute-done.12.refs_11_.refs_3_), channel_id=1, source_target_pairs={{0,4},{4,0},{8,12},{12,8},{1,5},{5,1},{9,13},{13,9},{2,6},{6,2},{1... | collective-permute-start | bytes 786440 | tf_op jit(solution)/shard_map/w_out_core_2_1/ppermute | solution.py:29
  50.3 4.8 %collective-permute-start.17 = (bf16[256,256]{1,0:T(8,128)(2,1)S(1)}, bf16[256,256]{1,0:T(8,128)(2,1)S(1)}, u32[]{:S(2)}, u32[]{:S(2)}) collective-permute-start(bf16[256,256]{1,0:T(8,128)(2,1)S(1)} %get-tuple-element.35), channel_id=1, source_target_pairs={{0,1},{1,0},{2,3},{3,2},{4,5},{5,4},{6,7},{7,6},{8,9},{9,8},{10,11... | collective-permute-start | bytes 393224 | tf_op jit(solution)/shard_map/grad_sums/col_1/ppermute | solution.py:29
  51.4 11.1 %collective-permute-start.20 = (bf16[256,256]{1,0:T(8,128)(2,1)S(1)}, bf16[256,256]{1,0:T(8,128)(2,1)S(1)}, u32[]{:S(2)}, u32[]{:S(2)}) collective-permute-start(bf16[256,256]{1,0:T(8,128)(2,1)S(1)} %get-tuple-element.42), channel_id=1, source_target_pairs={{0,2},{1,3},{2,0},{3,1},{4,6},{5,7},{6,4},{7,5},{8,10},{9,11},{10,... | collective-permute-start | bytes 393224 | tf_op jit(solution)/shard_map/grad_sums/col_2/ppermute | solution.py:29
  52.5 10.0 %collective-permute-start.21 = (bf16[256,256]{1,0:T(8,128)(2,1)S(1)}, bf16[256,256]{1,0:T(8,128)(2,1)S(1)}, u32[]{:S(2)}, u32[]{:S(2)}) collective-permute-start(bf16[256,256]{1,0:T(8,128)(2,1)S(1)} %get-tuple-element.43), channel_id=1, source_target_pairs={{0,3},{1,2},{2,1},{3,0},{4,7},{5,6},{6,5},{7,4},{8,11},{9,10},{10,... | collective-permute-start | bytes 393224 | tf_op jit(solution)/shard_map/grad_sums/col_3/ppermute | solution.py:29
  56.1 9.8 %collective-permute-start.19 = (bf16[256,256]{1,0:T(8,128)(2,1)S(1)}, bf16[256,256]{1,0:T(8,128)(2,1)S(1)}, u32[]{:S(2)}, u32[]{:S(2)}) collective-permute-start(bf16[256,256]{1,0:T(8,128)(2,1)S(1)} %get-tuple-element.40), channel_id=1, source_target_pairs={{0,1},{1,0},{2,3},{3,2},{4,5},{5,4},{6,7},{7,6},{8,9},{9,8},{10,11... | collective-permute-start | bytes 393224 | tf_op jit(solution)/shard_map/branch_sums/col_1/ppermute | solution.py:29
  62.6 3.4 %collective-permute-start.22 = (bf16[48,256]{1,0:T(8,128)(2,1)S(1)}, bf16[48,256]{1,0:T(8,128)(2,1)S(1)}, u32[]{:S(2)}, u32[]{:S(2)}) collective-permute-start(bf16[48,256]{1,0:T(8,128)(2,1)S(1)} %get-tuple-element.44), channel_id=1, source_target_pairs={{0,16},{16,0},{1,17},{17,1},{2,18},{18,2},{3,19},{19,3},{4,20},{20... | collective-permute-start | bytes 73736 | tf_op jit(solution)/shard_map/grad_rows/ppermute | solution.py:44
  62.9 15.5 %collective-permute-start.18 = (bf16[256,256]{1,0:T(8,128)(2,1)S(1)}, bf16[256,256]{1,0:T(8,128)(2,1)S(1)}, u32[]{:S(2)}, u32[]{:S(2)}) collective-permute-start(bf16[256,256]{1,0:T(8,128)(2,1)S(1)} %get-tuple-element.38), channel_id=1, source_target_pairs={{0,1},{1,0},{2,3},{3,2},{4,5},{5,4},{6,7},{7,6},{8,9},{9,8},{10,11... | collective-permute-start | bytes 393224 | tf_op jit(solution)/shard_map/branch_sums/col_1/ppermute | solution.py:29
  66.0 12.4 %collective-permute-start.23 = (bf16[256,256]{1,0:T(8,128)(2,1)S(1)}, bf16[256,256]{1,0:T(8,128)(2,1)S(1)}, u32[]{:S(2)}, u32[]{:S(2)}) collective-permute-start(bf16[256,256]{1,0:T(8,128)(2,1)S(1)} %add_convert_fusion.1), channel_id=1, source_target_pairs={{0,2},{1,3},{2,0},{3,1},{4,6},{5,7},{6,4},{7,5},{8,10},{9,11},{10,... | collective-permute-start | bytes 393224 | tf_op jit(solution)/shard_map/branch_sums/col_2/ppermute | solution.py:29
  68.5 6.5 %collective-permute-start.24 = (bf16[80,256]{1,0:T(8,128)(2,1)S(1)}, bf16[80,256]{1,0:T(8,128)(2,1)S(1)}, u32[]{:S(2)}, u32[]{:S(2)}) collective-permute-start(bf16[80,256]{1,0:T(8,128)(2,1)S(1)} %get-tuple-element.47), channel_id=1, source_target_pairs={{0,4},{8,12},{4,0},{12,8},{1,5},{9,13},{5,1},{13,9},{2,6},{10,14},... | collective-permute-start | bytes 122888 | tf_op jit(solution)/shard_map/grad_columns/ppermute | solution.py:44
  71.1 5.5 %collective-permute-start.25 = (bf16[80,256]{1,0:T(8,128)(2,1)S(1)}, bf16[80,256]{1,0:T(8,128)(2,1)S(1)}, u32[]{:S(2)}, u32[]{:S(2)}) collective-permute-start(bf16[80,256]{1,0:T(8,128)(2,1)S(1)} %get-tuple-element.48), channel_id=1, source_target_pairs={{4,8},{8,4},{5,9},{9,5},{6,10},{10,6},{7,11},{11,7},{20,24},{24,20... | collective-permute-start | bytes 122888 | tf_op jit(solution)/shard_map/grad_columns/ppermute | solution.py:44

commit v4 on v3

--- a/solution.py
+++ b/solution.py
@@ -189,44 +189,26 @@
     message[message.shape[0] - cells :, :] = upstream[...]
 
 
-def copy_pieces(pieces, refs, whole, sems):
-    copies = []
-    for n, (ref, (row_at, column_at)) in enumerate(zip(refs, pieces)):
-        rows, columns = ref.shape
-        row, column = row_at(), column_at()
-        copy = pltpu.make_async_copy(
-            ref,
-            whole.at[
-                pl.ds(row if isinstance(row, int) else pl.multiple_of(row, rows), rows),
-                pl.ds(column if isinstance(column, int) else pl.multiple_of(column, columns), columns),
-            ],
-            sems.at[n],
-        )
-        copy.start()
-        copies.append(copy)
-    return copies
-
-
-def mlp_kernel(in_pieces, out_pieces, n_col, *refs):
+def mlp_kernel(in_slots, out_slots, n_col, *refs):
     messages, refs = refs[:n_col], refs[n_col:]
-    in_refs, refs = refs[: len(in_pieces)], refs[len(in_pieces) :]
-    out_refs, refs = refs[: len(out_pieces)], refs[len(out_pieces) :]
+    in_refs, refs = refs[: len(in_slots)], refs[len(in_slots) :]
+    n_out = len(out_slots) * n_col
+    out_refs, refs = refs[:n_out], refs[n_out:]
     outs, refs = refs[:n_col], refs[n_col:]
-    hidden, whole, whole_out, normed, scaled, act_grad, in_sems, out_sems = refs
-    copies = copy_pieces(in_pieces, in_refs, whole, in_sems)
-    out_copies = copy_pieces(out_pieces, out_refs, whole_out, out_sems)
+    hidden, normed, scaled, ups, gains, grads, act_grad = refs
     cells, channels = outs[0].shape
     up_at = messages[0].shape[0] - cells
     all_channels = n_col * channels
     per = cells // channels
 
-    means, gains = [], []
-    for message in messages:
+    means = []
+    for k, message in enumerate(messages):
         tail = message[cells:up_at, :].astype(F32)
         flat = tail[:per, :] + tail[per : 2 * per, :]
         row = jnp.concatenate([flat[p : p + 1, :] for p in range(per)], axis=1)
         means.append(jnp.broadcast_to(row, (128, cells)).T[:, :1])
-        gains.append(tail[2 * per : 2 * per + 1, :] + tail[2 * per + 1 : 2 * per + 2, :] + tail[2 * per + 2 : 2 * per + 3, :])
+        gains[k] = jnp.broadcast_to(sum(tail[2 * per + t : 2 * per + t + 1, :] for t in range(3)), gains.shape[1:])
+        ups[k] = message[up_at:, :]
     centre = sum(means) * (1.0 / n_col)
     spread = jnp.zeros((cells, 1), F32)
     for k, message in enumerate(messages):
@@ -237,55 +219,63 @@
     for k in range(n_col):
         value = normed[k] * inv_std
         normed[k] = value
-        scaled[:, k * channels : (k + 1) * channels] = (value * gains[k]).astype(BF16)
-    for copy in copies:
-        copy.wait()
-    for copy in out_copies:
-        copy.wait()
-    width = hidden.shape[1]
-    tile = min(256, width)
-    for start in range(0, width, tile):
-        hidden_grad = jnp.zeros((cells, tile), F32)
-        for k, message in enumerate(messages):
-            hidden_grad += lax.dot_general(
-                message[up_at:, :],
-                whole_out[start : start + tile, k * channels : (k + 1) * channels],
+        scaled[k] = (value * gains[k][:1, :]).astype(BF16)
+    share = act_grad.shape[2]
+    tile = min(256, share)
+    slots = [slot() for slot in in_slots]
+    places = []
+    for p, (part, blocks) in enumerate(out_slots):
+        blocks = [block() for block in blocks]
+        place = part() * share
+        places.append(place)
+        for start in range(0, share, tile):
+            columns = pl.ds(pl.multiple_of(place + start, tile), tile)
+            preact = sum(
+                jnp.dot(scaled[slot], ref[:, columns], preferred_element_type=F32)
+                for slot, ref in zip(slots, in_refs)
+            )
+            hidden_grad = sum(
+                lax.dot_general(
+                    ups[block],
+                    out_refs[p * n_col + j][start : start + tile, :],
+                    (((1,), (1,)), ((), ())),
+                    preferred_element_type=F32,
+                )
+                for j, block in enumerate(blocks)
+            )
+            phi = 0.5 * (1.0 + lax.erf(preact * math.sqrt(0.5)))
+            hidden[p, :, start : start + tile] = (preact * phi).astype(BF16)
+            slope = phi + preact * jnp.exp(-0.5 * preact * preact) * (1.0 / math.sqrt(2.0 * math.pi))
+            act_grad[p, :, start : start + tile] = (hidden_grad * slope).astype(BF16)
+    first, second = jnp.zeros((cells, 1), F32), jnp.zeros((cells, 1), F32)
+    for slot, ref in zip(slots, in_refs):
+        grad = sum(
+            lax.dot_general(
+                act_grad[p],
+                ref[:, pl.ds(pl.multiple_of(place, share), share)],
                 (((1,), (1,)), ((), ())),
                 preferred_element_type=F32,
             )
-        preact = jnp.dot(scaled[...], whole[:, start : start + tile], preferred_element_type=F32)
-        phi = 0.5 * (1.0 + lax.erf(preact * math.sqrt(0.5)))
-        hidden[:, start : start + tile] = (preact * phi).astype(BF16)
-        slope = phi + preact * jnp.exp(-0.5 * preact * preact) * (1.0 / math.sqrt(2.0 * math.pi))
-        act_grad[:, start : start + tile] = (hidden_grad * slope).astype(BF16)
-    first, second = jnp.zeros((cells, 1), F32), jnp.zeros((cells, 1), F32)
-    grads = []
-    for k in range(n_col):
-        grad = lax.dot_general(
-            act_grad[...],
-            whole[k * channels : (k + 1) * channels, :],
-            (((1,), (1,)), ((), ())),
-            preferred_element_type=F32,
-        ) * gains[k]
-        grads.append(grad)
+            for p, place in enumerate(places)
+        ) * gains[slot][:1, :]
+        grads[slot] = grad
         first += jnp.sum(grad, axis=1, keepdims=True)
-        second += jnp.sum(grad * normed[k], axis=1, keepdims=True)
+        second += jnp.sum(grad * normed[slot], axis=1, keepdims=True)
     first, second = first * (1.0 / all_channels), second * (1.0 / all_channels)
     for k in range(n_col):
         outs[k][...] = (inv_std * (grads[k] - first - normed[k] * second)).astype(BF16)
 
 
-def branch_kernel(pieces, n_col, hidden, *refs):
-    weights, refs = refs[: len(pieces)], refs[len(pieces) :]
-    outs, (whole, sems) = refs[:n_col], refs[n_col:]
-    copies = copy_pieces(pieces, weights, whole, sems)
-    channels = outs[0].shape[1]
-    for copy in copies:
-        copy.wait()
+def branch_kernel(out_slots, n_col, hidden, *refs):
+    n_out = len(out_slots) * n_col
+    out_refs, (*outs, whole) = refs[:n_out], refs[n_out:]
+    for j in range(n_col):
+        whole[out_slots[0][1][j]()] = sum(
+            jnp.dot(hidden[p], out_refs[p * n_col + j][...], preferred_element_type=F32)
+            for p in range(len(out_slots))
+        ).astype(BF16)
     for k in range(n_col):
-        outs[k][...] = jnp.dot(
-            hidden[...], whole[:, k * channels : (k + 1) * channels], preferred_element_type=F32
-        ).astype(BF16)
+        outs[k][...] = whole[k]
 
 
 def grad_sum_kernel(dims, n_col, *refs):
@@ -297,9 +287,10 @@
     emit_top(blocks, outs, *dims)
 
 
-def backward_conv_kernel(dims, n_top, n_side, grad, taps, upstream, *refs):
+def backward_conv_kernel(dims, n_top, n_side, n_terms, grad, taps, upstream, image, *refs):
     tops, columns, refs = refs[:n_top], refs[n_top : n_top + n_side], refs[n_top + n_side :]
-    out, pad, shifted = refs
+    terms, (out, output, pad, shifted) = refs[:n_terms], refs[n_terms:]
+    output[...] = (image[...].astype(F32) + sum(term[...].astype(F32) for term in terms)).astype(BF16)
     height, breadth = dims
     fill_padded(pad, grad, tops, columns, height, breadth)
 
@@ -325,7 +316,6 @@
 
 
 IN_VMEM = pl.BlockSpec(memory_space=pltpu.VMEM)
-ANYWHERE = pl.BlockSpec(memory_space=pl.ANY)
 
 
 def tie(x, *others):
@@ -378,15 +368,15 @@
         whole_out = lax.all_gather(w_out, "row", axis=0, tiled=True)
         whole_out = lax.all_to_all(whole_out, "col", 0, 1, tiled=True)
         whole_out = whole_out.reshape(hidden, n_col, channels)[:, order].reshape(hidden, -1)
-        none = (lambda: 0, lambda: 0)
-        return [whole_in], [none], [whole_out], [none]
-
-    share = hidden // n_sec
-
-    def place(row_bits, sec_bits):
-        block = lambda: ((lax.axis_index("row") ^ row_bits) ^ lax.axis_index("col")) * channels
-        part = (lambda: 0) if sec_bits is None else (lambda: (lax.axis_index("section") ^ sec_bits) * share)
-        return block, part
+        fixed = [functools.partial(int, k) for k in range(n_col)]
+        cut = [slice(k * channels, (k + 1) * channels) for k in range(n_col)]
+        return [whole_in[c] for c in cut], fixed, [whole_out[:, c] for c in cut], [(functools.partial(int, 0), fixed)]
+
+    def block(row_bits):
+        return lambda: (lax.axis_index("row") ^ row_bits) ^ lax.axis_index("col")
+
+    def part(sec_bits):
+        return lambda: lax.axis_index("section") ^ sec_bits
 
     core = bits_of(n_row)[:1]
     for bit in bits_of(n_sec):
@@ -406,9 +396,9 @@
         }
     return (
         list(got_in.values()),
-        [place(*k) for k in got_in],
-        list(got_out.values()),
-        [place(*k)[::-1] for k in got_out],
+        [block(r) for r, _ in got_in],
+        [got_out[r, p] for p in range(n_sec) for r in range(n_row)],
+        [(part(p), [block(r) for r in range(n_row)]) for p in range(n_sec)],
     )
 
 
@@ -492,23 +482,21 @@
     )
 
     product = 2 * cells * all_channels * hidden
-    weight = pltpu.VMEM((all_channels, hidden), BF16)
-    weight_t = pltpu.VMEM((hidden, all_channels), BF16)
     part = jax.ShapeDtypeStruct((cells, channels), BF16)
+    act_shape = (len(out_pieces), cells, hidden // len(out_pieces))
     *grads, act = call(
         "mlp",
-        20 * MIB,
+        24 * MIB,
         functools.partial(mlp_kernel, in_pieces, out_pieces, n_col),
-        [part] * n_col + [jax.ShapeDtypeStruct((cells, hidden), BF16)],
-        [IN_VMEM] * n_col + [ANYWHERE] * (len(in_refs) + len(out_refs)),
+        [part] * n_col + [jax.ShapeDtypeStruct(act_shape, BF16)],
+        [IN_VMEM] * (n_col + len(in_refs) + len(out_refs)),
         [
-            weight,
-            weight_t,
             pltpu.VMEM((n_col, cells, channels), F32),
-            pltpu.VMEM((cells, all_channels), BF16),
-            pltpu.VMEM((cells, hidden), BF16),
-            pltpu.SemaphoreType.DMA((len(in_refs),)),
-            pltpu.SemaphoreType.DMA((len(out_refs),)),
+            pltpu.VMEM((n_col, cells, channels), BF16),
+            pltpu.VMEM((n_col, cells, channels), BF16),
+            pltpu.VMEM((n_col, 8, channels), F32),
+            pltpu.VMEM((n_col, cells, channels), F32),
+            pltpu.VMEM(act_shape, BF16),
         ],
         flops=3 * product,
         transcendentals=2 * cells * hidden,
@@ -517,11 +505,11 @@
     act = tie(act, grads[1])
     branches = call(
         "branch",
-        8 * MIB,
+        12 * MIB,
         functools.partial(branch_kernel, out_pieces, n_col),
         [part] * n_col,
-        [IN_VMEM] + [ANYWHERE] * len(out_refs),
-        [weight_t, pltpu.SemaphoreType.DMA((len(out_refs),))],
+        [IN_VMEM] * (1 + len(out_refs)),
+        [pltpu.VMEM((n_col, cells, channels), BF16)],
         flops=product,
     )(act, *out_refs)
     mixed_grad, *sent = call(
@@ -535,17 +523,15 @@
     tops = meet(sent, "section", "grad_rows")
     branches = scatter_col(branches, "branch_sums", tops)
     columns = columns_of(mixed_grad, tops, "grad_columns")
-    image_grad = call(
+    image_grad, output = call(
         "backward_conv",
         8 * MIB,
-        functools.partial(backward_conv_kernel, dims, n_top, n_side),
-        jax.ShapeDtypeStruct((cells, channels), F32),
-        [IN_VMEM] * (3 + n_top + n_side),
+        functools.partial(backward_conv_kernel, dims, n_top, n_side, len(branches)),
+        [jax.ShapeDtypeStruct((cells, channels), F32), part],
+        [IN_VMEM] * (4 + n_top + n_side + len(branches)),
         padded,
         **conv_cost,
-    )(mixed_grad, conv_kernel, flat_up, *tops, *columns)
-    branches = tie(branches, image_grad)
-    output = (flat_image.astype(F32) + sum(b.astype(F32) for b in branches)).astype(BF16)
+    )(mixed_grad, conv_kernel, flat_up, flat_image, *tops, *columns, *branches)
     return output.reshape(image.shape), image_grad.reshape(image.shape)
 
 

time: 79.3 us -> 77.8 us (0.981)
  Pallas kernels: 8.39 us -> 7.29 us
    pallas_call x2, Pallas kernels: 4.86 us -> 3.66 us  [the longest x1 2.91 us: local(): call('mlp', 24 * MIB, functools.partial(mlp_kernel, in_pieces, out_pieces...]
  transfers between devices with their start and end apart: 26 -> 26, of which waited for: 14 -> 14; matrix products, arithmetic and copies ran while one was open for 0% -> 0% of each run, Pallas kernels for 6% -> 3%
where the time goes in v4:
time: 77.8 us; the launch traced here: 77.6 us
  starting transfers between devices  39.5 us (51%)
  waiting for transfers between devices  29.9 us (38%)
  Pallas kernels  7.29 us (9%)
  between operations  0.82 us (1%)
    ppermute x19, waiting for transfers between devices, swap(): return lax.ppermute(x, axis, [(i, i ^ bit) for i in range(count)])  22.5 us
    ppermute x19, starting transfers between devices, swap(): return lax.ppermute(x, axis, [(i, i ^ bit) for i in range(count)])  22.1 us
    ppermute x6, starting transfers between devices, meet(): lax.ppermute(strip, axis, pairs)  13.8 us
    ppermute x6, waiting for transfers between devices, meet(): lax.ppermute(strip, axis, pairs)  7.38 us
    ppermute x1, starting transfers between devices, weights_begin(): lax.ppermute(mine_out, ('row', 'col'), [(r * n_col + z, z * n_col + r) fo...  3.57 us
    pallas_call x1, Pallas kernels, local(): call('mlp', 24 * MIB, functools.partial(mlp_kernel, in_pieces, out_pieces...  2.91 us
    pallas_call x1, Pallas kernels, local(): call('backward_conv', 8 * MIB, functools.partial(backward_conv_kernel, di...  1.79 us
    pallas_call x1, Pallas kernels, local(): call('forward_conv', 8 * MIB, functools.partial(forward_conv_kernel, dims...  1.62 us
  transfers between devices with their start and end apart: 26, of which 14 were waited for; matrix products, arithmetic and copies ran while one was open for 0% of the time, Pallas kernels for 3%

profile of v4, /device:TPU:1, one launch (start us, length us, event | category | flops | bytes accessed | tf_op | source)
XLA Modules:
  0.0 77.6 jit_solution(17757578646392750716)
XLA Ops:
  0.6 0.0 copy-start
  0.6 0.1 collective-permute-start
  0.8 2.7 %collective-permute-start.7 = (bf16[256,1024]{1,0:T(8,128)(2,1)}, bf16[256,1024]{1,0:T(8,128)(2,1)S(1)}, u32[]{:S(2)}, u32[]{:S(2)}) collective-permute-start(bf16[256,1024]{1,0:T(8,128)(2,1)} %refs_4_.1), channel_id=1, source_target_pairs={{0,8},{4,12},{8,0},{12,4},{1,9},{5,13},{9,1},{13,5},{2,10},{6,14},... | collective-permute-start | bytes 1572872 | tf_op jit(solution)/shard_map/w_in_row/ppermute | solution.py:29
  3.5 0.0 copy-start.2
  3.5 3.6 %collective-permute-start.6 = (bf16[512,256]{1,0:T(8,128)(2,1)S(1)}, bf16[512,256]{1,0:T(8,128)(2,1)S(1)}, u32[]{:S(2)}, u32[]{:S(2)}) collective-permute-start(bf16[512,256]{1,0:T(8,128)(2,1)S(1)} %constant_dynamic-slice_fusion), channel_id=1, source_target_pairs={{0,0},{1,4},{2,8},{3,12},{4,1},{5,5},{6,9},{7,13},{8,2},{9,6},{10,... | collective-permute-start | bytes 786440 | tf_op jit(solution)/shard_map/w_out_transposed/ppermute | solution.py:337
  7.1 0.0 copy-start.5
  7.1 0.0 copy-start.3
  7.1 0.0 copy-start.4
  7.2 1.3 %collective-permute-start.1 = (bf16[48,256]{1,0:T(8,128)(2,1)S(1)}, bf16[48,256]{1,0:T(8,128)(2,1)S(1)}, u32[]{:S(2)}, u32[]{:S(2)}) collective-permute-start(bf16[48,256]{1,0:T(8,128)(2,1)S(1)} %constant_dynamic-slice_fusion.1), channel_id=1, source_target_pairs={{0,16},{16,0},{1,17},{17,1},{2,18},{18,2},{3,19},{19,3},{4,20},{20... | collective-permute-start | bytes 73736 | tf_op jit(solution)/shard_map/image_rows/ppermute | solution.py:44
  8.4 1.8 %collective-permute-done.1.refs_0_ = bf16[48,256]{1,0:T(8,128)(2,1)S(1)} collective-permute-done((bf16[48,256]{1,0:T(8,128)(2,1)S(1)}, bf16[48,256]{1,0:T(8,128)(2,1)S(1)}, u32[]{:S(2)}, u32[]{:S(2)}) %collective-permute-start.1) | collective-permute-done | bytes 24608 | tf_op jit(solution)/shard_map/image_rows/ppermute | solution.py:44
  10.2 0.1 image_columns.1
  10.3 0.1 collective-permute-start.2
  10.4 5.6 %collective-permute-start.3 = (bf16[80,256]{1,0:T(8,128)(2,1)S(1)}, bf16[80,256]{1,0:T(8,128)(2,1)S(1)}, u32[]{:S(2)}, u32[]{:S(2)}) collective-permute-start(bf16[80,256]{1,0:T(8,128)(2,1)S(1)} %get-tuple-element.28), channel_id=1, source_target_pairs={{4,8},{8,4},{5,9},{9,5},{6,10},{10,6},{7,11},{11,7},{20,24},{24,20... | collective-permute-start | bytes 122888 | tf_op jit(solution)/shard_map/image_columns/ppermute | solution.py:44
  16.0 0.0 collective-permute-done.refs_6_
  16.0 0.0 collective-permute-done.2.refs_1_
  16.0 3.9 %collective-permute-done.3.refs_2_ = bf16[80,256]{1,0:T(8,128)(2,1)S(1)} collective-permute-done((bf16[80,256]{1,0:T(8,128)(2,1)S(1)}, bf16[80,256]{1,0:T(8,128)(2,1)S(1)}, u32[]{:S(2)}, u32[]{:S(2)}) %collective-permute-start.3) | collective-permute-done | bytes 40992 | tf_op jit(solution)/shard_map/image_columns/ppermute | solution.py:44
  19.9 1.6 %forward_conv.1.refs_0_ = bf16[528,256]{1,0:T(8,128)(2,1)S(1)} custom-call(bf16[256,256]{1,0:T(8,128)(2,1)S(1)} %bitcast.7, f32[7,7,256]{2,1,0:T(8,128)S(1)} %copy-done.3, f32[1,256]{1,0:T(1,128)S(1)} %bitcast.11, bf16[256,256]{1,0:T(8,128)(2,1)S(1)} %bitcast.9, bf16[48,256]{1,0:T(8,128)(2,1)S(1)} %collective-permute-done.1.refs_0_, ...), custom_call_target="tpu_custom_call" | custom-call | flops 192675840 | bytes 1048576 | tf_op jit(solution)/shard_map/forward_conv/pallas_call | solution.py:467
  21.6 3.5 %collective-permute-start.5 = (bf16[528,256]{1,0:T(8,128)(2,1)S(1)}, bf16[528,256]{1,0:T(8,128)(2,1)S(1)}, u32[]{:S(2)}, u32[]{:S(2)}) collective-permute-start(bf16[528,256]{1,0:T(8,128)(2,1)S(1)} %forward_conv.1.refs_0_), channel_id=1, source_target_pairs={{0,2},{1,3},{2,0},{3,1},{4,6},{5,7},{6,4},{7,5},{8,10},{9,11},{10,... | collective-permute-start | bytes 811016 | tf_op jit(solution)/shard_map/features/col_2/ppermute | solution.py:29
  25.1 0.0 collective-permute-done.6.refs_8_.refs_0_
  25.1 0.0 collective-permute-done.7.refs_5_
  25.1 1.2 %collective-permute-start.9 = (bf16[512,256]{1,0:T(8,128)(2,1)S(1)}, bf16[512,256]{1,0:T(8,128)(2,1)S(1)}, u32[]{:S(2)}, u32[]{:S(2)}) collective-permute-start(bf16[512,256]{1,0:T(8,128)(2,1)S(1)} %collective-permute-done.6.refs_8_.refs_0_), channel_id=1, source_target_pairs={{0,16},{16,0},{1,17},{17,1},{2,18},{18,2},{3,19},{19,3},{4,20},{20... | collective-permute-start | bytes 786440 | tf_op jit(solution)/shard_map/w_out_section/ppermute | solution.py:29
  26.3 0.0 collective-permute-start.8
  26.3 1.0 %collective-permute-start.4 = (bf16[528,256]{1,0:T(8,128)(2,1)S(1)}, bf16[528,256]{1,0:T(8,128)(2,1)S(1)}, u32[]{:S(2)}, u32[]{:S(2)}) collective-permute-start(bf16[528,256]{1,0:T(8,128)(2,1)S(1)} %forward_conv.1.refs_0_), channel_id=1, source_target_pairs={{0,1},{1,0},{2,3},{3,2},{4,5},{5,4},{6,7},{7,6},{8,9},{9,8},{10,11... | collective-permute-start | bytes 811016 | tf_op jit(solution)/shard_map/features/col_1/ppermute | solution.py:29
  27.3 3.3 %collective-permute-done.9.refs_12_.refs_4_ = bf16[512,256]{1,0:T(8,128)(2,1)S(1)} collective-permute-done((bf16[512,256]{1,0:T(8,128)(2,1)S(1)}, bf16[512,256]{1,0:T(8,128)(2,1)S(1)}, u32[]{:S(2)}, u32[]{:S(2)}) %collective-permute-start.9) | collective-permute-done | bytes 262176 | tf_op jit(solution)/shard_map/w_out_section/ppermute | solution.py:29
  30.6 3.5 %collective-permute-done.8.refs_10_.refs_2_ = bf16[512,256]{1,0:T(8,128)(2,1)S(1)} collective-permute-done((bf16[512,256]{1,0:T(8,128)(2,1)S(1)}, bf16[512,256]{1,0:T(8,128)(2,1)S(1)}, u32[]{:S(2)}, u32[]{:S(2)}) %collective-permute-start.8) | collective-permute-done | bytes 262176 | tf_op jit(solution)/shard_map/w_out_row/ppermute | solution.py:29
  34.1 0.0 collective-permute-done.5.refs_2_
  34.1 1.5 %collective-permute-start.10 = (bf16[528,256]{1,0:T(8,128)(2,1)S(1)}, bf16[528,256]{1,0:T(8,128)(2,1)S(1)}, u32[]{:S(2)}, u32[]{:S(2)}) collective-permute-start(bf16[528,256]{1,0:T(8,128)(2,1)S(1)} %collective-permute-done.5.refs_2_), channel_id=1, source_target_pairs={{0,1},{1,0},{2,3},{3,2},{4,5},{5,4},{6,7},{7,6},{8,9},{9,8},{10,11... | collective-permute-start | bytes 811016 | tf_op jit(solution)/shard_map/features/col_1/ppermute | solution.py:29
  35.6 0.3 collective-permute-start.15
  35.8 0.1 collective-permute-done.4.refs_1_
  35.9 6.8 %collective-permute-done.10.refs_3_ = bf16[528,256]{1,0:T(8,128)(2,1)S(1)} collective-permute-done((bf16[528,256]{1,0:T(8,128)(2,1)S(1)}, bf16[528,256]{1,0:T(8,128)(2,1)S(1)}, u32[]{:S(2)}, u32[]{:S(2)}) %collective-permute-start.10) | collective-permute-done | bytes 270368 | tf_op jit(solution)/shard_map/features/col_1/ppermute | solution.py:29
  42.7 0.8 collective-permute-start.12
  43.4 0.0 collective-permute-start.11
  43.4 0.5 collective-permute-start.14
  44.0 0.0 collective-permute-start.13
  44.0 0.0 collective-permute-done.15.refs_14_.refs_6_
  44.0 0.6 collective-permute-done.12.refs_9_.refs_1_
  44.6 0.4 collective-permute-start.16
  45.0 0.4 collective-permute-done.11.refs_7_
  45.4 0.4 collective-permute-done.14.refs_13_.refs_5_
  45.7 0.4 collective-permute-done.13.refs_11_.refs_3_
  46.1 0.4 collective-permute-done.16.refs_15_.refs_7_
  46.5 2.9 %mlp.1 = (bf16[256,256]{1,0:T(8,128)(2,1)S(1)}, bf16[256,256]{1,0:T(8,128)(2,1)S(1)}, bf16[256,256]{1,0:T(8,128)(2,1)S(1)}, bf16[256,256]{1,0:T(8,128)(2,1)S(1)}, bf16[2,256,512]{2,1,0:T(8,128)(2,1)S(1)}) custom-call(bf16[528,256]{1,0:T(8,128)(2,1)S(1)} %forward_conv.1.refs_0_, bf16[528,256]{1,0:T(8,128)(2,1)S(1)} %collective-permute-done.4.refs_1_, ...), custom_call_target="tpu_custom_call" | custom-call | flops 1610612736 | bytes 1048576 | tf_op jit(solution)/shard_map/mlp/pallas_call | solution.py:487
  49.4 1.1 %collective-permute-start.17 = (bf16[256,256]{1,0:T(8,128)(2,1)S(1)}, bf16[256,256]{1,0:T(8,128)(2,1)S(1)}, u32[]{:S(2)}, u32[]{:S(2)}) collective-permute-start(bf16[256,256]{1,0:T(8,128)(2,1)S(1)} %get-tuple-element.34), channel_id=1, source_target_pairs={{0,1},{1,0},{2,3},{3,2},{4,5},{5,4},{6,7},{7,6},{8,9},{9,8},{10,11... | collective-permute-start | bytes 393224 | tf_op jit(solution)/shard_map/grad_sums/col_1/ppermute | solution.py:29
  50.5 1.1 %collective-permute-start.18 = (bf16[256,256]{1,0:T(8,128)(2,1)S(1)}, bf16[256,256]{1,0:T(8,128)(2,1)S(1)}, u32[]{:S(2)}, u32[]{:S(2)}) collective-permute-start(bf16[256,256]{1,0:T(8,128)(2,1)S(1)} %get-tuple-element.35), channel_id=1, source_target_pairs={{0,2},{1,3},{2,0},{3,1},{4,6},{5,7},{6,4},{7,5},{8,10},{9,11},{10,... | collective-permute-start | bytes 393224 | tf_op jit(solution)/shard_map/grad_sums/col_2/ppermute | solution.py:29
  51.6 1.4 %collective-permute-start.19 = (bf16[256,256]{1,0:T(8,128)(2,1)S(1)}, bf16[256,256]{1,0:T(8,128)(2,1)S(1)}, u32[]{:S(2)}, u32[]{:S(2)}) collective-permute-start(bf16[256,256]{1,0:T(8,128)(2,1)S(1)} %get-tuple-element.36), channel_id=1, source_target_pairs={{0,3},{1,2},{2,1},{3,0},{4,7},{5,6},{6,5},{7,4},{8,11},{9,10},{10,... | collective-permute-start | bytes 393224 | tf_op jit(solution)/shard_map/grad_sums/col_3/ppermute | solution.py:29
  53.0 1.2 %collective-permute-done.17.refs_1_ = bf16[256,256]{1,0:T(8,128)(2,1)S(1)} collective-permute-done((bf16[256,256]{1,0:T(8,128)(2,1)S(1)}, bf16[256,256]{1,0:T(8,128)(2,1)S(1)}, u32[]{:S(2)}, u32[]{:S(2)}) %collective-permute-start.17) | collective-permute-done | bytes 131104 | tf_op jit(solution)/shard_map/grad_sums/col_1/ppermute | solution.py:29
  54.2 0.7 branch.1
  54.9 1.1 %collective-permute-start.24 = (bf16[256,256]{1,0:T(8,128)(2,1)S(1)}, bf16[256,256]{1,0:T(8,128)(2,1)S(1)}, u32[]{:S(2)}, u32[]{:S(2)}) collective-permute-start(bf16[256,256]{1,0:T(8,128)(2,1)S(1)} %get-tuple-element.46), channel_id=1, source_target_pairs={{0,1},{1,0},{2,3},{3,2},{4,5},{5,4},{6,7},{7,6},{8,9},{9,8},{10,11... | collective-permute-start | bytes 393224 | tf_op jit(solution)/shard_map/branch_sums/col_1/ppermute | solution.py:29
  56.0 5.6 %collective-permute-done.18.refs_2_ = bf16[256,256]{1,0:T(8,128)(2,1)S(1)} collective-permute-done((bf16[256,256]{1,0:T(8,128)(2,1)S(1)}, bf16[256,256]{1,0:T(8,128)(2,1)S(1)}, u32[]{:S(2)}, u32[]{:S(2)}) %collective-permute-start.18) | collective-permute-done | bytes 131104 | tf_op jit(solution)/shard_map/grad_sums/col_2/ppermute | solution.py:29
  61.6 0.0 collective-permute-done.19.refs_3_
  61.6 0.1 grad_sum.1
  61.7 0.3 collective-permute-start.20
  62.0 3.1 %collective-permute-start.23 = (bf16[256,256]{1,0:T(8,128)(2,1)S(1)}, bf16[256,256]{1,0:T(8,128)(2,1)S(1)}, u32[]{:S(2)}, u32[]{:S(2)}) collective-permute-start(bf16[256,256]{1,0:T(8,128)(2,1)S(1)} %get-tuple-element.44), channel_id=1, source_target_pairs={{0,1},{1,0},{2,3},{3,2},{4,5},{5,4},{6,7},{7,6},{8,9},{9,8},{10,11... | collective-permute-start | bytes 393224 | tf_op jit(solution)/shard_map/branch_sums/col_1/ppermute | solution.py:29
  65.1 0.0 collective-permute-done.20.refs_0_
  65.1 0.0 collective-permute-done.24
  65.1 2.3 %collective-permute-start.25 = (bf16[256,256]{1,0:T(8,128)(2,1)S(1)}, bf16[256,256]{1,0:T(8,128)(2,1)S(1)}, u32[]{:S(2)}, u32[]{:S(2)}) collective-permute-start(bf16[256,256]{1,0:T(8,128)(2,1)S(1)} %add_convert_fusion), channel_id=1, source_target_pairs={{0,2},{1,3},{2,0},{3,1},{4,6},{5,7},{6,4},{7,5},{8,10},{9,11},{10,... | collective-permute-start | bytes 393224 | tf_op jit(solution)/shard_map/branch_sums/col_2/ppermute | solution.py:29
  67.5 0.1 grad_columns.1
  67.6 2.7 %collective-permute-start.21 = (bf16[80,256]{1,0:T(8,128)(2,1)S(1)}, bf16[80,256]{1,0:T(8,128)(2,1)S(1)}, u32[]{:S(2)}, u32[]{:S(2)}) collective-permute-start(bf16[80,256]{1,0:T(8,128)(2,1)S(1)} %get-tuple-element.39), channel_id=1, source_target_pairs={{0,4},{8,12},{4,0},{12,8},{1,5},{9,13},{5,1},{13,9},{2,6},{10,14},... | collective-permute-start | bytes 122888 | tf_op jit(solution)/shard_map/grad_columns/ppermute | solution.py:44
  70.3 3.9 %collective-permute-start.22 = (bf16[80,256]{1,0:T(8,128)(2,1)S(1)}, bf16[80,256]{1,0:T(8,128)(2,1)S(1)}, u32[]{:S(2)}, u32[]{:S(2)}) collective-permute-start(bf16[80,256]{1,0:T(8,128)(2,1)S(1)} %get-tuple-element.40), channel_id=1, source_target_pairs={{4,8},{8,4},{5,9},{9,5},{6,10},{10,6},{7,11},{11,7},{20,24},{24,20... | collective-permute-start | bytes 122888 | tf_op jit(solution)/shard_map/grad_columns/ppermute | solution.py:44
  74.2 0.0 collective-permute-done.21.refs_1_
  74.2 1.7 %collective-permute-done.22.refs_2_ = bf16[80,256]{1,0:T(8,128)(2,1)S(1)} collective-permute-done((bf16[80,256]{1,0:T(8,128)(2,1)S(1)}, bf16[80,256]{1,0:T(8,128)(2,1)S(1)}, u32[]{:S(2)}, u32[]{:S(2)}) %collective-permute-start.22) | collective-permute-done | bytes 40992 | tf_op jit(solution)/shard_map/grad_columns/ppermute | solution.py:44
  75.8 0.0 collective-permute-done.23.refs_4_
  75.8 0.0 collective-permute-done.25.refs_5_
  75.8 1.8 %backward_conv.1 = (f32[256,256]{1,0:T(8,128)}, bf16[256,256]{1,0:T(8,128)(2,1)}) custom-call(f32[256,256]{1,0:T(8,128)S(1)} %get-tuple-element.37.cells.grad, f32[7,7,256]{2,1,0:T(8,128)S(1)} %copy-done.3, bf16[256,256]{1,0:T(8,128)(2,1)S(1)} %bitcast.10, bf16[256,256]{1,0:T(8,128)(2,1)S(1)} %bitcast.8, ...), custom_call_target="tpu_custom_call" | custom-call | flops 192675840 | bytes 1048576 | tf_op jit(solution)/shard_map/backward_conv/pallas_call | solution.py:526
  (10 shorter events, 0.1 us)
Async XLA Ops:
  0.6 2.8 %copy-start = (bf16[1024,256]{1,0:T(8,128)(2,1)S(1)}, bf16[1024,256]{1,0:T(8,128)(2,1)}, u32[]{:S(2)}) copy-start(bf16[1024,256]{1,0:T(8,128)(2,1)} %param.10) | copy-start | bytes 1572868
  0.6 15.3 %collective-permute-start = (bf16[256,1024]{1,0:T(8,128)(2,1)}, bf16[256,1024]{1,0:T(8,128)(2,1)S(1)}, u32[]{:S(2)}, u32[]{:S(2)}) collective-permute-start(bf16[256,1024]{1,0:T(8,128)(2,1)} %refs_4_.1), channel_id=1, source_target_pairs={{0,4},{4,0},{8,12},{12,8},{1,5},{5,1},{9,13},{13,9},{2,6},{6,2},{1... | collective-permute-start | bytes 1572872 | tf_op jit(solution)/shard_map/w_in_core/ppermute | solution.py:29
  0.8 24.3 %collective-permute-start.7 = (bf16[256,1024]{1,0:T(8,128)(2,1)}, bf16[256,1024]{1,0:T(8,128)(2,1)S(1)}, u32[]{:S(2)}, u32[]{:S(2)}) collective-permute-start(bf16[256,1024]{1,0:T(8,128)(2,1)} %refs_4_.1), channel_id=1, source_target_pairs={{0,8},{4,12},{8,0},{12,4},{1,9},{5,13},{9,1},{13,5},{2,10},{6,14},... | collective-permute-start | bytes 1572872 | tf_op jit(solution)/shard_map/w_in_row/ppermute | solution.py:29
  3.5 3.6 %copy-start.1 = (bf16[16,16,256]{2,1,0:T(8,128)(2,1)S(1)}, bf16[16,16,256]{2,1,0:T(8,128)(2,1)}, u32[]{:S(2)}) copy-start(bf16[16,16,256]{2,1,0:T(8,128)(2,1)} %param.6) | copy-start | bytes 393220
  3.5 16.4 %copy-start.2 = (bf16[16,16,256]{2,1,0:T(8,128)(2,1)S(1)}, bf16[16,16,256]{2,1,0:T(8,128)(2,1)}, u32[]{:S(2)}) copy-start(bf16[16,16,256]{2,1,0:T(8,128)(2,1)} %param.11) | copy-start | bytes 393220
  3.5 21.6 %collective-permute-start.6 = (bf16[512,256]{1,0:T(8,128)(2,1)S(1)}, bf16[512,256]{1,0:T(8,128)(2,1)S(1)}, u32[]{:S(2)}, u32[]{:S(2)}) collective-permute-start(bf16[512,256]{1,0:T(8,128)(2,1)S(1)} %constant_dynamic-slice_fusion), channel_id=1, source_target_pairs={{0,0},{1,4},{2,8},{3,12},{4,1},{5,5},{6,9},{7,13},{8,2},{9,6},{10,... | collective-permute-start | bytes 786440 | tf_op jit(solution)/shard_map/w_out_transposed/ppermute | solution.py:337
  7.1 12.8 %copy-start.5 = (f32[256]{0:T(256)S(1)}, f32[256]{0:T(256)}, u32[]{:S(2)}) copy-start(f32[256]{0:T(256)} %param.8) | copy-start | bytes 3076
  7.1 12.8 %copy-start.3 = (f32[7,7,256]{2,1,0:T(8,128)S(1)}, f32[7,7,256]{2,1,0:T(8,128)}, u32[]{:S(2)}) copy-start(f32[7,7,256]{2,1,0:T(8,128)} %taps.3) | copy-start | bytes 150532
  7.1 39.3 %copy-start.4 = (bf16[256,1024]{1,0:T(8,128)(2,1)S(1)}, bf16[256,1024]{1,0:T(8,128)(2,1)}, u32[]{:S(2)}) copy-start(bf16[256,1024]{1,0:T(8,128)(2,1)} %refs_4_.1) | copy-start | bytes 1572868
  7.2 3.0 %collective-permute-start.1 = (bf16[48,256]{1,0:T(8,128)(2,1)S(1)}, bf16[48,256]{1,0:T(8,128)(2,1)S(1)}, u32[]{:S(2)}, u32[]{:S(2)}) collective-permute-start(bf16[48,256]{1,0:T(8,128)(2,1)S(1)} %constant_dynamic-slice_fusion.1), channel_id=1, source_target_pairs={{0,16},{16,0},{1,17},{17,1},{2,18},{18,2},{3,19},{19,3},{4,20},{20... | collective-permute-start | bytes 73736 | tf_op jit(solution)/shard_map/image_rows/ppermute | solution.py:44
  10.3 5.7 %collective-permute-start.2 = (bf16[80,256]{1,0:T(8,128)(2,1)S(1)}, bf16[80,256]{1,0:T(8,128)(2,1)S(1)}, u32[]{:S(2)}, u32[]{:S(2)}) collective-permute-start(bf16[80,256]{1,0:T(8,128)(2,1)S(1)} %get-tuple-element.27), channel_id=1, source_target_pairs={{0,4},{8,12},{4,0},{12,8},{1,5},{9,13},{5,1},{13,9},{2,6},{10,14},... | collective-permute-start | bytes 122888 | tf_op jit(solution)/shard_map/image_columns/ppermute | solution.py:44
  10.4 9.6 %collective-permute-start.3 = (bf16[80,256]{1,0:T(8,128)(2,1)S(1)}, bf16[80,256]{1,0:T(8,128)(2,1)S(1)}, u32[]{:S(2)}, u32[]{:S(2)}) collective-permute-start(bf16[80,256]{1,0:T(8,128)(2,1)S(1)} %get-tuple-element.28), channel_id=1, source_target_pairs={{4,8},{8,4},{5,9},{9,5},{6,10},{10,6},{7,11},{11,7},{20,24},{24,20... | collective-permute-start | bytes 122888 | tf_op jit(solution)/shard_map/image_columns/ppermute | solution.py:44
  21.6 12.5 %collective-permute-start.5 = (bf16[528,256]{1,0:T(8,128)(2,1)S(1)}, bf16[528,256]{1,0:T(8,128)(2,1)S(1)}, u32[]{:S(2)}, u32[]{:S(2)}) collective-permute-start(bf16[528,256]{1,0:T(8,128)(2,1)S(1)} %forward_conv.1.refs_0_), channel_id=1, source_target_pairs={{0,2},{1,3},{2,0},{3,1},{4,6},{5,7},{6,4},{7,5},{8,10},{9,11},{10,... | collective-permute-start | bytes 811016 | tf_op jit(solution)/shard_map/features/col_2/ppermute | solution.py:29
  25.1 5.5 %collective-permute-start.9 = (bf16[512,256]{1,0:T(8,128)(2,1)S(1)}, bf16[512,256]{1,0:T(8,128)(2,1)S(1)}, u32[]{:S(2)}, u32[]{:S(2)}) collective-permute-start(bf16[512,256]{1,0:T(8,128)(2,1)S(1)} %collective-permute-done.6.refs_8_.refs_0_), channel_id=1, source_target_pairs={{0,16},{16,0},{1,17},{17,1},{2,18},{18,2},{3,19},{19,3},{4,20},{20... | collective-permute-start | bytes 786440 | tf_op jit(solution)/shard_map/w_out_section/ppermute | solution.py:29
  26.3 7.8 %collective-permute-start.8 = (bf16[512,256]{1,0:T(8,128)(2,1)S(1)}, bf16[512,256]{1,0:T(8,128)(2,1)S(1)}, u32[]{:S(2)}, u32[]{:S(2)}) collective-permute-start(bf16[512,256]{1,0:T(8,128)(2,1)S(1)} %collective-permute-done.6.refs_8_.refs_0_), channel_id=1, source_target_pairs={{0,8},{4,12},{8,0},{12,4},{1,9},{5,13},{9,1},{13,5},{2,10},{6,14},... | collective-permute-start | bytes 786440 | tf_op jit(solution)/shard_map/w_out_row/ppermute | solution.py:29
  26.3 9.6 %collective-permute-start.4 = (bf16[528,256]{1,0:T(8,128)(2,1)S(1)}, bf16[528,256]{1,0:T(8,128)(2,1)S(1)}, u32[]{:S(2)}, u32[]{:S(2)}) collective-permute-start(bf16[528,256]{1,0:T(8,128)(2,1)S(1)} %forward_conv.1.refs_0_), channel_id=1, source_target_pairs={{0,1},{1,0},{2,3},{3,2},{4,5},{5,4},{6,7},{7,6},{8,9},{9,8},{10,11... | collective-permute-start | bytes 811016 | tf_op jit(solution)/shard_map/features/col_1/ppermute | solution.py:29
  34.1 8.6 %collective-permute-start.10 = (bf16[528,256]{1,0:T(8,128)(2,1)S(1)}, bf16[528,256]{1,0:T(8,128)(2,1)S(1)}, u32[]{:S(2)}, u32[]{:S(2)}) collective-permute-start(bf16[528,256]{1,0:T(8,128)(2,1)S(1)} %collective-permute-done.5.refs_2_), channel_id=1, source_target_pairs={{0,1},{1,0},{2,3},{3,2},{4,5},{5,4},{6,7},{7,6},{8,9},{9,8},{10,11... | collective-permute-start | bytes 811016 | tf_op jit(solution)/shard_map/features/col_1/ppermute | solution.py:29
  35.6 8.4 %collective-permute-start.15 = (bf16[512,256]{1,0:T(8,128)(2,1)S(1)}, bf16[512,256]{1,0:T(8,128)(2,1)S(1)}, u32[]{:S(2)}, u32[]{:S(2)}) collective-permute-start(bf16[512,256]{1,0:T(8,128)(2,1)S(1)} %collective-permute-done.8.refs_10_.refs_2_), channel_id=1, source_target_pairs={{0,16},{16,0},{1,17},{17,1},{2,18},{18,2},{3,19},{19,3},{4,20},{20... | collective-permute-start | bytes 786440 | tf_op jit(solution)/shard_map/w_out_both/ppermute | solution.py:29
  42.7 1.9 %collective-permute-start.12 = (bf16[512,256]{1,0:T(8,128)(2,1)S(1)}, bf16[512,256]{1,0:T(8,128)(2,1)S(1)}, u32[]{:S(2)}, u32[]{:S(2)}) collective-permute-start(bf16[512,256]{1,0:T(8,128)(2,1)S(1)} %collective-permute-done.6.refs_8_.refs_0_), channel_id=1, source_target_pairs={{0,4},{4,0},{8,12},{12,8},{1,5},{5,1},{9,13},{13,9},{2,6},{6,2},{1... | collective-permute-start | bytes 786440 | tf_op jit(solution)/shard_map/w_out_core_0_0/ppermute | solution.py:29
  43.4 1.9 %collective-permute-start.11 = (bf16[256,1024]{1,0:T(8,128)(2,1)S(1)}, bf16[256,1024]{1,0:T(8,128)(2,1)S(1)}, u32[]{:S(2)}, u32[]{:S(2)}) collective-permute-start(bf16[256,1024]{1,0:T(8,128)(2,1)S(1)} %collective-permute-done.7.refs_5_), channel_id=1, source_target_pairs={{0,4},{4,0},{8,12},{12,8},{1,5},{5,1},{9,13},{13,9},{2,6},{6,2},{1... | collective-permute-start | bytes 1572872 | tf_op jit(solution)/shard_map/w_in_core_2/ppermute | solution.py:29
  43.4 2.3 %collective-permute-start.14 = (bf16[512,256]{1,0:T(8,128)(2,1)S(1)}, bf16[512,256]{1,0:T(8,128)(2,1)S(1)}, u32[]{:S(2)}, u32[]{:S(2)}) collective-permute-start(bf16[512,256]{1,0:T(8,128)(2,1)S(1)} %collective-permute-done.9.refs_12_.refs_4_), channel_id=1, source_target_pairs={{0,4},{4,0},{8,12},{12,8},{1,5},{5,1},{9,13},{13,9},{2,6},{6,2},{1... | collective-permute-start | bytes 786440 | tf_op jit(solution)/shard_map/w_out_core_0_1/ppermute | solution.py:29
  44.0 2.2 %collective-permute-start.13 = (bf16[512,256]{1,0:T(8,128)(2,1)S(1)}, bf16[512,256]{1,0:T(8,128)(2,1)S(1)}, u32[]{:S(2)}, u32[]{:S(2)}) collective-permute-start(bf16[512,256]{1,0:T(8,128)(2,1)S(1)} %collective-permute-done.8.refs_10_.refs_2_), channel_id=1, source_target_pairs={{0,4},{4,0},{8,12},{12,8},{1,5},{5,1},{9,13},{13,9},{2,6},{6,2},{1... | collective-permute-start | bytes 786440 | tf_op jit(solution)/shard_map/w_out_core_2_0/ppermute | solution.py:29
  44.6 1.9 %collective-permute-start.16 = (bf16[512,256]{1,0:T(8,128)(2,1)S(1)}, bf16[512,256]{1,0:T(8,128)(2,1)S(1)}, u32[]{:S(2)}, u32[]{:S(2)}) collective-permute-start(bf16[512,256]{1,0:T(8,128)(2,1)S(1)} %collective-permute-done.15.refs_14_.refs_6_), channel_id=1, source_target_pairs={{0,4},{4,0},{8,12},{12,8},{1,5},{5,1},{9,13},{13,9},{2,6},{6,2},{1... | collective-permute-start | bytes 786440 | tf_op jit(solution)/shard_map/w_out_core_2_1/ppermute | solution.py:29
  49.4 4.8 %collective-permute-start.17 = (bf16[256,256]{1,0:T(8,128)(2,1)S(1)}, bf16[256,256]{1,0:T(8,128)(2,1)S(1)}, u32[]{:S(2)}, u32[]{:S(2)}) collective-permute-start(bf16[256,256]{1,0:T(8,128)(2,1)S(1)} %get-tuple-element.34), channel_id=1, source_target_pairs={{0,1},{1,0},{2,3},{3,2},{4,5},{5,4},{6,7},{7,6},{8,9},{9,8},{10,11... | collective-permute-start | bytes 393224 | tf_op jit(solution)/shard_map/grad_sums/col_1/ppermute | solution.py:29
  50.5 11.1 %collective-permute-start.18 = (bf16[256,256]{1,0:T(8,128)(2,1)S(1)}, bf16[256,256]{1,0:T(8,128)(2,1)S(1)}, u32[]{:S(2)}, u32[]{:S(2)}) collective-permute-start(bf16[256,256]{1,0:T(8,128)(2,1)S(1)} %get-tuple-element.35), channel_id=1, source_target_pairs={{0,2},{1,3},{2,0},{3,1},{4,6},{5,7},{6,4},{7,5},{8,10},{9,11},{10,... | collective-permute-start | bytes 393224 | tf_op jit(solution)/shard_map/grad_sums/col_2/ppermute | solution.py:29
  51.6 10.1 %collective-permute-start.19 = (bf16[256,256]{1,0:T(8,128)(2,1)S(1)}, bf16[256,256]{1,0:T(8,128)(2,1)S(1)}, u32[]{:S(2)}, u32[]{:S(2)}) collective-permute-start(bf16[256,256]{1,0:T(8,128)(2,1)S(1)} %get-tuple-element.36), channel_id=1, source_target_pairs={{0,3},{1,2},{2,1},{3,0},{4,7},{5,6},{6,5},{7,4},{8,11},{9,10},{10,... | collective-permute-start | bytes 393224 | tf_op jit(solution)/shard_map/grad_sums/col_3/ppermute | solution.py:29
  54.9 10.2 %collective-permute-start.24 = (bf16[256,256]{1,0:T(8,128)(2,1)S(1)}, bf16[256,256]{1,0:T(8,128)(2,1)S(1)}, u32[]{:S(2)}, u32[]{:S(2)}) collective-permute-start(bf16[256,256]{1,0:T(8,128)(2,1)S(1)} %get-tuple-element.46), channel_id=1, source_target_pairs={{0,1},{1,0},{2,3},{3,2},{4,5},{5,4},{6,7},{7,6},{8,9},{9,8},{10,11... | collective-permute-start | bytes 393224 | tf_op jit(solution)/shard_map/branch_sums/col_1/ppermute | solution.py:29
  61.7 3.4 %collective-permute-start.20 = (bf16[48,256]{1,0:T(8,128)(2,1)S(1)}, bf16[48,256]{1,0:T(8,128)(2,1)S(1)}, u32[]{:S(2)}, u32[]{:S(2)}) collective-permute-start(bf16[48,256]{1,0:T(8,128)(2,1)S(1)} %get-tuple-element.38), channel_id=1, source_target_pairs={{0,16},{16,0},{1,17},{17,1},{2,18},{18,2},{3,19},{19,3},{4,20},{20... | collective-permute-start | bytes 73736 | tf_op jit(solution)/shard_map/grad_rows/ppermute | solution.py:44
  62.0 13.8 %collective-permute-start.23 = (bf16[256,256]{1,0:T(8,128)(2,1)S(1)}, bf16[256,256]{1,0:T(8,128)(2,1)S(1)}, u32[]{:S(2)}, u32[]{:S(2)}) collective-permute-start(bf16[256,256]{1,0:T(8,128)(2,1)S(1)} %get-tuple-element.44), channel_id=1, source_target_pairs={{0,1},{1,0},{2,3},{3,2},{4,5},{5,4},{6,7},{7,6},{8,9},{9,8},{10,11... | collective-permute-start | bytes 393224 | tf_op jit(solution)/shard_map/branch_sums/col_1/ppermute | solution.py:29
  65.1 10.7 %collective-permute-start.25 = (bf16[256,256]{1,0:T(8,128)(2,1)S(1)}, bf16[256,256]{1,0:T(8,128)(2,1)S(1)}, u32[]{:S(2)}, u32[]{:S(2)}) collective-permute-start(bf16[256,256]{1,0:T(8,128)(2,1)S(1)} %add_convert_fusion), channel_id=1, source_target_pairs={{0,2},{1,3},{2,0},{3,1},{4,6},{5,7},{6,4},{7,5},{8,10},{9,11},{10,... | collective-permute-start | bytes 393224 | tf_op jit(solution)/shard_map/branch_sums/col_2/ppermute | solution.py:29
  67.6 6.6 %collective-permute-start.21 = (bf16[80,256]{1,0:T(8,128)(2,1)S(1)}, bf16[80,256]{1,0:T(8,128)(2,1)S(1)}, u32[]{:S(2)}, u32[]{:S(2)}) collective-permute-start(bf16[80,256]{1,0:T(8,128)(2,1)S(1)} %get-tuple-element.39), channel_id=1, source_target_pairs={{0,4},{8,12},{4,0},{12,8},{1,5},{9,13},{5,1},{13,9},{2,6},{10,14},... | collective-permute-start | bytes 122888 | tf_op jit(solution)/shard_map/grad_columns/ppermute | solution.py:44
  70.3 5.6 %collective-permute-start.22 = (bf16[80,256]{1,0:T(8,128)(2,1)S(1)}, bf16[80,256]{1,0:T(8,128)(2,1)S(1)}, u32[]{:S(2)}, u32[]{:S(2)}) collective-permute-start(bf16[80,256]{1,0:T(8,128)(2,1)S(1)} %get-tuple-element.40), channel_id=1, source_target_pairs={{4,8},{8,4},{5,9},{9,5},{6,10},{10,6},{7,11},{11,7},{20,24},{24,20... | collective-permute-start | bytes 122888 | tf_op jit(solution)/shard_map/grad_columns/ppermute | solution.py:44

commit v5 on v4

--- a/solution.py
+++ b/solution.py
@@ -142,12 +142,17 @@
                 start = i * width + LEFT - MARGIN + b
                 shifted[b, i * breadth : (i + 1) * breadth, :] = pad[lane, start : start + breadth, :]
         for top in range(0, height, step):
-            total = jnp.zeros((step * breadth, 128), F32)
-            for a in range(KERNEL):
-                for b in range(KERNEL):
+            totals = [jnp.zeros((breadth, 128), F32) for _ in range(step)]
+            for b in range(KERNEL):
+                rows = [
+                    shifted[b, (top + i) * breadth : (top + i + 1) * breadth, :]
+                    for i in range(step + 2 * MARGIN)
+                ]
+                for a in range(KERNEL):
                     p, q = (KERNEL - 1 - a, KERNEL - 1 - b) if flip else (a, b)
-                    first = (top + a) * breadth
-                    total += shifted[b, first : first + step * breadth, :] * taps[p, q, lanes][None, :]
+                    tap = taps[p, q, lanes][None, :]
+                    totals = [total + rows[i + a] * tap for i, total in enumerate(totals)]
+            total = jnp.concatenate(totals, axis=0)
             store(slice(top * breadth, (top + step) * breadth), lanes, total)
 
 
@@ -191,7 +196,8 @@
 
 def mlp_kernel(in_slots, out_slots, n_col, *refs):
     messages, refs = refs[:n_col], refs[n_col:]
-    in_refs, refs = refs[: len(in_slots)], refs[len(in_slots) :]
+    n_in = sum(len(indices) for _, indices in in_slots)
+    in_refs, refs = refs[:n_in], refs[n_in:]
     n_out = len(out_slots) * n_col
     out_refs, refs = refs[:n_out], refs[n_out:]
     outs, refs = refs[:n_col], refs[n_col:]
@@ -222,17 +228,23 @@
         scaled[k] = (value * gains[k][:1, :]).astype(BF16)
     share = act_grad.shape[2]
     tile = min(256, share)
-    slots = [slot() for slot in in_slots]
+    slots = [slot() for slot, _ in in_slots]
     places = []
+
+    def w_in_columns(j, p, start, size):
+        indices = in_slots[j][1]
+        if len(indices) > 1:
+            return in_refs[indices[p]][:, start : start + size]
+        return in_refs[indices[0]][:, pl.ds(pl.multiple_of(places[p] + start, size), size)]
+
     for p, (part, blocks) in enumerate(out_slots):
         blocks = [block() for block in blocks]
         place = part() * share
         places.append(place)
         for start in range(0, share, tile):
-            columns = pl.ds(pl.multiple_of(place + start, tile), tile)
             preact = sum(
-                jnp.dot(scaled[slot], ref[:, columns], preferred_element_type=F32)
-                for slot, ref in zip(slots, in_refs)
+                jnp.dot(scaled[slot], w_in_columns(j, p, start, tile), preferred_element_type=F32)
+                for j, slot in enumerate(slots)
             )
             hidden_grad = sum(
                 lax.dot_general(
@@ -248,15 +260,12 @@
             slope = phi + preact * jnp.exp(-0.5 * preact * preact) * (1.0 / math.sqrt(2.0 * math.pi))
             act_grad[p, :, start : start + tile] = (hidden_grad * slope).astype(BF16)
     first, second = jnp.zeros((cells, 1), F32), jnp.zeros((cells, 1), F32)
-    for slot, ref in zip(slots, in_refs):
+    for j, slot in enumerate(slots):
         grad = sum(
             lax.dot_general(
-                act_grad[p],
-                ref[:, pl.ds(pl.multiple_of(place, share), share)],
-                (((1,), (1,)), ((), ())),
-                preferred_element_type=F32,
+                act_grad[p], w_in_columns(j, p, 0, share), (((1,), (1,)), ((), ())), preferred_element_type=F32
             )
-            for p, place in enumerate(places)
+            for p in range(len(places))
         ) * gains[slot][:1, :]
         grads[slot] = grad
         first += jnp.sum(grad, axis=1, keepdims=True)
@@ -327,6 +336,16 @@
     return n_row == n_col and not n_row & (n_row - 1) and not n_sec & (n_sec - 1)
 
 
+def far_rows(w_in, p, *others):
+    share = w_in.shape[1] // lax.axis_size("section")
+    mine = lax.dynamic_slice_in_dim(w_in, (lax.axis_index("section") ^ p) * share, share, 1)
+    got = {(0, p): tie(mine, *others) if others else mine}
+    for bit in bits_of(lax.axis_size("row"))[1:]:
+        got |= {(r ^ bit, p): swap(x, "row", bit, f"w_in_row_{p}") for (r, p), x in got.items()}
+    del got[0, p]
+    return got
+
+
 def weights_begin(w_in, w_out):
     n_sec, n_row, n_col = (lax.axis_size(a) for a in ("section", "row", "col"))
     if not exchangeable():
@@ -337,11 +356,9 @@
         mine_out = lax.ppermute(
             mine_out,
             ("row", "col"),
-            [(r * n_col + z, z * n_col + r) for r in range(n_row) for z in range(n_col)],
+            [(r * n_col + z, (z ^ (n_row // 2)) * n_col + r) for r in range(n_row) for z in range(n_col)],
         )
-    early = {(0, None): w_in}
-    for bit in bits_of(n_row)[1:]:
-        early |= {(r ^ bit, None): swap(x, "row", bit, "w_in_row") for (r, _), x in early.items()}
+    early = far_rows(w_in, 0)
     return mine_out, early, [swap(w_in, "row", bit, "w_in_core") for bit in bits_of(n_row)[:1]]
 
 
@@ -358,7 +375,7 @@
     return got, list(got.values())
 
 
-def weights_finish(w_in, w_out, got_out, got_in, core_in, messages):
+def weights_finish(w_in, w_out, got_out, got_in, core_in, rows_done, messages):
     n_sec, n_row, n_col = (lax.axis_size(a) for a in ("section", "row", "col"))
     channels, hidden = w_in.shape[0] * n_row // n_col, w_in.shape[1]
     if not exchangeable():
@@ -370,7 +387,7 @@
         whole_out = whole_out.reshape(hidden, n_col, channels)[:, order].reshape(hidden, -1)
         fixed = [functools.partial(int, k) for k in range(n_col)]
         cut = [slice(k * channels, (k + 1) * channels) for k in range(n_col)]
-        return [whole_in[c] for c in cut], fixed, [whole_out[:, c] for c in cut], [(functools.partial(int, 0), fixed)]
+        return [whole_in[c] for c in cut], [(f, [k]) for k, f in enumerate(fixed)], [whole_out[:, c] for c in cut], [(functools.partial(int, 0), fixed)]
 
     def block(row_bits):
         return lambda: (lax.axis_index("row") ^ row_bits) ^ lax.axis_index("col")
@@ -383,9 +400,12 @@
         got_out |= {
             (r, s ^ bit): swap(x, "section", bit, "w_out_both") for (r, s), x in got_out.items() if r and s < bit
         }
+    for p in range(1, n_sec):
+        got_in |= far_rows(w_in, p, rows_done)
+    got_in[0, None] = w_in
     for bit in core:
         got_in |= {
-            (r ^ bit, s): core_in[0] if r == 0 else swap(x, "row", bit, f"w_in_core_{r}")
+            (r ^ bit, s): core_in[0] if r == 0 else swap(x, "row", bit, f"w_in_core_{r}_{s}")
             for (r, s), x in got_in.items()
         }
         gate = swap(tie(got_out[0, 0], messages), "row", bit, "w_out_core_0_0")
@@ -394,11 +414,14 @@
             for (r, s), x in got_out.items()
             if r or s
         }
+    keys = list(got_in)
+    whole = [(block(r), [n]) for n, (r, p) in enumerate(keys) if p is None]
+    cut = [(block(r), [keys.index((r, p)) for p in range(n_sec)]) for r, p in keys if p == 0]
     return (
         list(got_in.values()),
-        [block(r) for r, _ in got_in],
+        whole + cut,
         [got_out[r, p] for p in range(n_sec) for r in range(n_row)],
-        [(part(p), [block(r) for r in range(n_row)]) for p in range(n_sec)],
+        [(part(p), [block(r ^ (n_row // 2)) for r in range(n_row)]) for p in range(n_sec)],
     )
 
 
@@ -436,7 +459,9 @@
         got = {0: part}
         with jax.named_scope(name):
             for bit in reversed(bits_of(n_col)):
-                got |= {k ^ bit: swap(tie(x, others) if k else x, "col", bit) for k, x in got.items()}
+                own = swap(part, "col", bit)
+                got |= {k ^ bit: swap(tie(x, others, own), "col", bit) for k, x in got.items() if k}
+                got[bit] = own
         return [got[k] for k in range(n_col)]
 
     def scatter_col(parts, name, others):
@@ -478,7 +503,7 @@
     got_out, rows_done = weights_far(mine_out, [message, early])
     messages = gather_col(message, "features", rows_done)
     in_refs, in_pieces, out_refs, out_pieces = weights_finish(
-        w_in, w_out, got_out, early_in, core_in, messages
+        w_in, w_out, got_out, early_in, core_in, rows_done, messages
     )
 
     product = 2 * cells * all_channels * hidden
@@ -502,7 +527,7 @@
         transcendentals=2 * cells * hidden,
     )(*messages, *in_refs, *out_refs)
     grads = to_col(grads, "grad_sums")
-    act = tie(act, grads[1])
+    act = tie(act, grads[2])
     branches = call(
         "branch",
         12 * MIB,

time: 77.8 us -> 74.4 us (0.956)
  starting transfers between devices: 39.5 us -> 32 us
  waiting for transfers between devices: 29.9 us -> 32.4 us
  local copies, waits for them, and re-layouts: 0.07 us -> 1.65 us
    ppermute x6, starting transfers between devices: 13.8 us -> 8.51 us  [meet(): lax.ppermute(strip, axis, pairs)]
    ppermute x19 -> x21, starting transfers between devices: 22.1 us -> 19.8 us  [swap(): return lax.ppermute(x, axis, [(i, i ^ bit) for i in range(count)])]
    ppermute x6, waiting for transfers between devices: 7.38 us -> 9.13 us  [meet(): lax.ppermute(strip, axis, pairs)]
    unnamed x12, local copies, waits for them, and re-layouts: 0.04 us -> 1.6 us
    ppermute x19 -> x21, waiting for transfers between devices: 22.5 us -> 23.2 us  [swap(): return lax.ppermute(x, axis, [(i, i ^ bit) for i in range(count)])]
  transfers between devices with their start and end apart: 26 -> 28, of which waited for: 14 -> 14; matrix products, arithmetic and copies ran while one was open for 0% -> 0% of each run, Pallas kernels for 3% -> 4%
where the time goes in v5:
time: 74.4 us; the launch traced here: 74.2 us
  waiting for transfers between devices  32.4 us (44%)
  starting transfers between devices  32 us (43%)
  Pallas kernels  7.42 us (10%)
  local copies, waits for them, and re-layouts  1.65 us (2%)
  between operations  0.78 us (1%)
    ppermute x21, waiting for transfers between devices, swap(): return lax.ppermute(x, axis, [(i, i ^ bit) for i in range(count)])  23.2 us
    ppermute x21, starting transfers between devices, swap(): return lax.ppermute(x, axis, [(i, i ^ bit) for i in range(count)])  19.8 us
    ppermute x6, waiting for transfers between devices, meet(): lax.ppermute(strip, axis, pairs)  9.13 us
    ppermute x6, starting transfers between devices, meet(): lax.ppermute(strip, axis, pairs)  8.51 us
    ppermute x1, starting transfers between devices, weights_begin(): lax.ppermute(mine_out, ('row', 'col'), [(r * n_col + z, (z ^ n_row // 2)...  3.69 us
    pallas_call x1, Pallas kernels, local(): call('mlp', 24 * MIB, functools.partial(mlp_kernel, in_pieces, out_pieces...  2.83 us
    pallas_call x1, Pallas kernels, local(): call('forward_conv', 8 * MIB, functools.partial(forward_conv_kernel, dims...  1.84 us
    pallas_call x1, Pallas kernels, local(): call('backward_conv', 8 * MIB, functools.partial(backward_conv_kernel, di...  1.79 us
  transfers between devices with their start and end apart: 28, of which 14 were waited for; matrix products, arithmetic and copies ran while one was open for 0% of the time, Pallas kernels for 4%

profile of v5, /device:TPU:1, one launch (start us, length us, event | category | flops | bytes accessed | tf_op | source)
XLA Modules:
  0.0 74.2 jit_solution(8537824569591720383)
XLA Ops:
  0.6 0.0 copy-start
  0.7 0.1 collective-permute-start
  0.8 0.9 %copy-done = bf16[1024,256]{1,0:T(8,128)(2,1)S(1)} copy-done((bf16[1024,256]{1,0:T(8,128)(2,1)S(1)}, bf16[1024,256]{1,0:T(8,128)(2,1)}, u32[]{:S(2)}) %copy-start) | copy-done | bytes 524312
  1.7 3.7 %collective-permute-start.6 = (bf16[512,256]{1,0:T(8,128)(2,1)S(1)}, bf16[512,256]{1,0:T(8,128)(2,1)S(1)}, u32[]{:S(2)}, u32[]{:S(2)}) collective-permute-start(bf16[512,256]{1,0:T(8,128)(2,1)S(1)} %constant_dynamic-slice_fusion.2), channel_id=1, source_target_pairs={{0,8},{1,12},{2,0},{3,4},{4,9},{5,13},{6,1},{7,5},{8,10},{9,14},{1... | collective-permute-start | bytes 786440 | tf_op jit(solution)/shard_map/w_out_transposed/ppermute | solution.py:356
  5.4 0.0 copy-start.3
  5.5 2.4 %collective-permute-start.7 = (bf16[256,512]{1,0:T(8,128)(2,1)S(1)}, bf16[256,512]{1,0:T(8,128)(2,1)S(1)}, u32[]{:S(2)}, u32[]{:S(2)}) collective-permute-start(bf16[256,512]{1,0:T(8,128)(2,1)S(1)} %get-tuple-element.53), channel_id=1, source_target_pairs={{0,8},{4,12},{8,0},{12,4},{1,9},{5,13},{9,1},{13,5},{2,10},{6,14},... | collective-permute-start | bytes 786440 | tf_op jit(solution)/shard_map/w_in_row_0/ppermute | solution.py:29
  7.8 1.3 %collective-permute-start.1 = (bf16[48,256]{1,0:T(8,128)(2,1)S(1)}, bf16[48,256]{1,0:T(8,128)(2,1)S(1)}, u32[]{:S(2)}, u32[]{:S(2)}) collective-permute-start(bf16[48,256]{1,0:T(8,128)(2,1)S(1)} %constant_dynamic-slice_fusion.3), channel_id=1, source_target_pairs={{0,16},{16,0},{1,17},{17,1},{2,18},{18,2},{3,19},{19,3},{4,20},{20... | collective-permute-start | bytes 73736 | tf_op jit(solution)/shard_map/image_rows/ppermute | solution.py:44
  9.1 1.9 %collective-permute-done.1.refs_0_ = bf16[48,256]{1,0:T(8,128)(2,1)S(1)} collective-permute-done((bf16[48,256]{1,0:T(8,128)(2,1)S(1)}, bf16[48,256]{1,0:T(8,128)(2,1)S(1)}, u32[]{:S(2)}, u32[]{:S(2)}) %collective-permute-start.1) | collective-permute-done | bytes 24608 | tf_op jit(solution)/shard_map/image_rows/ppermute | solution.py:44
  11.0 0.1 image_columns.1
  11.1 0.6 collective-permute-start.2
  11.7 2.5 %collective-permute-start.3 = (bf16[80,256]{1,0:T(8,128)(2,1)S(1)}, bf16[80,256]{1,0:T(8,128)(2,1)S(1)}, u32[]{:S(2)}, u32[]{:S(2)}) collective-permute-start(bf16[80,256]{1,0:T(8,128)(2,1)S(1)} %get-tuple-element.29), channel_id=1, source_target_pairs={{4,8},{8,4},{5,9},{9,5},{6,10},{10,6},{7,11},{11,7},{20,24},{24,20... | collective-permute-start | bytes 122888 | tf_op jit(solution)/shard_map/image_columns/ppermute | solution.py:44
  14.1 0.0 collective-permute-done.refs_9_
  14.1 0.0 collective-permute-done.2.refs_1_
  14.2 3.1 %collective-permute-done.3.refs_2_ = bf16[80,256]{1,0:T(8,128)(2,1)S(1)} collective-permute-done((bf16[80,256]{1,0:T(8,128)(2,1)S(1)}, bf16[80,256]{1,0:T(8,128)(2,1)S(1)}, u32[]{:S(2)}, u32[]{:S(2)}) %collective-permute-start.3) | collective-permute-done | bytes 40992 | tf_op jit(solution)/shard_map/image_columns/ppermute | solution.py:44
  17.3 0.7 copy-done.5
  18.0 1.8 %forward_conv.1.refs_0_ = bf16[528,256]{1,0:T(8,128)(2,1)S(1)} custom-call(bf16[256,256]{1,0:T(8,128)(2,1)S(1)} %bitcast.7, f32[7,7,256]{2,1,0:T(8,128)S(1)} %copy-done.4, f32[1,256]{1,0:T(1,128)S(1)} %bitcast.11, bf16[256,256]{1,0:T(8,128)(2,1)S(1)} %bitcast.9, bf16[48,256]{1,0:T(8,128)(2,1)S(1)} %collective-permute-done.1.refs_0_, ...), custom_call_target="tpu_custom_call" | custom-call | flops 192675840 | bytes 1048576 | tf_op jit(solution)/shard_map/forward_conv/pallas_call | solution.py:492
  19.8 3.2 %collective-permute-start.5 = (bf16[528,256]{1,0:T(8,128)(2,1)S(1)}, bf16[528,256]{1,0:T(8,128)(2,1)S(1)}, u32[]{:S(2)}, u32[]{:S(2)}) collective-permute-start(bf16[528,256]{1,0:T(8,128)(2,1)S(1)} %forward_conv.1.refs_0_), channel_id=1, source_target_pairs={{0,2},{1,3},{2,0},{3,1},{4,6},{5,7},{6,4},{7,5},{8,10},{9,11},{10,... | collective-permute-start | bytes 811016 | tf_op jit(solution)/shard_map/features/col_2/ppermute | solution.py:29
  23.0 0.0 collective-permute-start.4
  23.0 0.0 collective-permute-done.6.refs_10_.refs_0_
  23.0 0.0 collective-permute-done.7.refs_4_
  23.0 1.3 %collective-permute-start.9 = (bf16[512,256]{1,0:T(8,128)(2,1)S(1)}, bf16[512,256]{1,0:T(8,128)(2,1)S(1)}, u32[]{:S(2)}, u32[]{:S(2)}) collective-permute-start(bf16[512,256]{1,0:T(8,128)(2,1)S(1)} %collective-permute-done.6.refs_10_.refs_0_), channel_id=1, source_target_pairs={{0,16},{16,0},{1,17},{17,1},{2,18},{18,2},{3,19},{19,3},{4,20},{20... | collective-permute-start | bytes 786440 | tf_op jit(solution)/shard_map/w_out_section/ppermute | solution.py:29
  24.2 0.0 collective-permute-start.8
  24.3 4.3 %collective-permute-done.9.refs_14_.refs_4_ = bf16[512,256]{1,0:T(8,128)(2,1)S(1)} collective-permute-done((bf16[512,256]{1,0:T(8,128)(2,1)S(1)}, bf16[512,256]{1,0:T(8,128)(2,1)S(1)}, u32[]{:S(2)}, u32[]{:S(2)}) %collective-permute-start.9) | collective-permute-done | bytes 262176 | tf_op jit(solution)/shard_map/w_out_section/ppermute | solution.py:29
  28.6 2.7 %collective-permute-done.8.refs_12_.refs_2_ = bf16[512,256]{1,0:T(8,128)(2,1)S(1)} collective-permute-done((bf16[512,256]{1,0:T(8,128)(2,1)S(1)}, bf16[512,256]{1,0:T(8,128)(2,1)S(1)}, u32[]{:S(2)}, u32[]{:S(2)}) %collective-permute-start.8) | collective-permute-done | bytes 262176 | tf_op jit(solution)/shard_map/w_out_row/ppermute | solution.py:29
  31.2 0.0 collective-permute-done.5.refs_2_
  31.2 0.3 collective-permute-done.4.refs_1_
  31.5 1.4 %collective-permute-start.10 = (bf16[528,256]{1,0:T(8,128)(2,1)S(1)}, bf16[528,256]{1,0:T(8,128)(2,1)S(1)}, u32[]{:S(2)}, u32[]{:S(2)}) collective-permute-start(bf16[528,256]{1,0:T(8,128)(2,1)S(1)} %collective-permute-done.5.refs_2_), channel_id=1, source_target_pairs={{0,1},{1,0},{2,3},{3,2},{4,5},{5,4},{6,7},{7,6},{8,9},{9,8},{10,11... | collective-permute-start | bytes 811016 | tf_op jit(solution)/shard_map/features/col_1/ppermute | solution.py:29
  32.9 0.1 collective-permute-start.11
  33.0 0.3 collective-permute-start.17
  33.3 6.7 %collective-permute-done.10.refs_3_ = bf16[528,256]{1,0:T(8,128)(2,1)S(1)} collective-permute-done((bf16[528,256]{1,0:T(8,128)(2,1)S(1)}, bf16[528,256]{1,0:T(8,128)(2,1)S(1)}, u32[]{:S(2)}, u32[]{:S(2)}) %collective-permute-start.10) | collective-permute-done | bytes 270368 | tf_op jit(solution)/shard_map/features/col_1/ppermute | solution.py:29
  39.9 0.5 collective-permute-start.14
  40.4 0.1 collective-permute-start.12
  40.5 0.5 collective-permute-start.16
  40.9 0.0 collective-permute-done.11.refs_5_
  40.9 0.7 collective-permute-start.15
  41.6 0.0 collective-permute-done.17.refs_16_.refs_6_
  41.6 0.1 collective-permute-start.13
  41.8 0.0 collective-permute-done.14.refs_11_.refs_1_
  41.8 0.4 collective-permute-start.18
  42.1 0.0 collective-permute-done.12.refs_7_
  42.1 0.2 collective-permute-done.16.refs_15_.refs_5_
  42.3 0.5 collective-permute-done.15.refs_13_.refs_3_
  42.8 0.4 collective-permute-done.13.refs_8_
  43.2 0.4 collective-permute-done.18.refs_17_.refs_7_
  43.5 2.8 %mlp.1 = (bf16[256,256]{1,0:T(8,128)(2,1)S(1)}, bf16[256,256]{1,0:T(8,128)(2,1)S(1)}, bf16[256,256]{1,0:T(8,128)(2,1)S(1)}, bf16[256,256]{1,0:T(8,128)(2,1)S(1)}, bf16[2,256,512]{2,1,0:T(8,128)(2,1)S(1)}) custom-call(bf16[528,256]{1,0:T(8,128)(2,1)S(1)} %forward_conv.1.refs_0_, bf16[528,256]{1,0:T(8,128)(2,1)S(1)} %collective-permute-done.4.refs_1_, ...), custom_call_target="tpu_custom_call" | custom-call | flops 1610612736 | bytes 1048576 | tf_op jit(solution)/shard_map/mlp/pallas_call | solution.py:512
  46.4 1.0 %collective-permute-start.20 = (bf16[256,256]{1,0:T(8,128)(2,1)S(1)}, bf16[256,256]{1,0:T(8,128)(2,1)S(1)}, u32[]{:S(2)}, u32[]{:S(2)}) collective-permute-start(bf16[256,256]{1,0:T(8,128)(2,1)S(1)} %get-tuple-element.37), channel_id=1, source_target_pairs={{0,2},{1,3},{2,0},{3,1},{4,6},{5,7},{6,4},{7,5},{8,10},{9,11},{10,... | collective-permute-start | bytes 393224 | tf_op jit(solution)/shard_map/grad_sums/col_2/ppermute | solution.py:29
  47.4 1.3 %collective-permute-start.19 = (bf16[256,256]{1,0:T(8,128)(2,1)S(1)}, bf16[256,256]{1,0:T(8,128)(2,1)S(1)}, u32[]{:S(2)}, u32[]{:S(2)}) collective-permute-start(bf16[256,256]{1,0:T(8,128)(2,1)S(1)} %get-tuple-element.36), channel_id=1, source_target_pairs={{0,1},{1,0},{2,3},{3,2},{4,5},{5,4},{6,7},{7,6},{8,9},{9,8},{10,11... | collective-permute-start | bytes 393224 | tf_op jit(solution)/shard_map/grad_sums/col_1/ppermute | solution.py:29
  48.7 1.3 %collective-permute-start.21 = (bf16[256,256]{1,0:T(8,128)(2,1)S(1)}, bf16[256,256]{1,0:T(8,128)(2,1)S(1)}, u32[]{:S(2)}, u32[]{:S(2)}) collective-permute-start(bf16[256,256]{1,0:T(8,128)(2,1)S(1)} %get-tuple-element.38), channel_id=1, source_target_pairs={{0,3},{1,2},{2,1},{3,0},{4,7},{5,6},{6,5},{7,4},{8,11},{9,10},{10,... | collective-permute-start | bytes 393224 | tf_op jit(solution)/shard_map/grad_sums/col_3/ppermute | solution.py:29
  50.0 4.9 %collective-permute-done.20.refs_2_ = bf16[256,256]{1,0:T(8,128)(2,1)S(1)} collective-permute-done((bf16[256,256]{1,0:T(8,128)(2,1)S(1)}, bf16[256,256]{1,0:T(8,128)(2,1)S(1)}, u32[]{:S(2)}, u32[]{:S(2)}) %collective-permute-start.20) | collective-permute-done | bytes 131104 | tf_op jit(solution)/shard_map/grad_sums/col_2/ppermute | solution.py:29
  54.9 0.7 %branch.1 = (bf16[256,256]{1,0:T(8,128)(2,1)S(1)}, bf16[256,256]{1,0:T(8,128)(2,1)S(1)}, bf16[256,256]{1,0:T(8,128)(2,1)S(1)}, bf16[256,256]{1,0:T(8,128)(2,1)S(1)}) custom-call(bf16[2,256,512]{2,1,0:T(8,128)(2,1)S(1)} %get-tuple-element.44.hidden, bf16[512,256]{1,0:T(8,128)(2,1)S(1)} %collective-permute-done.6.refs_10_.refs_0_, ...), custom_call_target="tpu_custom_call" | custom-call | flops 536870912 | bytes 1048576 | tf_op jit(solution)/shard_map/branch/pallas_call | solution.py:531
  55.6 0.1 collective-permute-start.26
  55.7 0.0 collective-permute-done.19.refs_1_
  55.7 3.1 %collective-permute-done.21.refs_3_ = bf16[256,256]{1,0:T(8,128)(2,1)S(1)} collective-permute-done((bf16[256,256]{1,0:T(8,128)(2,1)S(1)}, bf16[256,256]{1,0:T(8,128)(2,1)S(1)}, u32[]{:S(2)}, u32[]{:S(2)}) %collective-permute-start.21) | collective-permute-done | bytes 131104 | tf_op jit(solution)/shard_map/grad_sums/col_3/ppermute | solution.py:29
  58.8 0.1 grad_sum.1
  58.8 0.3 collective-permute-start.22
  59.1 2.0 %collective-permute-start.25 = (bf16[256,256]{1,0:T(8,128)(2,1)S(1)}, bf16[256,256]{1,0:T(8,128)(2,1)S(1)}, u32[]{:S(2)}, u32[]{:S(2)}) collective-permute-start(bf16[256,256]{1,0:T(8,128)(2,1)S(1)} %get-tuple-element.46), channel_id=1, source_target_pairs={{0,1},{1,0},{2,3},{3,2},{4,5},{5,4},{6,7},{7,6},{8,9},{9,8},{10,11... | collective-permute-start | bytes 393224 | tf_op jit(solution)/shard_map/branch_sums/col_1/ppermute | solution.py:29
  61.1 0.7 collective-permute-done.22.refs_0_
  61.9 3.2 %collective-permute-start.27 = (bf16[256,256]{1,0:T(8,128)(2,1)S(1)}, bf16[256,256]{1,0:T(8,128)(2,1)S(1)}, u32[]{:S(2)}, u32[]{:S(2)}) collective-permute-start(bf16[256,256]{1,0:T(8,128)(2,1)S(1)} %add_convert_fusion), channel_id=1, source_target_pairs={{0,2},{1,3},{2,0},{3,1},{4,6},{5,7},{6,4},{7,5},{8,10},{9,11},{10,... | collective-permute-start | bytes 393224 | tf_op jit(solution)/shard_map/branch_sums/col_2/ppermute | solution.py:29
  65.1 0.1 grad_columns.1
  65.2 2.0 %collective-permute-start.23 = (bf16[80,256]{1,0:T(8,128)(2,1)S(1)}, bf16[80,256]{1,0:T(8,128)(2,1)S(1)}, u32[]{:S(2)}, u32[]{:S(2)}) collective-permute-start(bf16[80,256]{1,0:T(8,128)(2,1)S(1)} %get-tuple-element.41), channel_id=1, source_target_pairs={{0,4},{8,12},{4,0},{12,8},{1,5},{9,13},{5,1},{13,9},{2,6},{10,14},... | collective-permute-start | bytes 122888 | tf_op jit(solution)/shard_map/grad_columns/ppermute | solution.py:44
  67.1 1.9 %collective-permute-start.24 = (bf16[80,256]{1,0:T(8,128)(2,1)S(1)}, bf16[80,256]{1,0:T(8,128)(2,1)S(1)}, u32[]{:S(2)}, u32[]{:S(2)}) collective-permute-start(bf16[80,256]{1,0:T(8,128)(2,1)S(1)} %get-tuple-element.42), channel_id=1, source_target_pairs={{4,8},{8,4},{5,9},{9,5},{6,10},{10,6},{7,11},{11,7},{20,24},{24,20... | collective-permute-start | bytes 122888 | tf_op jit(solution)/shard_map/grad_columns/ppermute | solution.py:44
  69.0 0.0 collective-permute-done.23.refs_1_
  69.1 3.4 %collective-permute-done.24.refs_2_ = bf16[80,256]{1,0:T(8,128)(2,1)S(1)} collective-permute-done((bf16[80,256]{1,0:T(8,128)(2,1)S(1)}, bf16[80,256]{1,0:T(8,128)(2,1)S(1)}, u32[]{:S(2)}, u32[]{:S(2)}) %collective-permute-start.24) | collective-permute-done | bytes 40992 | tf_op jit(solution)/shard_map/grad_columns/ppermute | solution.py:44
  72.4 1.8 %backward_conv.1 = (f32[256,256]{1,0:T(8,128)}, bf16[256,256]{1,0:T(8,128)(2,1)}) custom-call(f32[256,256]{1,0:T(8,128)S(1)} %get-tuple-element.39.cells.grad, f32[7,7,256]{2,1,0:T(8,128)S(1)} %copy-done.4, bf16[256,256]{1,0:T(8,128)(2,1)S(1)} %bitcast.10, bf16[256,256]{1,0:T(8,128)(2,1)S(1)} %bitcast.8, ...), custom_call_target="tpu_custom_call" | custom-call | flops 192675840 | bytes 1048576 | tf_op jit(solution)/shard_map/backward_conv/pallas_call | solution.py:551
  (15 shorter events, 0.1 us)
Async XLA Ops:
  0.6 1.0 %copy-start = (bf16[1024,256]{1,0:T(8,128)(2,1)S(1)}, bf16[1024,256]{1,0:T(8,128)(2,1)}, u32[]{:S(2)}) copy-start(bf16[1024,256]{1,0:T(8,128)(2,1)} %param.10) | copy-start | bytes 1572868
  0.6 4.8 %copy-start.2 = (bf16[256,1024]{1,0:T(8,128)(2,1)S(1)}, bf16[256,1024]{1,0:T(8,128)(2,1)}, u32[]{:S(2)}) copy-start(bf16[256,1024]{1,0:T(8,128)(2,1)} %refs_6_.1) | copy-start | bytes 1572868
  0.7 13.5 %collective-permute-start = (bf16[256,1024]{1,0:T(8,128)(2,1)}, bf16[256,1024]{1,0:T(8,128)(2,1)S(1)}, u32[]{:S(2)}, u32[]{:S(2)}) collective-permute-start(bf16[256,1024]{1,0:T(8,128)(2,1)} %refs_6_.1), channel_id=1, source_target_pairs={{0,4},{4,0},{8,12},{12,8},{1,5},{5,1},{9,13},{13,9},{2,6},{6,2},{1... | collective-permute-start | bytes 1572872 | tf_op jit(solution)/shard_map/w_in_core/ppermute | solution.py:29
  1.7 21.3 %collective-permute-start.6 = (bf16[512,256]{1,0:T(8,128)(2,1)S(1)}, bf16[512,256]{1,0:T(8,128)(2,1)S(1)}, u32[]{:S(2)}, u32[]{:S(2)}) collective-permute-start(bf16[512,256]{1,0:T(8,128)(2,1)S(1)} %constant_dynamic-slice_fusion.2), channel_id=1, source_target_pairs={{0,8},{1,12},{2,0},{3,4},{4,9},{5,13},{6,1},{7,5},{8,10},{9,14},{1... | collective-permute-start | bytes 786440 | tf_op jit(solution)/shard_map/w_out_transposed/ppermute | solution.py:356
  5.4 2.4 %copy-start.1 = (bf16[16,16,256]{2,1,0:T(8,128)(2,1)S(1)}, bf16[16,16,256]{2,1,0:T(8,128)(2,1)}, u32[]{:S(2)}) copy-start(bf16[16,16,256]{2,1,0:T(8,128)(2,1)} %param.6) | copy-start | bytes 393220
  5.4 11.8 %copy-start.3 = (bf16[16,16,256]{2,1,0:T(8,128)(2,1)S(1)}, bf16[16,16,256]{2,1,0:T(8,128)(2,1)}, u32[]{:S(2)}) copy-start(bf16[16,16,256]{2,1,0:T(8,128)(2,1)} %param.11) | copy-start | bytes 393220
  5.5 17.5 %collective-permute-start.7 = (bf16[256,512]{1,0:T(8,128)(2,1)S(1)}, bf16[256,512]{1,0:T(8,128)(2,1)S(1)}, u32[]{:S(2)}, u32[]{:S(2)}) collective-permute-start(bf16[256,512]{1,0:T(8,128)(2,1)S(1)} %get-tuple-element.53), channel_id=1, source_target_pairs={{0,8},{4,12},{8,0},{12,4},{1,9},{5,13},{9,1},{13,5},{2,10},{6,14},... | collective-permute-start | bytes 786440 | tf_op jit(solution)/shard_map/w_in_row_0/ppermute | solution.py:29
  7.8 9.4 %copy-start.4 = (f32[7,7,256]{2,1,0:T(8,128)S(1)}, f32[7,7,256]{2,1,0:T(8,128)}, u32[]{:S(2)}) copy-start(f32[7,7,256]{2,1,0:T(8,128)} %taps.3) | copy-start | bytes 150532
  7.8 3.2 %collective-permute-start.1 = (bf16[48,256]{1,0:T(8,128)(2,1)S(1)}, bf16[48,256]{1,0:T(8,128)(2,1)S(1)}, u32[]{:S(2)}, u32[]{:S(2)}) collective-permute-start(bf16[48,256]{1,0:T(8,128)(2,1)S(1)} %constant_dynamic-slice_fusion.3), channel_id=1, source_target_pairs={{0,16},{16,0},{1,17},{17,1},{2,18},{18,2},{3,19},{19,3},{4,20},{20... | collective-permute-start | bytes 73736 | tf_op jit(solution)/shard_map/image_rows/ppermute | solution.py:44
  11.1 3.1 %collective-permute-start.2 = (bf16[80,256]{1,0:T(8,128)(2,1)S(1)}, bf16[80,256]{1,0:T(8,128)(2,1)S(1)}, u32[]{:S(2)}, u32[]{:S(2)}) collective-permute-start(bf16[80,256]{1,0:T(8,128)(2,1)S(1)} %get-tuple-element.28), channel_id=1, source_target_pairs={{0,4},{8,12},{4,0},{12,8},{1,5},{9,13},{5,1},{13,9},{2,6},{10,14},... | collective-permute-start | bytes 122888 | tf_op jit(solution)/shard_map/image_columns/ppermute | solution.py:44
  11.7 5.6 %collective-permute-start.3 = (bf16[80,256]{1,0:T(8,128)(2,1)S(1)}, bf16[80,256]{1,0:T(8,128)(2,1)S(1)}, u32[]{:S(2)}, u32[]{:S(2)}) collective-permute-start(bf16[80,256]{1,0:T(8,128)(2,1)S(1)} %get-tuple-element.29), channel_id=1, source_target_pairs={{4,8},{8,4},{5,9},{9,5},{6,10},{10,6},{7,11},{11,7},{20,24},{24,20... | collective-permute-start | bytes 122888 | tf_op jit(solution)/shard_map/image_columns/ppermute | solution.py:44
  17.3 0.7 copy-start.5
  19.8 11.4 %collective-permute-start.5 = (bf16[528,256]{1,0:T(8,128)(2,1)S(1)}, bf16[528,256]{1,0:T(8,128)(2,1)S(1)}, u32[]{:S(2)}, u32[]{:S(2)}) collective-permute-start(bf16[528,256]{1,0:T(8,128)(2,1)S(1)} %forward_conv.1.refs_0_), channel_id=1, source_target_pairs={{0,2},{1,3},{2,0},{3,1},{4,6},{5,7},{6,4},{7,5},{8,10},{9,11},{10,... | collective-permute-start | bytes 811016 | tf_op jit(solution)/shard_map/features/col_2/ppermute | solution.py:29
  23.0 8.5 %collective-permute-start.4 = (bf16[528,256]{1,0:T(8,128)(2,1)S(1)}, bf16[528,256]{1,0:T(8,128)(2,1)S(1)}, u32[]{:S(2)}, u32[]{:S(2)}) collective-permute-start(bf16[528,256]{1,0:T(8,128)(2,1)S(1)} %forward_conv.1.refs_0_), channel_id=1, source_target_pairs={{0,1},{1,0},{2,3},{3,2},{4,5},{5,4},{6,7},{7,6},{8,9},{9,8},{10,11... | collective-permute-start | bytes 811016 | tf_op jit(solution)/shard_map/features/col_1/ppermute | solution.py:29
  23.0 5.6 %collective-permute-start.9 = (bf16[512,256]{1,0:T(8,128)(2,1)S(1)}, bf16[512,256]{1,0:T(8,128)(2,1)S(1)}, u32[]{:S(2)}, u32[]{:S(2)}) collective-permute-start(bf16[512,256]{1,0:T(8,128)(2,1)S(1)} %collective-permute-done.6.refs_10_.refs_0_), channel_id=1, source_target_pairs={{0,16},{16,0},{1,17},{17,1},{2,18},{18,2},{3,19},{19,3},{4,20},{20... | collective-permute-start | bytes 786440 | tf_op jit(solution)/shard_map/w_out_section/ppermute | solution.py:29
  24.2 7.0 %collective-permute-start.8 = (bf16[512,256]{1,0:T(8,128)(2,1)S(1)}, bf16[512,256]{1,0:T(8,128)(2,1)S(1)}, u32[]{:S(2)}, u32[]{:S(2)}) collective-permute-start(bf16[512,256]{1,0:T(8,128)(2,1)S(1)} %collective-permute-done.6.refs_10_.refs_0_), channel_id=1, source_target_pairs={{0,8},{4,12},{8,0},{12,4},{1,9},{5,13},{9,1},{13,5},{2,10},{6,14},... | collective-permute-start | bytes 786440 | tf_op jit(solution)/shard_map/w_out_row/ppermute | solution.py:29
  31.5 8.4 %collective-permute-start.10 = (bf16[528,256]{1,0:T(8,128)(2,1)S(1)}, bf16[528,256]{1,0:T(8,128)(2,1)S(1)}, u32[]{:S(2)}, u32[]{:S(2)}) collective-permute-start(bf16[528,256]{1,0:T(8,128)(2,1)S(1)} %collective-permute-done.5.refs_2_), channel_id=1, source_target_pairs={{0,1},{1,0},{2,3},{3,2},{4,5},{5,4},{6,7},{7,6},{8,9},{9,8},{10,11... | collective-permute-start | bytes 811016 | tf_op jit(solution)/shard_map/features/col_1/ppermute | solution.py:29
  32.9 8.0 %collective-permute-start.11 = (bf16[256,512]{1,0:T(8,128)(2,1)S(1)}, bf16[256,512]{1,0:T(8,128)(2,1)S(1)}, u32[]{:S(2)}, u32[]{:S(2)}) collective-permute-start(bf16[256,512]{1,0:T(8,128)(2,1)S(1)} %get-tuple-element.32), channel_id=1, source_target_pairs={{0,8},{4,12},{8,0},{12,4},{1,9},{5,13},{9,1},{13,5},{2,10},{6,14},... | collective-permute-start | bytes 786440 | tf_op jit(solution)/shard_map/w_in_row_1/ppermute | solution.py:29
  33.0 8.6 %collective-permute-start.17 = (bf16[512,256]{1,0:T(8,128)(2,1)S(1)}, bf16[512,256]{1,0:T(8,128)(2,1)S(1)}, u32[]{:S(2)}, u32[]{:S(2)}) collective-permute-start(bf16[512,256]{1,0:T(8,128)(2,1)S(1)} %collective-permute-done.8.refs_12_.refs_2_), channel_id=1, source_target_pairs={{0,16},{16,0},{1,17},{17,1},{2,18},{18,2},{3,19},{19,3},{4,20},{20... | collective-permute-start | bytes 786440 | tf_op jit(solution)/shard_map/w_out_both/ppermute | solution.py:29
  39.9 1.8 %collective-permute-start.14 = (bf16[512,256]{1,0:T(8,128)(2,1)S(1)}, bf16[512,256]{1,0:T(8,128)(2,1)S(1)}, u32[]{:S(2)}, u32[]{:S(2)}) collective-permute-start(bf16[512,256]{1,0:T(8,128)(2,1)S(1)} %collective-permute-done.6.refs_10_.refs_0_), channel_id=1, source_target_pairs={{0,4},{4,0},{8,12},{12,8},{1,5},{5,1},{9,13},{13,9},{2,6},{6,2},{1... | collective-permute-start | bytes 786440 | tf_op jit(solution)/shard_map/w_out_core_0_0/ppermute | solution.py:29
  40.4 1.7 %collective-permute-start.12 = (bf16[256,512]{1,0:T(8,128)(2,1)S(1)}, bf16[256,512]{1,0:T(8,128)(2,1)S(1)}, u32[]{:S(2)}, u32[]{:S(2)}) collective-permute-start(bf16[256,512]{1,0:T(8,128)(2,1)S(1)} %collective-permute-done.7.refs_4_), channel_id=1, source_target_pairs={{0,4},{4,0},{8,12},{12,8},{1,5},{5,1},{9,13},{13,9},{2,6},{6,2},{1... | collective-permute-start | bytes 786440 | tf_op jit(solution)/shard_map/w_in_core_2_0/ppermute | solution.py:29
  40.5 1.9 %collective-permute-start.16 = (bf16[512,256]{1,0:T(8,128)(2,1)S(1)}, bf16[512,256]{1,0:T(8,128)(2,1)S(1)}, u32[]{:S(2)}, u32[]{:S(2)}) collective-permute-start(bf16[512,256]{1,0:T(8,128)(2,1)S(1)} %collective-permute-done.9.refs_14_.refs_4_), channel_id=1, source_target_pairs={{0,4},{4,0},{8,12},{12,8},{1,5},{5,1},{9,13},{13,9},{2,6},{6,2},{1... | collective-permute-start | bytes 786440 | tf_op jit(solution)/shard_map/w_out_core_0_1/ppermute | solution.py:29
  40.9 1.9 %collective-permute-start.15 = (bf16[512,256]{1,0:T(8,128)(2,1)S(1)}, bf16[512,256]{1,0:T(8,128)(2,1)S(1)}, u32[]{:S(2)}, u32[]{:S(2)}) collective-permute-start(bf16[512,256]{1,0:T(8,128)(2,1)S(1)} %collective-permute-done.8.refs_12_.refs_2_), channel_id=1, source_target_pairs={{0,4},{4,0},{8,12},{12,8},{1,5},{5,1},{9,13},{13,9},{2,6},{6,2},{1... | collective-permute-start | bytes 786440 | tf_op jit(solution)/shard_map/w_out_core_2_0/ppermute | solution.py:29
  41.6 1.5 %collective-permute-start.13 = (bf16[256,512]{1,0:T(8,128)(2,1)S(1)}, bf16[256,512]{1,0:T(8,128)(2,1)S(1)}, u32[]{:S(2)}, u32[]{:S(2)}) collective-permute-start(bf16[256,512]{1,0:T(8,128)(2,1)S(1)} %collective-permute-done.11.refs_5_), channel_id=1, source_target_pairs={{0,4},{4,0},{8,12},{12,8},{1,5},{5,1},{9,13},{13,9},{2,6},{6,2},{1... | collective-permute-start | bytes 786440 | tf_op jit(solution)/shard_map/w_in_core_2_1/ppermute | solution.py:29
  41.8 1.8 %collective-permute-start.18 = (bf16[512,256]{1,0:T(8,128)(2,1)S(1)}, bf16[512,256]{1,0:T(8,128)(2,1)S(1)}, u32[]{:S(2)}, u32[]{:S(2)}) collective-permute-start(bf16[512,256]{1,0:T(8,128)(2,1)S(1)} %collective-permute-done.17.refs_16_.refs_6_), channel_id=1, source_target_pairs={{0,4},{4,0},{8,12},{12,8},{1,5},{5,1},{9,13},{13,9},{2,6},{6,2},{1... | collective-permute-start | bytes 786440 | tf_op jit(solution)/shard_map/w_out_core_2_1/ppermute | solution.py:29
  46.4 8.5 %collective-permute-start.20 = (bf16[256,256]{1,0:T(8,128)(2,1)S(1)}, bf16[256,256]{1,0:T(8,128)(2,1)S(1)}, u32[]{:S(2)}, u32[]{:S(2)}) collective-permute-start(bf16[256,256]{1,0:T(8,128)(2,1)S(1)} %get-tuple-element.37), channel_id=1, source_target_pairs={{0,2},{1,3},{2,0},{3,1},{4,6},{5,7},{6,4},{7,5},{8,10},{9,11},{10,... | collective-permute-start | bytes 393224 | tf_op jit(solution)/shard_map/grad_sums/col_2/ppermute | solution.py:29
  47.4 8.3 %collective-permute-start.19 = (bf16[256,256]{1,0:T(8,128)(2,1)S(1)}, bf16[256,256]{1,0:T(8,128)(2,1)S(1)}, u32[]{:S(2)}, u32[]{:S(2)}) collective-permute-start(bf16[256,256]{1,0:T(8,128)(2,1)S(1)} %get-tuple-element.36), channel_id=1, source_target_pairs={{0,1},{1,0},{2,3},{3,2},{4,5},{5,4},{6,7},{7,6},{8,9},{9,8},{10,11... | collective-permute-start | bytes 393224 | tf_op jit(solution)/shard_map/grad_sums/col_1/ppermute | solution.py:29
  48.7 10.1 %collective-permute-start.21 = (bf16[256,256]{1,0:T(8,128)(2,1)S(1)}, bf16[256,256]{1,0:T(8,128)(2,1)S(1)}, u32[]{:S(2)}, u32[]{:S(2)}) collective-permute-start(bf16[256,256]{1,0:T(8,128)(2,1)S(1)} %get-tuple-element.38), channel_id=1, source_target_pairs={{0,3},{1,2},{2,1},{3,0},{4,7},{5,6},{6,5},{7,4},{8,11},{9,10},{10,... | collective-permute-start | bytes 393224 | tf_op jit(solution)/shard_map/grad_sums/col_3/ppermute | solution.py:29
  55.6 6.3 %collective-permute-start.26 = (bf16[256,256]{1,0:T(8,128)(2,1)S(1)}, bf16[256,256]{1,0:T(8,128)(2,1)S(1)}, u32[]{:S(2)}, u32[]{:S(2)}) collective-permute-start(bf16[256,256]{1,0:T(8,128)(2,1)S(1)} %get-tuple-element.48), channel_id=1, source_target_pairs={{0,1},{1,0},{2,3},{3,2},{4,5},{5,4},{6,7},{7,6},{8,9},{9,8},{10,11... | collective-permute-start | bytes 393224 | tf_op jit(solution)/shard_map/branch_sums/col_1/ppermute | solution.py:29
  58.8 3.0 %collective-permute-start.22 = (bf16[48,256]{1,0:T(8,128)(2,1)S(1)}, bf16[48,256]{1,0:T(8,128)(2,1)S(1)}, u32[]{:S(2)}, u32[]{:S(2)}) collective-permute-start(bf16[48,256]{1,0:T(8,128)(2,1)S(1)} %get-tuple-element.40), channel_id=1, source_target_pairs={{0,16},{16,0},{1,17},{17,1},{2,18},{18,2},{3,19},{19,3},{4,20},{20... | collective-permute-start | bytes 73736 | tf_op jit(solution)/shard_map/grad_rows/ppermute | solution.py:44
  59.1 13.3 %collective-permute-start.25 = (bf16[256,256]{1,0:T(8,128)(2,1)S(1)}, bf16[256,256]{1,0:T(8,128)(2,1)S(1)}, u32[]{:S(2)}, u32[]{:S(2)}) collective-permute-start(bf16[256,256]{1,0:T(8,128)(2,1)S(1)} %get-tuple-element.46), channel_id=1, source_target_pairs={{0,1},{1,0},{2,3},{3,2},{4,5},{5,4},{6,7},{7,6},{8,9},{9,8},{10,11... | collective-permute-start | bytes 393224 | tf_op jit(solution)/shard_map/branch_sums/col_1/ppermute | solution.py:29
  61.9 10.5 %collective-permute-start.27 = (bf16[256,256]{1,0:T(8,128)(2,1)S(1)}, bf16[256,256]{1,0:T(8,128)(2,1)S(1)}, u32[]{:S(2)}, u32[]{:S(2)}) collective-permute-start(bf16[256,256]{1,0:T(8,128)(2,1)S(1)} %add_convert_fusion), channel_id=1, source_target_pairs={{0,2},{1,3},{2,0},{3,1},{4,6},{5,7},{6,4},{7,5},{8,10},{9,11},{10,... | collective-permute-start | bytes 393224 | tf_op jit(solution)/shard_map/branch_sums/col_2/ppermute | solution.py:29
  65.2 3.9 %collective-permute-start.23 = (bf16[80,256]{1,0:T(8,128)(2,1)S(1)}, bf16[80,256]{1,0:T(8,128)(2,1)S(1)}, u32[]{:S(2)}, u32[]{:S(2)}) collective-permute-start(bf16[80,256]{1,0:T(8,128)(2,1)S(1)} %get-tuple-element.41), channel_id=1, source_target_pairs={{0,4},{8,12},{4,0},{12,8},{1,5},{9,13},{5,1},{13,9},{2,6},{10,14},... | collective-permute-start | bytes 122888 | tf_op jit(solution)/shard_map/grad_columns/ppermute | solution.py:44
  67.1 5.3 %collective-permute-start.24 = (bf16[80,256]{1,0:T(8,128)(2,1)S(1)}, bf16[80,256]{1,0:T(8,128)(2,1)S(1)}, u32[]{:S(2)}, u32[]{:S(2)}) collective-permute-start(bf16[80,256]{1,0:T(8,128)(2,1)S(1)} %get-tuple-element.42), channel_id=1, source_target_pairs={{4,8},{8,4},{5,9},{9,5},{6,10},{10,6},{7,11},{11,7},{20,24},{24,20... | collective-permute-start | bytes 122888 | tf_op jit(solution)/shard_map/grad_columns/ppermute | solution.py:44

commit v6 on v5

--- a/solution.py
+++ b/solution.py
@@ -169,7 +169,9 @@
 
 def forward_conv_kernel(dims, n_top, n_side, image, taps, gain, upstream, *refs):
     tops, columns, refs = refs[:n_top], refs[n_top : n_top + n_side], refs[n_top + n_side :]
-    message, pad, shifted, mixed, tail = refs
+    message, pad, shifted, mixed, tail, gain_here, sem = refs
+    gain_copy = pltpu.make_async_copy(gain, gain_here, sem)
+    gain_copy.start()
     height, breadth = dims
     cells, channels = image.shape
     fill_padded(pad, image, tops, columns, height, breadth)
@@ -188,7 +190,8 @@
         flat = jnp.broadcast_to(column, (cells, 128)).T
         for p in range(per):
             tail[t * per + p : t * per + p + 1, :] = flat[:1, p * channels : (p + 1) * channels]
-    for t, part in enumerate(split3(gain[...])):
+    gain_copy.wait()
+    for t, part in enumerate(split3(gain_here[...])):
         tail[2 * per + t : 2 * per + t + 1, :] = part.astype(F32)
     message[cells : message.shape[0] - cells, :] = tail[...].astype(BF16)
     message[message.shape[0] - cells :, :] = upstream[...]
@@ -227,7 +230,7 @@
         normed[k] = value
         scaled[k] = (value * gains[k][:1, :]).astype(BF16)
     share = act_grad.shape[2]
-    tile = min(256, share)
+    tile = min(512, share)
     slots = [slot() for slot, _ in in_slots]
     places = []
 
@@ -325,6 +328,7 @@
 
 
 IN_VMEM = pl.BlockSpec(memory_space=pltpu.VMEM)
+IN_HBM = pl.BlockSpec(memory_space=pltpu.HBM)
 
 
 def tie(x, *others):
@@ -408,11 +412,9 @@
             (r ^ bit, s): core_in[0] if r == 0 else swap(x, "row", bit, f"w_in_core_{r}_{s}")
             for (r, s), x in got_in.items()
         }
-        gate = swap(tie(got_out[0, 0], messages), "row", bit, "w_out_core_0_0")
-        got_out |= {(bit, 0): gate} | {
-            (r ^ bit, s): swap(tie(x, gate) if r and s else x, "row", bit, f"w_out_core_{r}_{s}")
+        got_out |= {
+            (r ^ bit, s): swap(tie(x, messages) if r and s else x, "row", bit, f"w_out_core_{r}_{s}")
             for (r, s), x in got_out.items()
-            if r or s
         }
     keys = list(got_in)
     whole = [(block(r), [n]) for n, (r, p) in enumerate(keys) if p is None]
@@ -494,8 +496,9 @@
         8 * MIB,
         functools.partial(forward_conv_kernel, dims, n_top, n_side),
         jax.ShapeDtypeStruct((rows, channels), BF16),
-        [IN_VMEM] * (4 + n_top + n_side),
-        padded + [pltpu.VMEM((cells, channels), F32), pltpu.VMEM((rows - 2 * cells, channels), F32)],
+        [IN_VMEM] * 2 + [IN_HBM] + [IN_VMEM] * (1 + n_top + n_side),
+        padded + [pltpu.VMEM((cells, channels), F32), pltpu.VMEM((rows - 2 * cells, channels), F32)]
+        + [pltpu.VMEM((1, channels), F32), pltpu.SemaphoreType.DMA],
         **conv_cost,
     )(tie(flat_image, core_in), conv_kernel, norm_gain.reshape(1, channels), flat_up, *tops, *columns)
 

time: 74.4 us -> 74.1 us (level)
  waiting for transfers between devices: 32.4 us -> 28.3 us
  starting transfers between devices: 32 us -> 35.4 us
    ppermute x21, waiting for transfers between devices: 23.2 us -> 20.8 us  [swap(): return lax.ppermute(x, axis, [(i, i ^ bit) for i in range(count)])]
    ppermute x6, starting transfers between devices: 8.51 us -> 10.6 us  [meet(): lax.ppermute(strip, axis, pairs)]
    ppermute x6, waiting for transfers between devices: 9.13 us -> 7.45 us  [meet(): lax.ppermute(strip, axis, pairs)]
    ppermute x21, starting transfers between devices: 19.8 us -> 21.1 us  [swap(): return lax.ppermute(x, axis, [(i, i ^ bit) for i in range(count)])]
  transfers between devices with their start and end apart: 28 -> 28, of which waited for: 14 -> 13; matrix products, arithmetic and copies ran while one was open for 0% -> 0% of each run, Pallas kernels for 4% -> 4%
where the time goes in v6:
time: 74.1 us; the launch traced here: 73.6 us
  starting transfers between devices  35.4 us (48%)
  waiting for transfers between devices  28.3 us (38%)
  Pallas kernels  7.49 us (10%)
  local copies, waits for them, and re-layouts  1.65 us (2%)
  between operations  0.79 us (1%)
    ppermute x21, starting transfers between devices, swap(): return lax.ppermute(x, axis, [(i, i ^ bit) for i in range(count)])  21.1 us
    ppermute x21, waiting for transfers between devices, swap(): return lax.ppermute(x, axis, [(i, i ^ bit) for i in range(count)])  20.8 us
    ppermute x6, starting transfers between devices, meet(): lax.ppermute(strip, axis, pairs)  10.6 us
    ppermute x6, waiting for transfers between devices, meet(): lax.ppermute(strip, axis, pairs)  7.45 us
    ppermute x1, starting transfers between devices, weights_begin(): lax.ppermute(mine_out, ('row', 'col'), [(r * n_col + z, (z ^ n_row // 2)...  3.69 us
    pallas_call x1, Pallas kernels, local(): call('mlp', 24 * MIB, functools.partial(mlp_kernel, in_pieces, out_pieces...  2.85 us
    pallas_call x1, Pallas kernels, local(): call('forward_conv', 8 * MIB, functools.partial(forward_conv_kernel, dims...  1.88 us
    pallas_call x1, Pallas kernels, local(): call('backward_conv', 8 * MIB, functools.partial(backward_conv_kernel, di...  1.79 us
  transfers between devices with their start and end apart: 28, of which 13 were waited for; matrix products, arithmetic and copies ran while one was open for 0% of the time, Pallas kernels for 4%

profile of v6, /device:TPU:1, one launch (start us, length us, event | category | flops | bytes accessed | tf_op | source)
XLA Modules:
  0.0 73.6 jit_solution(2625861723212609260)
XLA Ops:
  0.6 0.0 copy-start
  0.7 0.1 collective-permute-start
  0.8 0.9 %copy-done = bf16[1024,256]{1,0:T(8,128)(2,1)S(1)} copy-done((bf16[1024,256]{1,0:T(8,128)(2,1)S(1)}, bf16[1024,256]{1,0:T(8,128)(2,1)}, u32[]{:S(2)}) %copy-start) | copy-done | bytes 524312
  1.7 3.7 %collective-permute-start.6 = (bf16[512,256]{1,0:T(8,128)(2,1)S(1)}, bf16[512,256]{1,0:T(8,128)(2,1)S(1)}, u32[]{:S(2)}, u32[]{:S(2)}) collective-permute-start(bf16[512,256]{1,0:T(8,128)(2,1)S(1)} %constant_dynamic-slice_fusion.2), channel_id=1, source_target_pairs={{0,8},{1,12},{2,0},{3,4},{4,9},{5,13},{6,1},{7,5},{8,10},{9,14},{1... | collective-permute-start | bytes 786440 | tf_op jit(solution)/shard_map/w_out_transposed/ppermute | solution.py:360
  5.4 0.0 copy-start.3
  5.5 2.4 %collective-permute-start.7 = (bf16[256,512]{1,0:T(8,128)(2,1)S(1)}, bf16[256,512]{1,0:T(8,128)(2,1)S(1)}, u32[]{:S(2)}, u32[]{:S(2)}) collective-permute-start(bf16[256,512]{1,0:T(8,128)(2,1)S(1)} %get-tuple-element.51), channel_id=1, source_target_pairs={{0,8},{4,12},{8,0},{12,4},{1,9},{5,13},{9,1},{13,5},{2,10},{6,14},... | collective-permute-start | bytes 786440 | tf_op jit(solution)/shard_map/w_in_row_0/ppermute | solution.py:29
  7.8 1.3 %collective-permute-start.1 = (bf16[48,256]{1,0:T(8,128)(2,1)S(1)}, bf16[48,256]{1,0:T(8,128)(2,1)S(1)}, u32[]{:S(2)}, u32[]{:S(2)}) collective-permute-start(bf16[48,256]{1,0:T(8,128)(2,1)S(1)} %constant_dynamic-slice_fusion.3), channel_id=1, source_target_pairs={{0,16},{16,0},{1,17},{17,1},{2,18},{18,2},{3,19},{19,3},{4,20},{20... | collective-permute-start | bytes 73736 | tf_op jit(solution)/shard_map/image_rows/ppermute | solution.py:44
  9.1 1.9 %collective-permute-done.1.refs_0_ = bf16[48,256]{1,0:T(8,128)(2,1)S(1)} collective-permute-done((bf16[48,256]{1,0:T(8,128)(2,1)S(1)}, bf16[48,256]{1,0:T(8,128)(2,1)S(1)}, u32[]{:S(2)}, u32[]{:S(2)}) %collective-permute-start.1) | collective-permute-done | bytes 24608 | tf_op jit(solution)/shard_map/image_rows/ppermute | solution.py:44
  11.0 0.1 image_columns.1
  11.1 0.6 collective-permute-start.2
  11.7 2.5 %collective-permute-start.3 = (bf16[80,256]{1,0:T(8,128)(2,1)S(1)}, bf16[80,256]{1,0:T(8,128)(2,1)S(1)}, u32[]{:S(2)}, u32[]{:S(2)}) collective-permute-start(bf16[80,256]{1,0:T(8,128)(2,1)S(1)} %get-tuple-element.28), channel_id=1, source_target_pairs={{4,8},{8,4},{5,9},{9,5},{6,10},{10,6},{7,11},{11,7},{20,24},{24,20... | collective-permute-start | bytes 122888 | tf_op jit(solution)/shard_map/image_columns/ppermute | solution.py:44
  14.1 0.0 collective-permute-done.refs_9_
  14.1 0.0 collective-permute-done.2.refs_1_
  14.2 3.1 %collective-permute-done.3.refs_2_ = bf16[80,256]{1,0:T(8,128)(2,1)S(1)} collective-permute-done((bf16[80,256]{1,0:T(8,128)(2,1)S(1)}, bf16[80,256]{1,0:T(8,128)(2,1)S(1)}, u32[]{:S(2)}, u32[]{:S(2)}) %collective-permute-start.3) | collective-permute-done | bytes 40992 | tf_op jit(solution)/shard_map/image_columns/ppermute | solution.py:44
  17.3 0.7 copy-done.5
  18.0 1.9 %forward_conv.1.refs_0_ = bf16[528,256]{1,0:T(8,128)(2,1)S(1)} custom-call(bf16[256,256]{1,0:T(8,128)(2,1)S(1)} %bitcast.7, f32[7,7,256]{2,1,0:T(8,128)S(1)} %copy-done.4, f32[1,256]{1,0:T(1,128)S(1)} %bitcast.11, bf16[256,256]{1,0:T(8,128)(2,1)S(1)} %bitcast.9, bf16[48,256]{1,0:T(8,128)(2,1)S(1)} %collective-permute-done.1.refs_0_, ...), custom_call_target="tpu_custom_call" | custom-call | flops 192675840 | bytes 1048576 | tf_op jit(solution)/shard_map/forward_conv/pallas_call | solution.py:494
  19.8 3.2 %collective-permute-start.5 = (bf16[528,256]{1,0:T(8,128)(2,1)S(1)}, bf16[528,256]{1,0:T(8,128)(2,1)S(1)}, u32[]{:S(2)}, u32[]{:S(2)}) collective-permute-start(bf16[528,256]{1,0:T(8,128)(2,1)S(1)} %forward_conv.1.refs_0_), channel_id=1, source_target_pairs={{0,2},{1,3},{2,0},{3,1},{4,6},{5,7},{6,4},{7,5},{8,10},{9,11},{10,... | collective-permute-start | bytes 811016 | tf_op jit(solution)/shard_map/features/col_2/ppermute | solution.py:29
  23.0 0.0 collective-permute-start.4
  23.0 0.0 collective-permute-done.6.refs_10_.refs_0_
  23.1 0.0 collective-permute-done.7.refs_4_
  23.1 1.3 %collective-permute-start.9 = (bf16[512,256]{1,0:T(8,128)(2,1)S(1)}, bf16[512,256]{1,0:T(8,128)(2,1)S(1)}, u32[]{:S(2)}, u32[]{:S(2)}) collective-permute-start(bf16[512,256]{1,0:T(8,128)(2,1)S(1)} %collective-permute-done.6.refs_10_.refs_0_), channel_id=1, source_target_pairs={{0,16},{16,0},{1,17},{17,1},{2,18},{18,2},{3,19},{19,3},{4,20},{20... | collective-permute-start | bytes 786440 | tf_op jit(solution)/shard_map/w_out_section/ppermute | solution.py:29
  24.3 0.0 collective-permute-start.8
  24.3 4.3 %collective-permute-done.9.refs_14_.refs_4_ = bf16[512,256]{1,0:T(8,128)(2,1)S(1)} collective-permute-done((bf16[512,256]{1,0:T(8,128)(2,1)S(1)}, bf16[512,256]{1,0:T(8,128)(2,1)S(1)}, u32[]{:S(2)}, u32[]{:S(2)}) %collective-permute-start.9) | collective-permute-done | bytes 262176 | tf_op jit(solution)/shard_map/w_out_section/ppermute | solution.py:29
  28.6 2.7 %collective-permute-done.8.refs_12_.refs_2_ = bf16[512,256]{1,0:T(8,128)(2,1)S(1)} collective-permute-done((bf16[512,256]{1,0:T(8,128)(2,1)S(1)}, bf16[512,256]{1,0:T(8,128)(2,1)S(1)}, u32[]{:S(2)}, u32[]{:S(2)}) %collective-permute-start.8) | collective-permute-done | bytes 262176 | tf_op jit(solution)/shard_map/w_out_row/ppermute | solution.py:29
  31.3 0.0 collective-permute-done.5.refs_2_
  31.3 0.3 collective-permute-done.4.refs_1_
  31.6 1.4 %collective-permute-start.10 = (bf16[528,256]{1,0:T(8,128)(2,1)S(1)}, bf16[528,256]{1,0:T(8,128)(2,1)S(1)}, u32[]{:S(2)}, u32[]{:S(2)}) collective-permute-start(bf16[528,256]{1,0:T(8,128)(2,1)S(1)} %collective-permute-done.5.refs_2_), channel_id=1, source_target_pairs={{0,1},{1,0},{2,3},{3,2},{4,5},{5,4},{6,7},{7,6},{8,9},{9,8},{10,11... | collective-permute-start | bytes 811016 | tf_op jit(solution)/shard_map/features/col_1/ppermute | solution.py:29
  33.0 0.1 collective-permute-start.11
  33.1 0.3 collective-permute-start.17
  33.4 2.2 %collective-permute-start.12 = (bf16[256,512]{1,0:T(8,128)(2,1)S(1)}, bf16[256,512]{1,0:T(8,128)(2,1)S(1)}, u32[]{:S(2)}, u32[]{:S(2)}) collective-permute-start(bf16[256,512]{1,0:T(8,128)(2,1)S(1)} %collective-permute-done.7.refs_4_), channel_id=1, source_target_pairs={{0,4},{4,0},{8,12},{12,8},{1,5},{5,1},{9,13},{13,9},{2,6},{6,2},{1... | collective-permute-start | bytes 786440 | tf_op jit(solution)/shard_map/w_in_core_2_0/ppermute | solution.py:29
  35.6 0.0 collective-permute-start.14
  35.6 5.1 %collective-permute-done.11.refs_5_ = bf16[256,512]{1,0:T(8,128)(2,1)S(1)} collective-permute-done((bf16[256,512]{1,0:T(8,128)(2,1)S(1)}, bf16[256,512]{1,0:T(8,128)(2,1)S(1)}, u32[]{:S(2)}, u32[]{:S(2)}) %collective-permute-start.11) | collective-permute-done | bytes 262176 | tf_op jit(solution)/shard_map/w_in_row_1/ppermute | solution.py:29
  40.7 1.0 %collective-permute-start.16 = (bf16[512,256]{1,0:T(8,128)(2,1)S(1)}, bf16[512,256]{1,0:T(8,128)(2,1)S(1)}, u32[]{:S(2)}, u32[]{:S(2)}) collective-permute-start(bf16[512,256]{1,0:T(8,128)(2,1)S(1)} %collective-permute-done.9.refs_14_.refs_4_), channel_id=1, source_target_pairs={{0,4},{4,0},{8,12},{12,8},{1,5},{5,1},{9,13},{13,9},{2,6},{6,2},{1... | collective-permute-start | bytes 786440 | tf_op jit(solution)/shard_map/w_out_core_0_1/ppermute | solution.py:29
  41.7 0.0 collective-permute-done.17.refs_16_.refs_6_
  41.7 0.1 collective-permute-start.15
  41.8 0.0 collective-permute-done.10.refs_3_
  41.8 0.4 collective-permute-start.13
  42.2 0.0 collective-permute-done.12.refs_7_
  42.2 0.1 collective-permute-start.18
  42.4 0.0 collective-permute-done.14.refs_11_.refs_1_
  42.4 0.5 collective-permute-done.16.refs_15_.refs_5_
  42.9 0.4 collective-permute-done.15.refs_13_.refs_3_
  43.2 0.4 collective-permute-done.13.refs_8_
  43.6 0.4 collective-permute-done.18.refs_17_.refs_7_
  44.0 2.9 %mlp.1 = (bf16[256,256]{1,0:T(8,128)(2,1)S(1)}, bf16[256,256]{1,0:T(8,128)(2,1)S(1)}, bf16[256,256]{1,0:T(8,128)(2,1)S(1)}, bf16[256,256]{1,0:T(8,128)(2,1)S(1)}, bf16[2,256,512]{2,1,0:T(8,128)(2,1)S(1)}) custom-call(bf16[528,256]{1,0:T(8,128)(2,1)S(1)} %forward_conv.1.refs_0_, bf16[528,256]{1,0:T(8,128)(2,1)S(1)} %collective-permute-done.4.refs_1_, ...), custom_call_target="tpu_custom_call" | custom-call | flops 1610612736 | bytes 1048576 | tf_op jit(solution)/shard_map/mlp/pallas_call | solution.py:515
  46.9 1.0 %collective-permute-start.20 = (bf16[256,256]{1,0:T(8,128)(2,1)S(1)}, bf16[256,256]{1,0:T(8,128)(2,1)S(1)}, u32[]{:S(2)}, u32[]{:S(2)}) collective-permute-start(bf16[256,256]{1,0:T(8,128)(2,1)S(1)} %get-tuple-element.35), channel_id=1, source_target_pairs={{0,2},{1,3},{2,0},{3,1},{4,6},{5,7},{6,4},{7,5},{8,10},{9,11},{10,... | collective-permute-start | bytes 393224 | tf_op jit(solution)/shard_map/grad_sums/col_2/ppermute | solution.py:29
  47.8 0.1 collective-permute-start.19
  47.9 2.6 %collective-permute-start.21 = (bf16[256,256]{1,0:T(8,128)(2,1)S(1)}, bf16[256,256]{1,0:T(8,128)(2,1)S(1)}, u32[]{:S(2)}, u32[]{:S(2)}) collective-permute-start(bf16[256,256]{1,0:T(8,128)(2,1)S(1)} %get-tuple-element.36), channel_id=1, source_target_pairs={{0,3},{1,2},{2,1},{3,0},{4,7},{5,6},{6,5},{7,4},{8,11},{9,10},{10,... | collective-permute-start | bytes 393224 | tf_op jit(solution)/shard_map/grad_sums/col_3/ppermute | solution.py:29
  50.5 6.2 %collective-permute-done.20.refs_2_ = bf16[256,256]{1,0:T(8,128)(2,1)S(1)} collective-permute-done((bf16[256,256]{1,0:T(8,128)(2,1)S(1)}, bf16[256,256]{1,0:T(8,128)(2,1)S(1)}, u32[]{:S(2)}, u32[]{:S(2)}) %collective-permute-start.20) | collective-permute-done | bytes 131104 | tf_op jit(solution)/shard_map/grad_sums/col_2/ppermute | solution.py:29
  56.7 0.7 %branch.1 = (bf16[256,256]{1,0:T(8,128)(2,1)S(1)}, bf16[256,256]{1,0:T(8,128)(2,1)S(1)}, bf16[256,256]{1,0:T(8,128)(2,1)S(1)}, bf16[256,256]{1,0:T(8,128)(2,1)S(1)}) custom-call(bf16[2,256,512]{2,1,0:T(8,128)(2,1)S(1)} %get-tuple-element.42.hidden, bf16[512,256]{1,0:T(8,128)(2,1)S(1)} %collective-permute-done.6.refs_10_.refs_0_, ...), custom_call_target="tpu_custom_call" | custom-call | flops 536870912 | bytes 1048576 | tf_op jit(solution)/shard_map/branch/pallas_call | solution.py:534
  57.5 0.1 collective-permute-start.26
  57.5 0.0 collective-permute-done.19.refs_1_
  57.5 0.6 collective-permute-done.21.refs_3_
  58.1 0.1 grad_sum.1
  58.2 0.8 %collective-permute-start.22 = (bf16[48,256]{1,0:T(8,128)(2,1)S(1)}, bf16[48,256]{1,0:T(8,128)(2,1)S(1)}, u32[]{:S(2)}, u32[]{:S(2)}) collective-permute-start(bf16[48,256]{1,0:T(8,128)(2,1)S(1)} %get-tuple-element.38), channel_id=1, source_target_pairs={{0,16},{16,0},{1,17},{17,1},{2,18},{18,2},{3,19},{19,3},{4,20},{20... | collective-permute-start | bytes 73736 | tf_op jit(solution)/shard_map/grad_rows/ppermute | solution.py:44
  59.0 3.1 %collective-permute-start.25 = (bf16[256,256]{1,0:T(8,128)(2,1)S(1)}, bf16[256,256]{1,0:T(8,128)(2,1)S(1)}, u32[]{:S(2)}, u32[]{:S(2)}) collective-permute-start(bf16[256,256]{1,0:T(8,128)(2,1)S(1)} %get-tuple-element.44), channel_id=1, source_target_pairs={{0,1},{1,0},{2,3},{3,2},{4,5},{5,4},{6,7},{7,6},{8,9},{9,8},{10,11... | collective-permute-start | bytes 393224 | tf_op jit(solution)/shard_map/branch_sums/col_1/ppermute | solution.py:29
  62.1 0.0 collective-permute-done.22.refs_0_
  62.1 1.6 %collective-permute-start.27 = (bf16[256,256]{1,0:T(8,128)(2,1)S(1)}, bf16[256,256]{1,0:T(8,128)(2,1)S(1)}, u32[]{:S(2)}, u32[]{:S(2)}) collective-permute-start(bf16[256,256]{1,0:T(8,128)(2,1)S(1)} %add_convert_fusion), channel_id=1, source_target_pairs={{0,2},{1,3},{2,0},{3,1},{4,6},{5,7},{6,4},{7,5},{8,10},{9,11},{10,... | collective-permute-start | bytes 393224 | tf_op jit(solution)/shard_map/branch_sums/col_2/ppermute | solution.py:29
  63.8 0.1 grad_columns.1
  63.9 2.6 %collective-permute-start.23 = (bf16[80,256]{1,0:T(8,128)(2,1)S(1)}, bf16[80,256]{1,0:T(8,128)(2,1)S(1)}, u32[]{:S(2)}, u32[]{:S(2)}) collective-permute-start(bf16[80,256]{1,0:T(8,128)(2,1)S(1)} %get-tuple-element.39), channel_id=1, source_target_pairs={{0,4},{8,12},{4,0},{12,8},{1,5},{9,13},{5,1},{13,9},{2,6},{10,14},... | collective-permute-start | bytes 122888 | tf_op jit(solution)/shard_map/grad_columns/ppermute | solution.py:44
  66.5 2.9 %collective-permute-start.24 = (bf16[80,256]{1,0:T(8,128)(2,1)S(1)}, bf16[80,256]{1,0:T(8,128)(2,1)S(1)}, u32[]{:S(2)}, u32[]{:S(2)}) collective-permute-start(bf16[80,256]{1,0:T(8,128)(2,1)S(1)} %get-tuple-element.40), channel_id=1, source_target_pairs={{4,8},{8,4},{5,9},{9,5},{6,10},{10,6},{7,11},{11,7},{20,24},{24,20... | collective-permute-start | bytes 122888 | tf_op jit(solution)/shard_map/grad_columns/ppermute | solution.py:44
  69.4 0.0 collective-permute-done.23.refs_1_
  69.4 2.4 %collective-permute-done.24.refs_2_ = bf16[80,256]{1,0:T(8,128)(2,1)S(1)} collective-permute-done((bf16[80,256]{1,0:T(8,128)(2,1)S(1)}, bf16[80,256]{1,0:T(8,128)(2,1)S(1)}, u32[]{:S(2)}, u32[]{:S(2)}) %collective-permute-start.24) | collective-permute-done | bytes 40992 | tf_op jit(solution)/shard_map/grad_columns/ppermute | solution.py:44
  71.8 1.8 %backward_conv.1 = (f32[256,256]{1,0:T(8,128)}, bf16[256,256]{1,0:T(8,128)(2,1)}) custom-call(f32[256,256]{1,0:T(8,128)S(1)} %get-tuple-element.37.cells.grad, f32[7,7,256]{2,1,0:T(8,128)S(1)} %copy-done.4, bf16[256,256]{1,0:T(8,128)(2,1)S(1)} %bitcast.10, bf16[256,256]{1,0:T(8,128)(2,1)S(1)} %bitcast.8, ...), custom_call_target="tpu_custom_call" | custom-call | flops 192675840 | bytes 1048576 | tf_op jit(solution)/shard_map/backward_conv/pallas_call | solution.py:554
  (15 shorter events, 0.1 us)
Async XLA Ops:
  0.6 1.0 %copy-start = (bf16[1024,256]{1,0:T(8,128)(2,1)S(1)}, bf16[1024,256]{1,0:T(8,128)(2,1)}, u32[]{:S(2)}) copy-start(bf16[1024,256]{1,0:T(8,128)(2,1)} %param.10) | copy-start | bytes 1572868
  0.6 4.8 %copy-start.2 = (bf16[256,1024]{1,0:T(8,128)(2,1)S(1)}, bf16[256,1024]{1,0:T(8,128)(2,1)}, u32[]{:S(2)}) copy-start(bf16[256,1024]{1,0:T(8,128)(2,1)} %refs_6_.1) | copy-start | bytes 1572868
  0.7 13.5 %collective-permute-start = (bf16[256,1024]{1,0:T(8,128)(2,1)}, bf16[256,1024]{1,0:T(8,128)(2,1)S(1)}, u32[]{:S(2)}, u32[]{:S(2)}) collective-permute-start(bf16[256,1024]{1,0:T(8,128)(2,1)} %refs_6_.1), channel_id=1, source_target_pairs={{0,4},{4,0},{8,12},{12,8},{1,5},{5,1},{9,13},{13,9},{2,6},{6,2},{1... | collective-permute-start | bytes 1572872 | tf_op jit(solution)/shard_map/w_in_core/ppermute | solution.py:29
  1.7 21.4 %collective-permute-start.6 = (bf16[512,256]{1,0:T(8,128)(2,1)S(1)}, bf16[512,256]{1,0:T(8,128)(2,1)S(1)}, u32[]{:S(2)}, u32[]{:S(2)}) collective-permute-start(bf16[512,256]{1,0:T(8,128)(2,1)S(1)} %constant_dynamic-slice_fusion.2), channel_id=1, source_target_pairs={{0,8},{1,12},{2,0},{3,4},{4,9},{5,13},{6,1},{7,5},{8,10},{9,14},{1... | collective-permute-start | bytes 786440 | tf_op jit(solution)/shard_map/w_out_transposed/ppermute | solution.py:360
  5.4 2.4 %copy-start.1 = (bf16[16,16,256]{2,1,0:T(8,128)(2,1)S(1)}, bf16[16,16,256]{2,1,0:T(8,128)(2,1)}, u32[]{:S(2)}) copy-start(bf16[16,16,256]{2,1,0:T(8,128)(2,1)} %param.6) | copy-start | bytes 393220
  5.4 11.8 %copy-start.3 = (bf16[16,16,256]{2,1,0:T(8,128)(2,1)S(1)}, bf16[16,16,256]{2,1,0:T(8,128)(2,1)}, u32[]{:S(2)}) copy-start(bf16[16,16,256]{2,1,0:T(8,128)(2,1)} %param.11) | copy-start | bytes 393220
  5.5 17.6 %collective-permute-start.7 = (bf16[256,512]{1,0:T(8,128)(2,1)S(1)}, bf16[256,512]{1,0:T(8,128)(2,1)S(1)}, u32[]{:S(2)}, u32[]{:S(2)}) collective-permute-start(bf16[256,512]{1,0:T(8,128)(2,1)S(1)} %get-tuple-element.51), channel_id=1, source_target_pairs={{0,8},{4,12},{8,0},{12,4},{1,9},{5,13},{9,1},{13,5},{2,10},{6,14},... | collective-permute-start | bytes 786440 | tf_op jit(solution)/shard_map/w_in_row_0/ppermute | solution.py:29
  7.8 9.4 %copy-start.4 = (f32[7,7,256]{2,1,0:T(8,128)S(1)}, f32[7,7,256]{2,1,0:T(8,128)}, u32[]{:S(2)}) copy-start(f32[7,7,256]{2,1,0:T(8,128)} %taps.3) | copy-start | bytes 150532
  7.8 3.2 %collective-permute-start.1 = (bf16[48,256]{1,0:T(8,128)(2,1)S(1)}, bf16[48,256]{1,0:T(8,128)(2,1)S(1)}, u32[]{:S(2)}, u32[]{:S(2)}) collective-permute-start(bf16[48,256]{1,0:T(8,128)(2,1)S(1)} %constant_dynamic-slice_fusion.3), channel_id=1, source_target_pairs={{0,16},{16,0},{1,17},{17,1},{2,18},{18,2},{3,19},{19,3},{4,20},{20... | collective-permute-start | bytes 73736 | tf_op jit(solution)/shard_map/image_rows/ppermute | solution.py:44
  11.1 3.1 %collective-permute-start.2 = (bf16[80,256]{1,0:T(8,128)(2,1)S(1)}, bf16[80,256]{1,0:T(8,128)(2,1)S(1)}, u32[]{:S(2)}, u32[]{:S(2)}) collective-permute-start(bf16[80,256]{1,0:T(8,128)(2,1)S(1)} %get-tuple-element.27), channel_id=1, source_target_pairs={{0,4},{8,12},{4,0},{12,8},{1,5},{9,13},{5,1},{13,9},{2,6},{10,14},... | collective-permute-start | bytes 122888 | tf_op jit(solution)/shard_map/image_columns/ppermute | solution.py:44
  11.7 5.6 %collective-permute-start.3 = (bf16[80,256]{1,0:T(8,128)(2,1)S(1)}, bf16[80,256]{1,0:T(8,128)(2,1)S(1)}, u32[]{:S(2)}, u32[]{:S(2)}) collective-permute-start(bf16[80,256]{1,0:T(8,128)(2,1)S(1)} %get-tuple-element.28), channel_id=1, source_target_pairs={{4,8},{8,4},{5,9},{9,5},{6,10},{10,6},{7,11},{11,7},{20,24},{24,20... | collective-permute-start | bytes 122888 | tf_op jit(solution)/shard_map/image_columns/ppermute | solution.py:44
  17.3 0.7 copy-start.5
  19.8 11.5 %collective-permute-start.5 = (bf16[528,256]{1,0:T(8,128)(2,1)S(1)}, bf16[528,256]{1,0:T(8,128)(2,1)S(1)}, u32[]{:S(2)}, u32[]{:S(2)}) collective-permute-start(bf16[528,256]{1,0:T(8,128)(2,1)S(1)} %forward_conv.1.refs_0_), channel_id=1, source_target_pairs={{0,2},{1,3},{2,0},{3,1},{4,6},{5,7},{6,4},{7,5},{8,10},{9,11},{10,... | collective-permute-start | bytes 811016 | tf_op jit(solution)/shard_map/features/col_2/ppermute | solution.py:29
  23.0 8.5 %collective-permute-start.4 = (bf16[528,256]{1,0:T(8,128)(2,1)S(1)}, bf16[528,256]{1,0:T(8,128)(2,1)S(1)}, u32[]{:S(2)}, u32[]{:S(2)}) collective-permute-start(bf16[528,256]{1,0:T(8,128)(2,1)S(1)} %forward_conv.1.refs_0_), channel_id=1, source_target_pairs={{0,1},{1,0},{2,3},{3,2},{4,5},{5,4},{6,7},{7,6},{8,9},{9,8},{10,11... | collective-permute-start | bytes 811016 | tf_op jit(solution)/shard_map/features/col_1/ppermute | solution.py:29
  23.1 5.6 %collective-permute-start.9 = (bf16[512,256]{1,0:T(8,128)(2,1)S(1)}, bf16[512,256]{1,0:T(8,128)(2,1)S(1)}, u32[]{:S(2)}, u32[]{:S(2)}) collective-permute-start(bf16[512,256]{1,0:T(8,128)(2,1)S(1)} %collective-permute-done.6.refs_10_.refs_0_), channel_id=1, source_target_pairs={{0,16},{16,0},{1,17},{17,1},{2,18},{18,2},{3,19},{19,3},{4,20},{20... | collective-permute-start | bytes 786440 | tf_op jit(solution)/shard_map/w_out_section/ppermute | solution.py:29
  24.3 7.0 %collective-permute-start.8 = (bf16[512,256]{1,0:T(8,128)(2,1)S(1)}, bf16[512,256]{1,0:T(8,128)(2,1)S(1)}, u32[]{:S(2)}, u32[]{:S(2)}) collective-permute-start(bf16[512,256]{1,0:T(8,128)(2,1)S(1)} %collective-permute-done.6.refs_10_.refs_0_), channel_id=1, source_target_pairs={{0,8},{4,12},{8,0},{12,4},{1,9},{5,13},{9,1},{13,5},{2,10},{6,14},... | collective-permute-start | bytes 786440 | tf_op jit(solution)/shard_map/w_out_row/ppermute | solution.py:29
  31.6 10.3 %collective-permute-start.10 = (bf16[528,256]{1,0:T(8,128)(2,1)S(1)}, bf16[528,256]{1,0:T(8,128)(2,1)S(1)}, u32[]{:S(2)}, u32[]{:S(2)}) collective-permute-start(bf16[528,256]{1,0:T(8,128)(2,1)S(1)} %collective-permute-done.5.refs_2_), channel_id=1, source_target_pairs={{0,1},{1,0},{2,3},{3,2},{4,5},{5,4},{6,7},{7,6},{8,9},{9,8},{10,11... | collective-permute-start | bytes 811016 | tf_op jit(solution)/shard_map/features/col_1/ppermute | solution.py:29
  33.0 7.7 %collective-permute-start.11 = (bf16[256,512]{1,0:T(8,128)(2,1)S(1)}, bf16[256,512]{1,0:T(8,128)(2,1)S(1)}, u32[]{:S(2)}, u32[]{:S(2)}) collective-permute-start(bf16[256,512]{1,0:T(8,128)(2,1)S(1)} %get-tuple-element.31), channel_id=1, source_target_pairs={{0,8},{4,12},{8,0},{12,4},{1,9},{5,13},{9,1},{13,5},{2,10},{6,14},... | collective-permute-start | bytes 786440 | tf_op jit(solution)/shard_map/w_in_row_1/ppermute | solution.py:29
  33.1 8.6 %collective-permute-start.17 = (bf16[512,256]{1,0:T(8,128)(2,1)S(1)}, bf16[512,256]{1,0:T(8,128)(2,1)S(1)}, u32[]{:S(2)}, u32[]{:S(2)}) collective-permute-start(bf16[512,256]{1,0:T(8,128)(2,1)S(1)} %collective-permute-done.8.refs_12_.refs_2_), channel_id=1, source_target_pairs={{0,16},{16,0},{1,17},{17,1},{2,18},{18,2},{3,19},{19,3},{4,20},{20... | collective-permute-start | bytes 786440 | tf_op jit(solution)/shard_map/w_out_both/ppermute | solution.py:29
  33.4 8.9 %collective-permute-start.12 = (bf16[256,512]{1,0:T(8,128)(2,1)S(1)}, bf16[256,512]{1,0:T(8,128)(2,1)S(1)}, u32[]{:S(2)}, u32[]{:S(2)}) collective-permute-start(bf16[256,512]{1,0:T(8,128)(2,1)S(1)} %collective-permute-done.7.refs_4_), channel_id=1, source_target_pairs={{0,4},{4,0},{8,12},{12,8},{1,5},{5,1},{9,13},{13,9},{2,6},{6,2},{1... | collective-permute-start | bytes 786440 | tf_op jit(solution)/shard_map/w_in_core_2_0/ppermute | solution.py:29
  35.6 6.8 %collective-permute-start.14 = (bf16[512,256]{1,0:T(8,128)(2,1)S(1)}, bf16[512,256]{1,0:T(8,128)(2,1)S(1)}, u32[]{:S(2)}, u32[]{:S(2)}) collective-permute-start(bf16[512,256]{1,0:T(8,128)(2,1)S(1)} %collective-permute-done.6.refs_10_.refs_0_), channel_id=1, source_target_pairs={{0,4},{4,0},{8,12},{12,8},{1,5},{5,1},{9,13},{13,9},{2,6},{6,2},{1... | collective-permute-start | bytes 786440 | tf_op jit(solution)/shard_map/w_out_core_0_0/ppermute | solution.py:29
  40.7 2.2 %collective-permute-start.16 = (bf16[512,256]{1,0:T(8,128)(2,1)S(1)}, bf16[512,256]{1,0:T(8,128)(2,1)S(1)}, u32[]{:S(2)}, u32[]{:S(2)}) collective-permute-start(bf16[512,256]{1,0:T(8,128)(2,1)S(1)} %collective-permute-done.9.refs_14_.refs_4_), channel_id=1, source_target_pairs={{0,4},{4,0},{8,12},{12,8},{1,5},{5,1},{9,13},{13,9},{2,6},{6,2},{1... | collective-permute-start | bytes 786440 | tf_op jit(solution)/shard_map/w_out_core_0_1/ppermute | solution.py:29
  41.7 1.5 %collective-permute-start.15 = (bf16[512,256]{1,0:T(8,128)(2,1)S(1)}, bf16[512,256]{1,0:T(8,128)(2,1)S(1)}, u32[]{:S(2)}, u32[]{:S(2)}) collective-permute-start(bf16[512,256]{1,0:T(8,128)(2,1)S(1)} %collective-permute-done.8.refs_12_.refs_2_), channel_id=1, source_target_pairs={{0,4},{4,0},{8,12},{12,8},{1,5},{5,1},{9,13},{13,9},{2,6},{6,2},{1... | collective-permute-start | bytes 786440 | tf_op jit(solution)/shard_map/w_out_core_2_0/ppermute | solution.py:29
  41.8 1.8 %collective-permute-start.13 = (bf16[256,512]{1,0:T(8,128)(2,1)S(1)}, bf16[256,512]{1,0:T(8,128)(2,1)S(1)}, u32[]{:S(2)}, u32[]{:S(2)}) collective-permute-start(bf16[256,512]{1,0:T(8,128)(2,1)S(1)} %collective-permute-done.11.refs_5_), channel_id=1, source_target_pairs={{0,4},{4,0},{8,12},{12,8},{1,5},{5,1},{9,13},{13,9},{2,6},{6,2},{1... | collective-permute-start | bytes 786440 | tf_op jit(solution)/shard_map/w_in_core_2_1/ppermute | solution.py:29
  42.2 1.8 %collective-permute-start.18 = (bf16[512,256]{1,0:T(8,128)(2,1)S(1)}, bf16[512,256]{1,0:T(8,128)(2,1)S(1)}, u32[]{:S(2)}, u32[]{:S(2)}) collective-permute-start(bf16[512,256]{1,0:T(8,128)(2,1)S(1)} %collective-permute-done.17.refs_16_.refs_6_), channel_id=1, source_target_pairs={{0,4},{4,0},{8,12},{12,8},{1,5},{5,1},{9,13},{13,9},{2,6},{6,2},{1... | collective-permute-start | bytes 786440 | tf_op jit(solution)/shard_map/w_out_core_2_1/ppermute | solution.py:29
  46.9 9.8 %collective-permute-start.20 = (bf16[256,256]{1,0:T(8,128)(2,1)S(1)}, bf16[256,256]{1,0:T(8,128)(2,1)S(1)}, u32[]{:S(2)}, u32[]{:S(2)}) collective-permute-start(bf16[256,256]{1,0:T(8,128)(2,1)S(1)} %get-tuple-element.35), channel_id=1, source_target_pairs={{0,2},{1,3},{2,0},{3,1},{4,6},{5,7},{6,4},{7,5},{8,10},{9,11},{10,... | collective-permute-start | bytes 393224 | tf_op jit(solution)/shard_map/grad_sums/col_2/ppermute | solution.py:29
  47.8 9.7 %collective-permute-start.19 = (bf16[256,256]{1,0:T(8,128)(2,1)S(1)}, bf16[256,256]{1,0:T(8,128)(2,1)S(1)}, u32[]{:S(2)}, u32[]{:S(2)}) collective-permute-start(bf16[256,256]{1,0:T(8,128)(2,1)S(1)} %get-tuple-element.34), channel_id=1, source_target_pairs={{0,1},{1,0},{2,3},{3,2},{4,5},{5,4},{6,7},{7,6},{8,9},{9,8},{10,11... | collective-permute-start | bytes 393224 | tf_op jit(solution)/shard_map/grad_sums/col_1/ppermute | solution.py:29
  47.9 10.2 %collective-permute-start.21 = (bf16[256,256]{1,0:T(8,128)(2,1)S(1)}, bf16[256,256]{1,0:T(8,128)(2,1)S(1)}, u32[]{:S(2)}, u32[]{:S(2)}) collective-permute-start(bf16[256,256]{1,0:T(8,128)(2,1)S(1)} %get-tuple-element.36), channel_id=1, source_target_pairs={{0,3},{1,2},{2,1},{3,0},{4,7},{5,6},{6,5},{7,4},{8,11},{9,10},{10,... | collective-permute-start | bytes 393224 | tf_op jit(solution)/shard_map/grad_sums/col_3/ppermute | solution.py:29
  57.5 4.7 %collective-permute-start.26 = (bf16[256,256]{1,0:T(8,128)(2,1)S(1)}, bf16[256,256]{1,0:T(8,128)(2,1)S(1)}, u32[]{:S(2)}, u32[]{:S(2)}) collective-permute-start(bf16[256,256]{1,0:T(8,128)(2,1)S(1)} %get-tuple-element.46), channel_id=1, source_target_pairs={{0,1},{1,0},{2,3},{3,2},{4,5},{5,4},{6,7},{7,6},{8,9},{9,8},{10,11... | collective-permute-start | bytes 393224 | tf_op jit(solution)/shard_map/branch_sums/col_1/ppermute | solution.py:29
  58.2 3.9 %collective-permute-start.22 = (bf16[48,256]{1,0:T(8,128)(2,1)S(1)}, bf16[48,256]{1,0:T(8,128)(2,1)S(1)}, u32[]{:S(2)}, u32[]{:S(2)}) collective-permute-start(bf16[48,256]{1,0:T(8,128)(2,1)S(1)} %get-tuple-element.38), channel_id=1, source_target_pairs={{0,16},{16,0},{1,17},{17,1},{2,18},{18,2},{3,19},{19,3},{4,20},{20... | collective-permute-start | bytes 73736 | tf_op jit(solution)/shard_map/grad_rows/ppermute | solution.py:44
  59.0 12.8 %collective-permute-start.25 = (bf16[256,256]{1,0:T(8,128)(2,1)S(1)}, bf16[256,256]{1,0:T(8,128)(2,1)S(1)}, u32[]{:S(2)}, u32[]{:S(2)}) collective-permute-start(bf16[256,256]{1,0:T(8,128)(2,1)S(1)} %get-tuple-element.44), channel_id=1, source_target_pairs={{0,1},{1,0},{2,3},{3,2},{4,5},{5,4},{6,7},{7,6},{8,9},{9,8},{10,11... | collective-permute-start | bytes 393224 | tf_op jit(solution)/shard_map/branch_sums/col_1/ppermute | solution.py:29
  62.1 9.7 %collective-permute-start.27 = (bf16[256,256]{1,0:T(8,128)(2,1)S(1)}, bf16[256,256]{1,0:T(8,128)(2,1)S(1)}, u32[]{:S(2)}, u32[]{:S(2)}) collective-permute-start(bf16[256,256]{1,0:T(8,128)(2,1)S(1)} %add_convert_fusion), channel_id=1, source_target_pairs={{0,2},{1,3},{2,0},{3,1},{4,6},{5,7},{6,4},{7,5},{8,10},{9,11},{10,... | collective-permute-start | bytes 393224 | tf_op jit(solution)/shard_map/branch_sums/col_2/ppermute | solution.py:29
  63.9 5.5 %collective-permute-start.23 = (bf16[80,256]{1,0:T(8,128)(2,1)S(1)}, bf16[80,256]{1,0:T(8,128)(2,1)S(1)}, u32[]{:S(2)}, u32[]{:S(2)}) collective-permute-start(bf16[80,256]{1,0:T(8,128)(2,1)S(1)} %get-tuple-element.39), channel_id=1, source_target_pairs={{0,4},{8,12},{4,0},{12,8},{1,5},{9,13},{5,1},{13,9},{2,6},{10,14},... | collective-permute-start | bytes 122888 | tf_op jit(solution)/shard_map/grad_columns/ppermute | solution.py:44
  66.5 5.3 %collective-permute-start.24 = (bf16[80,256]{1,0:T(8,128)(2,1)S(1)}, bf16[80,256]{1,0:T(8,128)(2,1)S(1)}, u32[]{:S(2)}, u32[]{:S(2)}) collective-permute-start(bf16[80,256]{1,0:T(8,128)(2,1)S(1)} %get-tuple-element.40), channel_id=1, source_target_pairs={{4,8},{8,4},{5,9},{9,5},{6,10},{10,6},{7,11},{11,7},{20,24},{24,20... | collective-permute-start | bytes 122888 | tf_op jit(solution)/shard_map/grad_columns/ppermute | solution.py:44
